TPU v7x, 256 devices: a whole 4x4x8 slice. The times are simulated.
256 devices in a mesh: sta: 32 (over x, y, core), tpl: 8 (over z).
Axes of the slice: x: 4, y: 4, z: 8, core: 2. Of those that a mesh axis runs over, the one named last changes fastest.
Arguments:
- waveforms: bfloat16 [512, 3, 5376], P('sta'), may hold values from -6 to 6
- station_home: int32 [512], replicated, may hold values from 0 to 511, as said below
- templates: bfloat16 [2048, 20, 768], P(('sta', 'tpl')), may hold values from -6 to 6
- template_stations: int32 [2048, 20], P(('sta', 'tpl')), may hold values from 0 to 511, as said below
- station_counts: int32 [2048], P(('sta', 'tpl')), may hold values from 4 to 20
- moveouts: int32 [2048, 20], P(('sta', 'tpl')), may hold values from 0 to 4
Outputs:
- stack: float32 [2048, 4608], P(('sta', 'tpl'))
- network: float32 [4608], replicated
Inputs may be any that keep to these rules, and one draw needn't show every extreme that they name: `station_home`: a permutation of the rows. `template_stations`: the live slots k < station_counts[t] of a template name distinct stations; later slots are ignored; among the live slots of the 8 templates of one device, at most 6 name stations whose rows station_home puts on one index of sta.
All inputs are finite; a program needn't handle non-finite values.
Results may differ from a plain program's by a relative error of at most 0.0003.
Values may be sent and summed in bfloat16 or wider, within the bound.
No kernel may reach another device: no remote copies, remote signals or barrier semaphores. Data moves between devices by JAX's collectives and lax.ppermute only.
A program may use at most 128 MiB of HBM per device.

v0:
```python
import jax
import jax.numpy as jnp
from jax import lax
from jax.sharding import PartitionSpec as P

SLOTS = 20
L = 256
BLOCK = 128
LAG_BLOCKS = 40
MOVE_BLOCKS = 4


EPS = 1e-06


def windows(x):
    count = x.shape[0]
    reach = L // BLOCK
    blocks = x.reshape(count, 3, LAG_BLOCKS + reach, BLOCK)
    parts = [blocks[:, :, start : start + LAG_BLOCKS, :] for start in range(reach + 1)]
    return jnp.concatenate(parts, axis=-1)


def energy(window):
    squares = jnp.sum(window.astype(jnp.float32) ** 2, axis=1)
    upper = jnp.arange(BLOCK + L)[:, None]
    lower = jnp.arange(BLOCK)[None, :]
    boxes = ((upper >= lower) & (upper - lower < L)).astype(jnp.float32)
    return jnp.einsum("nbu,uj->nbj", squares, boxes, precision=lax.Precision.HIGHEST) / (3.0 * L)


def toeplitz(pieces):
    count, comps, length = pieces.shape
    padded = jnp.concatenate([pieces, jnp.zeros((count, comps, BLOCK + 1), pieces.dtype)], axis=-1)
    flat = jnp.tile(padded, (1, 1, BLOCK))
    return flat[..., : BLOCK * (length + BLOCK)].reshape(count, comps, BLOCK, length + BLOCK)


def shift(traces, offsets):
    kept = LAG_BLOCKS - MOVE_BLOCKS
    moved = jax.vmap(lambda trace, offset: lax.dynamic_slice_in_dim(trace, offset, kept, 0))(
        traces, offsets
    )
    return moved.reshape(traces.shape[0], kept * BLOCK)


def pack(stations, counts, offsets, pieces, station_home, targets, sta_dev, capacity):
    total = stations.shape[0] * SLOTS
    flat_ids = stations.reshape(total)
    live = (jnp.arange(SLOTS)[None, :] < counts[:, None]).reshape(total)
    table = flat_ids[:, None] == jnp.arange(station_home.shape[0])[None, :]
    rows = jnp.sum(jnp.where(table, station_home[None, :], 0), axis=1)
    owner = rows // sta_dev
    local = rows % sta_dev
    match = live[None, :] & (owner[None, :] == targets[:, None])
    places = jnp.arange(total, dtype=jnp.int32)
    score = jnp.where(match, places[None, :], total + places[None, :])
    order = jnp.argsort(score, axis=1)[:, :capacity]
    valid = jnp.take_along_axis(match, order, axis=1).astype(jnp.int32)
    flat_moves = offsets.reshape(total)
    meta = jnp.stack([local[order], flat_moves[order], order // SLOTS, valid], axis=-1)
    flat_pieces = pieces.reshape(total, pieces.shape[2])
    return (flat_pieces[order], meta)


def body(waveforms, station_home, templates, template_stations, station_counts, moveouts):
    sta_dev = waveforms.shape[0]
    width = lax.axis_size("sta")
    tpl_dev = templates.shape[0]
    capacity = 2 * ((10 * tpl_dev + width - 1) // width)
    own_pieces, own_meta = pack(
        template_stations,
        station_counts,
        moveouts,
        templates,
        station_home,
        jnp.arange(width, dtype=jnp.int32),
        sta_dev,
        capacity,
    )
    all_pieces, all_ids, all_counts, all_moves = (
        lax.all_gather(templates, "sta", axis=0, tiled=True),
        lax.all_gather(template_stations, "sta", axis=0, tiled=True),
        lax.all_gather(station_counts, "sta", axis=0, tiled=True),
        lax.all_gather(moveouts, "sta", axis=0, tiled=True),
    )
    here = jnp.reshape(lax.axis_index("sta"), (1,))

    def for_source(pieces, ids, counts, moves):
        return pack(ids, counts, moves, pieces, station_home, here, sta_dev, capacity)

    got_pieces, got_meta = jax.vmap(for_source)(
        all_pieces.reshape(width, tpl_dev, SLOTS, all_pieces.shape[2]),
        all_ids.reshape(width, tpl_dev, SLOTS),
        all_counts.reshape(width, tpl_dev),
        all_moves.reshape(width, tpl_dev, SLOTS),
    )
    got_pieces = got_pieces[:, 0]
    got_meta = got_meta[:, 0]
    station_windows = windows(waveforms)
    station_power = energy(station_windows)
    piece_len = got_pieces.shape[2] // 3

    def correlate(items):
        pieces, meta = items
        rows = meta[:, 0]
        window = station_windows[rows]
        power = station_power[rows]
        split = pieces.reshape(pieces.shape[0], 3, piece_len)
        corr = jnp.einsum(
            "pcbu,pcju->pbj", window, toeplitz(split), preferred_element_type=jnp.float32
        )
        flat = split.astype(jnp.float32)
        tmean = jnp.mean(flat * flat, axis=(1, 2))
        scaled = corr / (
            3.0 * piece_len * jnp.sqrt(power + EPS) * jnp.sqrt(tmean + EPS)[:, None, None]
        )
        return shift(scaled, meta[:, 1]) * meta[:, 3][:, None].astype(jnp.float32)

    halves = width // 2
    traces = lax.map(
        correlate,
        (
            got_pieces.reshape(halves, 2 * capacity, got_pieces.shape[2]),
            got_meta.reshape(halves, 2 * capacity, 4),
        ),
    )
    traces = traces.reshape(width, capacity, traces.shape[-1])
    slots_of = jnp.arange(tpl_dev, dtype=jnp.int32)
    back = lax.all_to_all(traces, "sta", split_axis=0, concat_axis=0, tiled=True)
    weights = (
        (own_meta[..., 2][..., None] == slots_of) & (own_meta[..., 3][..., None] > 0)
    ).astype(jnp.float32)
    total = jnp.einsum("dkt,dkn->tn", weights, back, precision=lax.Precision.HIGHEST)
    stack = total * jnp.sqrt(3.0 * piece_len / station_counts.astype(jnp.float32))[:, None]
    network = lax.pmax(jnp.max(stack, axis=0), ("sta", "tpl"))
    return (stack, network)


def solution(mesh):
    in_specs = (
        P("sta", None, None),
        P(),
        P(("sta", "tpl"), None, None),
        P(("sta", "tpl"), None),
        P(("sta", "tpl")),
        P(("sta", "tpl"), None),
    )
    out_specs = (P(("sta", "tpl"), None), P())
    return jax.shard_map(body, mesh=mesh, in_specs=in_specs, out_specs=out_specs, check_vma=False)
```

profile of v0, /device:TPU:32, one launch (start us, length us, event | category | flops | bytes accessed | tf_op | source)
XLA Modules:
  0.0 820.5 jit_solution(9775686455658006622)
XLA Ops:
  10.7 16.9 %all-reduce.2 = s32[256]{0:T(256)S(1)} all-reduce(s32[256]{0:T(256)S(1)} %dynamic-update-slice), channel_id=1, replica_groups=mesh['sta'=32,'tpl'=8] {'sta'}, use_global_device_ids=true, to_apply=%add.2 | all-reduce | flops 256 | bytes 2048
  27.9 22.2 %all_gather.12 = s32[256,20]{1,0:T(8,128)S(1)} all-gather(s32[8,20]{1,0:T(8,128)} %param.11), channel_id=1, replica_groups=mesh['sta'=32,'tpl'=8] {'sta'}, dimensions={0}, use_global_device_ids=true | all-gather | bytes 21120 | tf_op jit(solution)/shard_map/all_gather | solution.py:83
  50.3 3.3 select_reduce_fusion
  53.7 3.7 sort.35
  62.4 24.3 %all_gather.14 = s32[256,20]{1,0:T(8,128)S(1)} all-gather(s32[8,20]{1,0:T(8,128)S(1)} %copy-done.5), channel_id=1, replica_groups=mesh['sta'=32,'tpl'=8] {'sta'}, dimensions={0}, use_global_device_ids=true | all-gather | bytes 21120 | tf_op jit(solution)/shard_map/all_gather | solution.py:85
  93.4 11.4 %copy.83 = bf16[256,20,768]{2,1,0:T(8,128)(2,1)} copy(bf16[256,20,768]{2,0,1:T(8,128)(2,1)} %all-gather.2.cloned.1.call-done) | data formatting | bytes 15728640 | tf_op jit(solution)/shard_map/all_gather | solution.py:82
  104.8 12.5 %reshape_reshape.8 = bf16[32,160,768]{2,1,0:T(8,128)(2,1)} reshape(bf16[256,20,768]{2,1,0:T(8,128)(2,1)} %copy.83) | data formatting | bytes 15728640 | tf_op jit(solution)/shard_map/vmap()/reshape;reshape | solution.py:62
  117.3 5.4 gather_fusion.7
  123.6 535.0 %while.10 = (s32[]{:T(128)}, f32[16,12,4608]{2,1,0:T(8,128)}, s32[16,12,4]{1,0,2:T(8,128)}, bf16[16,3,40,384]{3,2,1,0:T(8,128)(2,1)}, bf16[16,12,768]{2,1,0:T(8,...) while((s32[]{:T(128)}, f32[16,12,4608]{2,1,0:T(8,128)}, s32[16,12,4]{1,0,2:T(8,128)}, ...), condition=%wide.region_7.8_spmd, body=%wide.region_5.7_spmd.sunk | while | flops 141826224 | bytes 35165088 | solution.py:121
  133.1 9.6 %tile.12 = bf16[12,3,49280]{2,0,1:T(8,128)(2,1)} reshape(bf16[12,3,128,385]{3,2,0,1:T(8,128)(2,1)} %tile.11) | data formatting | bytes 7096320 | tf_op jit(solution)/shard_map/while/body/eval_jaxpr/tile | solution.py:35
  142.7 4.8 slice.96
  147.5 4.7 reshape.422
  166.6 9.6 %tile.12 = bf16[12,3,49280]{2,0,1:T(8,128)(2,1)} reshape(bf16[12,3,128,385]{3,2,0,1:T(8,128)(2,1)} %tile.11) | data formatting | bytes 7096320 | tf_op jit(solution)/shard_map/while/body/eval_jaxpr/tile | solution.py:35
  176.2 4.8 slice.96
  181.0 4.7 reshape.422
  200.0 9.6 %tile.12 = bf16[12,3,49280]{2,0,1:T(8,128)(2,1)} reshape(bf16[12,3,128,385]{3,2,0,1:T(8,128)(2,1)} %tile.11) | data formatting | bytes 7096320 | tf_op jit(solution)/shard_map/while/body/eval_jaxpr/tile | solution.py:35
  209.6 4.8 slice.96
  214.4 4.7 reshape.422
  233.4 9.6 %tile.12 = bf16[12,3,49280]{2,0,1:T(8,128)(2,1)} reshape(bf16[12,3,128,385]{3,2,0,1:T(8,128)(2,1)} %tile.11) | data formatting | bytes 7096320 | tf_op jit(solution)/shard_map/while/body/eval_jaxpr/tile | solution.py:35
  243.0 4.8 slice.96
  247.8 4.7 reshape.422
  258.0 3.1 gather_fusion
  266.9 9.6 %tile.12 = bf16[12,3,49280]{2,0,1:T(8,128)(2,1)} reshape(bf16[12,3,128,385]{3,2,0,1:T(8,128)(2,1)} %tile.11) | data formatting | bytes 7096320 | tf_op jit(solution)/shard_map/while/body/eval_jaxpr/tile | solution.py:35
  276.5 4.8 slice.96
  281.3 4.7 reshape.422
  300.3 9.6 %tile.12 = bf16[12,3,49280]{2,0,1:T(8,128)(2,1)} reshape(bf16[12,3,128,385]{3,2,0,1:T(8,128)(2,1)} %tile.11) | data formatting | bytes 7096320 | tf_op jit(solution)/shard_map/while/body/eval_jaxpr/tile | solution.py:35
  309.9 4.8 slice.96
  314.7 4.7 reshape.422
  333.8 9.6 %tile.12 = bf16[12,3,49280]{2,0,1:T(8,128)(2,1)} reshape(bf16[12,3,128,385]{3,2,0,1:T(8,128)(2,1)} %tile.11) | data formatting | bytes 7096320 | tf_op jit(solution)/shard_map/while/body/eval_jaxpr/tile | solution.py:35
  343.3 4.8 slice.96
  348.1 4.7 reshape.422
  367.2 9.6 %tile.12 = bf16[12,3,49280]{2,0,1:T(8,128)(2,1)} reshape(bf16[12,3,128,385]{3,2,0,1:T(8,128)(2,1)} %tile.11) | data formatting | bytes 7096320 | tf_op jit(solution)/shard_map/while/body/eval_jaxpr/tile | solution.py:35
  376.8 4.8 slice.96
  381.6 4.7 reshape.422
  400.6 9.6 %tile.12 = bf16[12,3,49280]{2,0,1:T(8,128)(2,1)} reshape(bf16[12,3,128,385]{3,2,0,1:T(8,128)(2,1)} %tile.11) | data formatting | bytes 7096320 | tf_op jit(solution)/shard_map/while/body/eval_jaxpr/tile | solution.py:35
  410.2 4.8 slice.96
  415.0 4.7 reshape.422
  434.1 9.6 %tile.12 = bf16[12,3,49280]{2,0,1:T(8,128)(2,1)} reshape(bf16[12,3,128,385]{3,2,0,1:T(8,128)(2,1)} %tile.11) | data formatting | bytes 7096320 | tf_op jit(solution)/shard_map/while/body/eval_jaxpr/tile | solution.py:35
  443.7 4.8 slice.96
  448.5 4.7 reshape.422
  467.5 9.6 %tile.12 = bf16[12,3,49280]{2,0,1:T(8,128)(2,1)} reshape(bf16[12,3,128,385]{3,2,0,1:T(8,128)(2,1)} %tile.11) | data formatting | bytes 7096320 | tf_op jit(solution)/shard_map/while/body/eval_jaxpr/tile | solution.py:35
  477.1 4.8 slice.96
  481.9 4.7 reshape.422
  501.0 9.6 %tile.12 = bf16[12,3,49280]{2,0,1:T(8,128)(2,1)} reshape(bf16[12,3,128,385]{3,2,0,1:T(8,128)(2,1)} %tile.11) | data formatting | bytes 7096320 | tf_op jit(solution)/shard_map/while/body/eval_jaxpr/tile | solution.py:35
  510.5 4.8 slice.96
  515.3 4.7 reshape.422
  534.4 9.6 %tile.12 = bf16[12,3,49280]{2,0,1:T(8,128)(2,1)} reshape(bf16[12,3,128,385]{3,2,0,1:T(8,128)(2,1)} %tile.11) | data formatting | bytes 7096320 | tf_op jit(solution)/shard_map/while/body/eval_jaxpr/tile | solution.py:35
  544.0 4.8 slice.96
  548.8 4.7 reshape.422
  567.8 9.6 %tile.12 = bf16[12,3,49280]{2,0,1:T(8,128)(2,1)} reshape(bf16[12,3,128,385]{3,2,0,1:T(8,128)(2,1)} %tile.11) | data formatting | bytes 7096320 | tf_op jit(solution)/shard_map/while/body/eval_jaxpr/tile | solution.py:35
  577.4 4.8 slice.96
  582.2 4.7 reshape.422
  601.3 9.6 %tile.12 = bf16[12,3,49280]{2,0,1:T(8,128)(2,1)} reshape(bf16[12,3,128,385]{3,2,0,1:T(8,128)(2,1)} %tile.11) | data formatting | bytes 7096320 | tf_op jit(solution)/shard_map/while/body/eval_jaxpr/tile | solution.py:35
  610.8 4.8 slice.96
  615.6 4.7 reshape.422
  634.7 9.6 %tile.12 = bf16[12,3,49280]{2,0,1:T(8,128)(2,1)} reshape(bf16[12,3,128,385]{3,2,0,1:T(8,128)(2,1)} %tile.11) | data formatting | bytes 7096320 | tf_op jit(solution)/shard_map/while/body/eval_jaxpr/tile | solution.py:35
  644.3 4.8 slice.96
  649.1 4.7 reshape.422
  658.6 5.1 reshape.318
  663.7 5.0 all-to-all-start
  669.2 3.7 sort.34
  675.5 52.0 %all-to-all-done = f32[32,6,4608]{2,1,0:T(8,128)} async-done(((f32[32,6,4608]{2,1,0:T(8,128)}), f32[32,6,4608]{2,1,0:T(8,128)}, u32[]{:S(2)}, u32[]{:S(2)}) %all-to-all-start) | async-done | bytes 3538976 | tf_op jit(solution)/shard_map/all_to_all | solution.py:130
  727.5 6.1 fusion.38
  733.6 80.0 %pmax.7 = f32[4608]{0:T(1024)} all-reduce(f32[4608]{0:T(1024)S(1)} %get-tuple-element.99), channel_id=1, replica_groups=mesh['sta'=32,'tpl'=8] {'sta','tpl'}, use_global_device_ids=true, to_apply=%region_9.10 | all-reduce | flops 4608 | bytes 36864 | tf_op jit(solution)/shard_map/pmax | solution.py:136
  (352 shorter events, 243.5 us)
Async XLA Ops:
  7.2 86.2 %all-gather.2.cloned.1.call-start = ((), (), s32[]{:S(2)}) async-start(), calls=%async_computation.1 | async-start | bytes 8110080 | tf_op jit(solution)/shard_map/all_gather | solution.py:82
  50.3 7.1 copy-start.3
  60.4 2.0 copy-start.5
  86.8 2.2 copy-start
  663.6 5.0 copy-start.1
  663.6 5.1 copy-start.6
  663.6 5.3 copy-start.2
  663.6 5.5 copy-start.4
  663.7 63.8 %all-to-all-start = ((f32[32,6,4608]{2,1,0:T(8,128)}), f32[32,6,4608]{2,1,0:T(8,128)}, u32[]{:S(2)}, u32[]{:S(2)}) async-start(f32[32,6,4608]{2,1,0:T(8,128)} %reshape.318), calls=%async_computation | async-start | bytes 9437184 | tf_op jit(solution)/shard_map/all_to_all | solution.py:130
Sparse Core Ops, SparseCore 0:
  10.7 59.7 all-gather.1
where the time goes:
time: 828 us; the launch traced here: 820 us
  local copies, waits for them, and re-layouts  513 us (62%)
  blocking collectives  143 us (17%)
  waiting for transfers between devices  52.7 us (6%)
  matrix products  50.4 us (6%)
  other arithmetic  39.3 us (5%)
  between operations  15 us (2%)
    another operation x32, local copies, waits for them, and re-layouts, toeplitz(): flat = jnp.tile(padded, (1, 1, BLOCK))  194 us
    pmax x1, blocking collectives, body(): network = lax.pmax(jnp.max(stack, axis=0), ('sta', 'tpl'))  80 us
    slice x16, local copies, waits for them, and re-layouts, toeplitz(): flat[..., :BLOCK * (length + BLOCK)]  76.8 us
    reshape x16, local copies, waits for them, and re-layouts, toeplitz(): flat[..., :BLOCK * (length + BLOCK)]  75.8 us
    all_to_all x1, waiting for transfers between devices, body(): lax.all_to_all(traces, 'sta', split_axis=0, concat_axis=0, tiled=True)  52 us
    gather x16, local copies, waits for them, and re-layouts, correlate(): window = station_windows[rows]  50.3 us
    dot_general x16, matrix products, correlate(): jnp.einsum('pcbu,pcju->pbj', window, toeplitz(split), preferred_element_t...  43 us
    gather x16, local copies, waits for them, and re-layouts, correlate(): power = station_power[rows]  35.9 us
  transfers between devices with their start and end apart: 2, of which 1 were waited for; matrix products, arithmetic and copies ran while one was open for 3% of the time, Pallas kernels for 0%

commit v1 on v0

v1 whole, which is shorter than its diff:
```python
import functools

import jax
import jax.numpy as jnp
from jax import lax
from jax.experimental import pallas as pl
from jax.experimental.pallas import tpu as pltpu
from jax.sharding import PartitionSpec as P

SLOTS = 20
L = 256
BLOCK = 128
LAG_BLOCKS = 40
MOVE_BLOCKS = 4
EPS = 1e-06

PHASES = 16
COLS = LAG_BLOCKS * BLOCK // PHASES
KEPT = (LAG_BLOCKS - MOVE_BLOCKS) * BLOCK // PHASES
WIDE = 384
REACH = L // PHASES
DEPTH = 3 * L + BLOCK
CHUNK = 8
CAP = 6
ROWS = 8
BLOCKS = 14

HIGHEST = lax.Precision.HIGHEST
NT = (((1,), (1,)), ((), ()))


def iota(shape, dim):
    return lax.broadcasted_iota(jnp.int32, shape, dim)


def dot(a, b, dims=None):
    if dims is None:
        dims = (((1,), (0,)), ((), ()))
    return lax.dot_general(a, b, dims, preferred_element_type=jnp.float32)


def pack_kernel(slots_ref, home_ref, templates_ref, send_ref, dest_ref):
    total = templates_ref.shape[0]
    width = send_ref.shape[0]
    sta_dev = home_ref.shape[1] // width
    stations = slots_ref[0:1, :]
    moves = slots_ref[1:2, :]
    counts = slots_ref[2:3, :]
    n_sta = home_ref.shape[1]
    home = home_ref[...]
    high = home // sta_dev
    low = home - high * sta_dev
    rows = iota((8, n_sta), 0)
    table = jnp.where(rows == 0, high, jnp.where(rows == 1, low, 0)).astype(jnp.bfloat16)
    hit = (iota((n_sta, total), 0) == stations).astype(jnp.bfloat16)
    found = dot(table, hit)
    owner = found[0:1, :].astype(jnp.int32)
    local = found[1:2, :]
    live = iota((1, total), 1) // 8 < counts
    at_owner = jnp.where((iota((width, total), 0) == owner) & live, 1.0, 0.0)
    before = (iota((total, total), 0) < iota((total, total), 1)).astype(jnp.bfloat16)
    rank = jnp.sum(at_owner * dot(at_owner.astype(jnp.bfloat16), before), axis=0, keepdims=True)
    dest = jnp.where(live, owner * ROWS + rank.astype(jnp.int32), -1)
    dest_ref[...] = dest
    pick = (iota((width * ROWS, total), 0) == dest).astype(jnp.bfloat16)
    send = dot(pick, templates_ref[...]).astype(jnp.bfloat16)
    kind = iota((BLOCK, total), 0)
    fields = jnp.where(
        kind == 0, local, jnp.where(kind == 1, moves.astype(jnp.float32), jnp.where(kind == 2, 1.0, 0.0))
    ).astype(jnp.bfloat16)
    tail = dot(pick, fields, NT).astype(jnp.bfloat16)
    send_ref[:, :, : 3 * L] = send.reshape(width, ROWS, 3 * L)
    send_ref[:, :, 3 * L :] = tail.reshape(width, ROWS, BLOCK)


def prep_kernel(wave_ref, xs_ref, inv_ref, wide_ref):
    stations = wave_ref.shape[1]
    tiles = wave_ref.shape[2] // BLOCK
    wide_ref[...] = wave_ref[...].astype(jnp.float32)
    lane = iota((8, BLOCK), 1)
    own = (lane // PHASES == iota((8, BLOCK), 0)).astype(jnp.float32)
    spread = (
        (iota((3 * PHASES, 3 * BLOCK), 1) // BLOCK == iota((3 * PHASES, 3 * BLOCK), 0) // PHASES)
        & (iota((3 * PHASES, 3 * BLOCK), 1) % PHASES == iota((3 * PHASES, 3 * BLOCK), 0) % PHASES)
    ).astype(jnp.bfloat16)
    sub = iota((PHASES, WIDE), 0)

    @pl.loop(0, stations)
    def _(s):
        comps = []
        for c in range(3):
            parts = []
            group = wide_ref[c, pl.ds(pl.multiple_of(s // 8 * 8, 8), 8), :]
            line = pltpu.roll(group, (8 - s % 8) % 8, 0)[0:1, :]
            for r in range(tiles):
                row = line[:, r * BLOCK : (r + 1) * BLOCK]
                parts.append(jnp.broadcast_to(row, (8, BLOCK)) * own)
            parts.append(jnp.zeros((WIDE - 8 * tiles, BLOCK), jnp.float32))
            comps.append(jnp.concatenate(parts, axis=0).astype(jnp.bfloat16))
        grid = jnp.concatenate(comps, axis=1)
        phases = dot(spread, grid, NT)
        squares = jnp.zeros((PHASES, WIDE), jnp.float32)
        for c in range(3):
            x = phases[c * PHASES : (c + 1) * PHASES]
            squares = squares + x * x
            for r in range(REACH + 1):
                moved = x if r == 0 else pltpu.roll(x, WIDE - r, 1)
                at = c * L + r * PHASES if r < REACH else 3 * L + c * PHASES
                xs_ref[s, at : at + PHASES, :] = moved.astype(jnp.bfloat16)
        xs_ref[s, 3 * L + 3 * PHASES :, :] = jnp.zeros((DEPTH - 3 * L - 3 * PHASES, WIDE), jnp.bfloat16)
        up = squares
        down = jnp.where(sub >= 1, pltpu.roll(squares, 1, 0), 0.0)
        for step in (1, 2, 4, 8):
            up = up + jnp.where(sub < PHASES - step, pltpu.roll(up, PHASES - step, 0), 0.0)
            down = down + jnp.where(sub >= step, pltpu.roll(down, step, 0), 0.0)
        whole = jnp.broadcast_to(up[0:1, :], (PHASES, WIDE))
        two = whole + pltpu.roll(whole, WIDE - 1, 1)
        four = two + pltpu.roll(two, WIDE - 2, 1)
        eight = four + pltpu.roll(four, WIDE - 4, 1)
        fifteen = (
            pltpu.roll(eight, WIDE - 1, 1)
            + pltpu.roll(four, WIDE - 9, 1)
            + pltpu.roll(two, WIDE - 13, 1)
            + pltpu.roll(whole, WIDE - 15, 1)
        )
        power = (up + fifteen + pltpu.roll(down, WIDE - REACH, 1)) / (3.0 * L)
        inv_ref[s] = 1.0 / (3.0 * L * jnp.sqrt(power + EPS))


def correlate_kernel(got_ref, xs_ref, inv_ref, out_ref, sorted_ref, order_ref, held_ref, tails_ref, table_ref, sem):
    width = got_ref.shape[0]
    stations = xs_ref.shape[0]
    total = width * ROWS
    room = sorted_ref.shape[0]
    got = got_ref[...].reshape(total, DEPTH)
    pieces = got[:, : 3 * L]
    eye = (iota((8, BLOCK), 0) == iota((8, BLOCK), 1)).astype(jnp.bfloat16)
    fields = dot(eye, got[:, 3 * L :], NT)
    live = fields[2:3, :] > 0.5
    at_station = jnp.where(
        (iota((stations, total), 0) == fields[0:1, :].astype(jnp.int32)) & live, 1.0, 0.0
    )
    before = (iota((total, total), 0) < iota((total, total), 1)).astype(jnp.bfloat16)
    rank = dot(at_station.astype(jnp.bfloat16), before)
    chunks = jnp.floor((jnp.sum(at_station, axis=1, keepdims=True) + (CHUNK - 1)) / CHUNK)
    earlier = (iota((stations, stations), 1) < iota((stations, stations), 0)).astype(jnp.bfloat16)
    start = dot(earlier, jnp.broadcast_to(chunks, (stations, BLOCK)).astype(jnp.bfloat16))[:, 0:1]
    place = jnp.sum(at_station * (start * CHUNK + rank), axis=0, keepdims=True).astype(jnp.int32)
    place = jnp.where(live, place, -1)
    pick = (iota((room, total), 0) == place).astype(jnp.bfloat16)
    sorted_ref[...] = dot(pick, pieces)
    kind = iota((8, total), 0)
    rows = jnp.where(
        kind == 3,
        iota((8, total), 1).astype(jnp.float32),
        jnp.where(kind < 3, fields, 0.0),
    ).astype(jnp.bfloat16)
    table = dot(rows, pick, NT)
    table = jnp.where(iota((8, room), 0) == 4, jnp.sum(chunks), table)
    order_ref[...] = table.astype(jnp.int32)
    copy = pltpu.make_async_copy(order_ref, table_ref, sem)
    copy.start()
    copy.wait()

    u = iota((PHASES, L), 1)
    j = iota((PHASES, L), 0)
    late = u >= j
    early = (u < j)[:, :BLOCK]
    lane = iota((PHASES, BLOCK), 1)
    column = iota((PHASES, WIDE), 1)

    @pl.loop(0, table_ref[4, 0])
    def _(i):
        first = pl.multiple_of(i * CHUNK, CHUNK)
        s = table_ref[0, first]
        slot = sorted_ref[pl.ds(first, CHUNK), :]
        mean = jnp.sum(slot * slot, axis=1, keepdims=True) / (3.0 * L)
        unit = 1.0 / jnp.sqrt(mean + EPS)
        bands = []
        for k in range(CHUNK):
            tail = jnp.zeros((PHASES, BLOCK), jnp.float32)
            band = []
            for c in range(3):
                row = jnp.broadcast_to(slot[k : k + 1, c * L : (c + 1) * L], (PHASES, L))
                turned = pltpu.roll(row, 0, 1, stride=1, stride_axis=0)
                band.append(jnp.where(late, turned, 0.0).astype(jnp.bfloat16))
                rest = jnp.where(early, turned[:, :BLOCK], 0.0)
                tail = tail + (rest if c == 0 else pltpu.roll(rest, c * PHASES, 1))
            band.append(tail.astype(jnp.bfloat16))
            bands.append(jnp.concatenate(band, axis=1))
        corr = dot(jnp.concatenate(bands, axis=0), xs_ref[s])
        inv = inv_ref[s]
        for k in range(CHUNK):
            held_ref[k] = corr[k * PHASES : (k + 1) * PHASES] * inv * unit[k : k + 1, :]
        for k in range(CHUNK):

            @pl.when(table_ref[2, first + k] > 0)
            def _(k=k):
                move = table_ref[1, first + k]
                target = table_ref[3, first + k]
                o = target // ROWS
                rk = target % ROWS
                y = pltpu.roll(held_ref[k], (WIDE - move * (BLOCK // PHASES)) % WIDE, 1)
                y = jnp.where(column < KEPT, y, 0.0)
                top = jnp.max(jnp.abs(y), axis=1, keepdims=True)
                power = jnp.zeros_like(top)
                for step in (64, 32, 16, 8, 4, 2, 1):
                    small = top < 2.0**-step
                    top = jnp.where(small, top * 2.0**step, top)
                    power = power + jnp.where(small, float(step), 0.0)
                scale = jnp.full_like(top, 32767.0)
                for step in (64, 32, 16, 8, 4, 2, 1):
                    on = jnp.floor(power / step) - 2.0 * jnp.floor(power / (2 * step)) > 0.5
                    scale = jnp.where(on, scale * 2.0**step, scale)
                q = jnp.clip(jnp.round(y * scale), -32767.0, 32767.0).astype(jnp.int32)
                out_ref[o, 2 * rk] = q[:, :BLOCK].astype(jnp.int16)
                out_ref[o, 2 * rk + 1] = q[:, BLOCK : 2 * BLOCK].astype(jnp.int16)
                left = 32 * (rk % 4)
                end = pltpu.roll(q[:, 2 * BLOCK :], left, 1)
                b = rk // 4
                tails_ref[o, b] = jnp.where((lane >= left) & (lane < left + 32), end, tails_ref[o, b])
                tails_ref[o, 1] = jnp.where(lane == 64 + rk, power.astype(jnp.int32), tails_ref[o, 1])

    @pl.loop(0, width)
    def _(o):
        out_ref[o, 12] = tails_ref[o, 0].astype(jnp.int16)
        out_ref[o, 13] = tails_ref[o, 1].astype(jnp.int16)


def add_kernel(dest_ref, count_ref, back_ref, stack_ref, best_ref):
    lane = iota((PHASES, BLOCK), 1)

    def one_template(t, best):
        count = count_ref[t]

        def one_slot(k, total):
            dest = dest_ref[0, k * 8 + t]
            o = dest // ROWS
            rk = dest % ROWS
            power = pltpu.roll(
                back_ref[o, 13].astype(jnp.int32).astype(jnp.float32), (64 - rk) % BLOCK, 1
            )[:, 0:1]
            scale = jnp.full_like(power, 1.0 / 32767.0)
            for step in (64, 32, 16, 8, 4, 2, 1):
                on = jnp.floor(power / step) - 2.0 * jnp.floor(power / (2 * step)) > 0.5
                scale = jnp.where(on, scale * 2.0**-step, scale)
            tail = back_ref[o, 12 + rk // 4].astype(jnp.int32)
            tail = pltpu.roll(tail, (BLOCK - 32 * (rk % 4)) % BLOCK, 1)
            parts = (
                back_ref[o, 2 * rk].astype(jnp.int32),
                back_ref[o, 2 * rk + 1].astype(jnp.int32),
                tail,
            )
            return tuple(a + p.astype(jnp.float32) * scale for a, p in zip(total, parts))

        zero = jnp.zeros((PHASES, BLOCK), jnp.float32)
        total = lax.fori_loop(0, count, one_slot, (zero, zero, zero))
        factor = jnp.sqrt(3.0 * L / jnp.full((1, 1), count, jnp.int32).astype(jnp.float32))
        whole = jnp.concatenate(total, axis=1) * factor
        stack_ref[t] = whole[:, :KEPT]
        return jnp.maximum(best, whole)

    start = jnp.full((PHASES, WIDE), -jnp.inf, jnp.float32)
    best = lax.fori_loop(0, stack_ref.shape[0], one_template, start)
    best_ref[...] = best[:, :KEPT]


VMEM = pl.BlockSpec(memory_space=pltpu.VMEM)
SMEM = pl.BlockSpec(memory_space=pltpu.SMEM)


def params(mib):
    return pltpu.CompilerParams(vmem_limit_bytes=mib * 2**20)


def body(waveforms, station_home, templates, template_stations, station_counts, moveouts):
    stations, _, samples = waveforms.shape
    tpl_dev = templates.shape[0]
    width = lax.axis_size("sta")
    total = tpl_dev * SLOTS
    slots = jnp.stack(
        [template_stations.T.reshape(total), moveouts.T.reshape(total), jnp.tile(station_counts, SLOTS)]
    )
    send, dest = pl.pallas_call(
        pack_kernel,
        out_shape=(
            jax.ShapeDtypeStruct((width, ROWS, DEPTH), jnp.bfloat16),
            jax.ShapeDtypeStruct((1, total), jnp.int32),
        ),
        in_specs=[VMEM] * 3,
        out_specs=(VMEM, VMEM),
        compiler_params=params(32),
    )(slots, station_home.reshape(1, -1), templates.transpose(1, 0, 2).reshape(total, 3 * L))
    got = lax.all_to_all(send, "sta", split_axis=0, concat_axis=0, tiled=True)
    xs, inv = pl.pallas_call(
        prep_kernel,
        out_shape=(
            jax.ShapeDtypeStruct((stations, DEPTH, WIDE), jnp.bfloat16),
            jax.ShapeDtypeStruct((stations, PHASES, WIDE), jnp.float32),
        ),
        in_specs=[VMEM],
        out_specs=(VMEM, VMEM),
        scratch_shapes=[pltpu.VMEM((3, stations, samples), jnp.float32)],
        compiler_params=params(32),
        cost_estimate=pl.CostEstimate(flops=2 * 10**9, bytes_accessed=12 * 2**20, transcendentals=0),
    )(waveforms.transpose(1, 0, 2))
    room = 8 * (width * CAP // CHUNK + stations)
    traces = pl.pallas_call(
        correlate_kernel,
        out_shape=jax.ShapeDtypeStruct((width, BLOCKS, PHASES, BLOCK), jnp.int16),
        in_specs=[VMEM] * 3,
        out_specs=VMEM,
        scratch_shapes=[
            pltpu.VMEM((room, 3 * L), jnp.float32),
            pltpu.VMEM((8, room), jnp.int32),
            pltpu.VMEM((CHUNK, PHASES, WIDE), jnp.float32),
            pltpu.VMEM((width, 2, PHASES, BLOCK), jnp.int32),
            pltpu.SMEM((8, room), jnp.int32),
            pltpu.SemaphoreType.DMA,
        ],
        compiler_params=params(40),
    )(got, xs, inv)
    back = lax.all_to_all(traces, "sta", split_axis=0, concat_axis=0, tiled=True)
    stack, best = pl.pallas_call(
        add_kernel,
        out_shape=(
            jax.ShapeDtypeStruct((tpl_dev, PHASES, KEPT), jnp.float32),
            jax.ShapeDtypeStruct((PHASES, KEPT), jnp.float32),
        ),
        in_specs=[SMEM, SMEM, VMEM],
        out_specs=(VMEM, VMEM),
        compiler_params=params(32),
    )(dest, station_counts, back)
    stack = stack.transpose(0, 2, 1).reshape(tpl_dev, PHASES * KEPT)
    best = best.T.reshape(PHASES * KEPT)
    network = best_of_all(best.reshape(-1, BLOCK)).reshape(PHASES * KEPT)
    return (stack, network)


def best_of_all(best):
    for axis in ("tpl", "sta"):
        size = lax.axis_size(axis)
        step = 1
        while step < size:
            other = lax.ppermute(best, axis, [(i, i ^ step) for i in range(size)])
            best = jnp.maximum(best, other)
            step *= 2
    return best


def solution(mesh):
    in_specs = (
        P("sta", None, None),
        P(),
        P(("sta", "tpl"), None, None),
        P(("sta", "tpl"), None),
        P(("sta", "tpl")),
        P(("sta", "tpl"), None),
    )
    out_specs = (P(("sta", "tpl"), None), P())
    return jax.shard_map(body, mesh=mesh, in_specs=in_specs, out_specs=out_specs, check_vma=False)
```

time: 828 us -> 169 us (0.20)
  local copies, waits for them, and re-layouts: 513 us -> 15.4 us
  blocking collectives: 143 us -> 37.1 us
  Pallas kernels: 0 us -> 66.1 us
  matrix products: 50.4 us -> 0 us
  other arithmetic: 39.3 us -> 0.65 us
  waiting for transfers between devices: 52.7 us -> 30.3 us
  between operations: 15 us -> 0.76 us
  starting transfers between devices: 5.06 us -> 17.5 us
    another operation x40 -> x5, local copies, waits for them, and re-layouts: 208 us -> 1.02 us  [the longest x1 0.66 us: body(): jnp.tile(station_counts, SLOTS)]
    gather x79 -> x0, local copies, waits for them, and re-layouts: 118 us -> none  [the longest x16 50.3 us: correlate(): window = station_windows[rows]]
    reshape x50 -> x1, local copies, waits for them, and re-layouts: 81.9 us -> 1.36 us  [body(): stack = stack.transpose(0, 2, 1).reshape(tpl_dev, PHASES * KEPT)]
    pmax x1 -> x0, blocking collectives: 80 us -> none  [body(): network = lax.pmax(jnp.max(stack, axis=0), ('sta', 'tpl'))]
    slice x17 -> x0, local copies, waits for them, and re-layouts: 77.1 us -> none  [the longest x16 76.8 us: toeplitz(): flat[..., :BLOCK * (length + BLOCK)]]
    pallas_call x0 -> x4, Pallas kernels: none -> 66.1 us  [the longest x1 38.4 us: body(): pl.pallas_call(correlate_kernel, out_shape=jax.ShapeDtypeStruct((width, B...]
    all_to_all x1, waiting for transfers between devices: 52 us -> 0.01 us  [body(): got = lax.all_to_all(send, 'sta', split_axis=0, concat_axis=0, tiled=True)]
    dot_general x18 -> x0, matrix products: 50.4 us -> none  [the longest x16 43 us: correlate(): jnp.einsum('pcbu,pcju->pbj', window, toeplitz(split), preferred_element_t...]
  transfers between devices with their start and end apart: 2 -> 9, of which waited for: 1 -> 8; matrix products, arithmetic and copies ran while one was open for 3% -> 1% of each run, Pallas kernels for 0% -> 6%
where the time goes in v1:
time: 169 us; the launch traced here: 168 us
  Pallas kernels  66.1 us (39%)
  blocking collectives  37.1 us (22%)
  waiting for transfers between devices  30.3 us (18%)
  starting transfers between devices  17.5 us (10%)
  local copies, waits for them, and re-layouts  15.4 us (9%)
    pallas_call x1, Pallas kernels, body(): pl.pallas_call(correlate_kernel, out_shape=jax.ShapeDtypeStruct((width, B...  38.4 us
    all_to_all x1, blocking collectives, body(): lax.all_to_all(traces, 'sta', split_axis=0, concat_axis=0, tiled=True)  37.1 us
    ppermute x8, waiting for transfers between devices, best_of_all(): other = lax.ppermute(best, axis, [(i, i ^ step) for i in range(size)])  30.3 us
    pallas_call x1, Pallas kernels, body(): pl.pallas_call(add_kernel, out_shape=(jax.ShapeDtypeStruct((tpl_dev, PHAS...  16.4 us
    unnamed x12, local copies, waits for them, and re-layouts  11 us
    ppermute x8, starting transfers between devices, best_of_all(): other = lax.ppermute(best, axis, [(i, i ^ step) for i in range(size)])  10.2 us
    pallas_call x1, Pallas kernels, body(): pl.pallas_call(prep_kernel, out_shape=(jax.ShapeDtypeStruct((stations, DE...  9.87 us
    all_to_all x1, starting transfers between devices, body(): got = lax.all_to_all(send, 'sta', split_axis=0, concat_axis=0, tiled=True)  7.32 us
  transfers between devices with their start and end apart: 9, of which 8 were waited for; matrix products, arithmetic and copies ran while one was open for 1% of the time, Pallas kernels for 6%

profile of v1, /device:TPU:32, one launch (start us, length us, event | category | flops | bytes accessed | tf_op | source)
XLA Modules:
  0.0 167.7 jit_solution(6378408012927959488)
XLA Ops:
  0.6 0.8 copy.10
  1.4 0.1 stack_reshape.6
  1.5 0.8 copy.11
  2.3 0.1 stack_reshape.7
  2.4 0.7 tile.2
  3.0 0.1 stack_tile.3
  3.1 0.0 copy-start.2
  3.1 0.9 copy-done.2
  4.1 0.0 copy-start.3
  4.1 0.7 copy-done.3
  4.7 1.4 shard_map.77
  6.1 7.3 %all-to-all-start = ((bf16[32,8,896]{2,1,0:T(8,128)(2,1)}), bf16[32,8,896]{2,1,0:T(8,128)(2,1)S(1)}, u32[]{:S(2)}, u32[]{:S(2)}) async-start(bf16[32,8,896]{2,1,0:T(8,128)(2,1)} %get-tuple-element.9), calls=%async_computation | async-start | bytes 917504 | tf_op jit(solution)/shard_map/all_to_all | solution.py:294
  13.5 0.0 copy-start.5
  13.5 1.0 copy-done.5
  14.5 9.9 %shard_map.78 = (bf16[16,896,384]{2,1,0:T(8,128)(2,1)S(1)}, f32[16,16,384]{2,1,0:T(8,128)S(1)}) custom-call(bf16[3,16,5376]{2,1,0:T(8,128)(2,1)S(1)} %bitcast.15), custom_call_target="tpu_custom_call" | custom-call | flops 2000000000 | bytes 12582912 | tf_op jit(solution)/shard_map/pallas_call | solution.py:295
  24.4 0.0 copy-start
  24.4 4.2 %copy-done = bf16[16,896,384]{2,1,0:T(8,128)(2,1)} copy-done((bf16[16,896,384]{2,1,0:T(8,128)(2,1)}, bf16[16,896,384]{2,1,0:T(8,128)(2,1)S(1)}, u32[]{:S(2)}) %copy-start) | copy-done | bytes 11010072
  28.6 0.0 all-to-all-done.got_ref
  28.6 0.0 copy-start.1
  28.6 4.1 %copy-done.1 = bf16[16,896,384]{2,1,0:T(8,128)(2,1)S(1)} copy-done((bf16[16,896,384]{2,1,0:T(8,128)(2,1)S(1)}, bf16[16,896,384]{2,1,0:T(8,128)(2,1)}, u32[]{:S(2)}) %copy-start.1) | copy-done | bytes 11010072
  32.7 38.4 %shard_map.79 = s16[32,14,16,128]{3,2,1,0:T(8,128)(2,1)S(1)} custom-call(bf16[32,8,896]{2,1,0:T(8,128)(2,1)S(1)} %all-to-all-done.got_ref, bf16[16,896,384]{2,1,0:T(8,128)(2,1)S(1)} %copy-done.1, f32[16,16,384]{2,1,0:T(8,128)S(1)} %get-tuple-element.11.inv_ref), custom_call_target="tpu_custom_call" | custom-call | tf_op jit(solution)/shard_map/pallas_call | solution.py:308
  71.1 0.0 copy-start.4
  71.1 37.1 %all_to_all.10.back_ref = s16[32,14,16,128]{3,2,1,0:T(8,128)(2,1)S(1)} all-to-all(s16[32,14,16,128]{3,2,1,0:T(8,128)(2,1)S(1)} %shard_map.79), channel_id=1, replica_groups=mesh['sta'=32,'tpl'=8] {'sta'}, dimensions={0} | all-to-all | bytes 3670016 | tf_op jit(solution)/shard_map/all_to_all | solution.py:323
  108.2 0.0 copy-done.4
  108.2 16.4 %shard_map.80 = (f32[8,16,288]{2,1,0:T(8,128)S(1)}, f32[16,288]{1,0:T(8,128)S(1)}) custom-call(s32[1,160]{1,0:T(1,128)S(1)} %get-tuple-element.8.dest_ref, s32[8]{0:T(128)S(1)} %copy-done.4, s16[32,14,16,128]{3,2,1,0:T(8,128)(2,1)S(1)} %all_to_all.10.back_ref), custom_call_target="tpu_custom_call" | custom-call | tf_op jit(solution)/shard_map/pallas_call | solution.py:324
  124.6 0.1 copy.13
  124.7 0.1 reshape_reshape.3
  124.9 8.8 %collective-permute-start = (f32[36,128]{1,0:T(8,128)S(1)}, f32[36,128]{1,0:T(8,128)S(1)}, u32[]{:S(2)}, u32[]{:S(2)}) collective-permute-start(f32[36,128]{1,0:T(8,128)S(1)} %reshape_reshape.3), channel_id=1, source_target_pairs={{0,1},{1,0},{2,3},{3,2},{4,5},{5,4},{6,7},{7,6},{8,9},{9,8},{10,11... | collective-permute-start | bytes 55304 | tf_op jit(solution)/shard_map/ppermute | solution.py:345
  133.6 1.8 %collective-permute-done = f32[36,128]{1,0:T(8,128)S(1)} collective-permute-done((f32[36,128]{1,0:T(8,128)S(1)}, f32[36,128]{1,0:T(8,128)S(1)}, u32[]{:S(2)}, u32[]{:S(2)}) %collective-permute-start) | collective-permute-done | bytes 18464 | tf_op jit(solution)/shard_map/ppermute | solution.py:345
  135.4 0.0 collective-permute-start.1
  135.4 4.7 %collective-permute-done.1 = f32[36,128]{1,0:T(8,128)S(1)} collective-permute-done((f32[36,128]{1,0:T(8,128)S(1)}, f32[36,128]{1,0:T(8,128)S(1)}, u32[]{:S(2)}, u32[]{:S(2)}) %collective-permute-start.1) | collective-permute-done | bytes 18464 | tf_op jit(solution)/shard_map/ppermute | solution.py:345
  140.1 0.0 collective-permute-start.2
  140.1 7.7 %collective-permute-done.2 = f32[36,128]{1,0:T(8,128)S(1)} collective-permute-done((f32[36,128]{1,0:T(8,128)S(1)}, f32[36,128]{1,0:T(8,128)S(1)}, u32[]{:S(2)}, u32[]{:S(2)}) %collective-permute-start.2) | collective-permute-done | bytes 18464 | tf_op jit(solution)/shard_map/ppermute | solution.py:345
  147.8 0.0 collective-permute-start.3
  147.8 1.2 collective-permute-done.3
  149.0 0.0 collective-permute-start.4
  149.0 3.8 %collective-permute-done.4 = f32[36,128]{1,0:T(8,128)S(1)} collective-permute-done((f32[36,128]{1,0:T(8,128)S(1)}, f32[36,128]{1,0:T(8,128)S(1)}, u32[]{:S(2)}, u32[]{:S(2)}) %collective-permute-start.4) | collective-permute-done | bytes 18464 | tf_op jit(solution)/shard_map/ppermute | solution.py:345
  152.8 1.0 collective-permute-start.5
  153.7 4.3 %collective-permute-done.5 = f32[36,128]{1,0:T(8,128)S(1)} collective-permute-done((f32[36,128]{1,0:T(8,128)S(1)}, f32[36,128]{1,0:T(8,128)S(1)}, u32[]{:S(2)}, u32[]{:S(2)}) %collective-permute-start.5) | collective-permute-done | bytes 18464 | tf_op jit(solution)/shard_map/ppermute | solution.py:345
  158.1 0.4 collective-permute-start.6
  158.5 3.4 %collective-permute-done.6 = f32[36,128]{1,0:T(8,128)S(1)} collective-permute-done((f32[36,128]{1,0:T(8,128)S(1)}, f32[36,128]{1,0:T(8,128)S(1)}, u32[]{:S(2)}, u32[]{:S(2)}) %collective-permute-start.6) | collective-permute-done | bytes 18464 | tf_op jit(solution)/shard_map/ppermute | solution.py:345
  161.8 0.0 collective-permute-start.7
  161.8 0.4 copy.12
  162.2 1.4 reshape.19
  163.6 3.5 %collective-permute-done.7 = f32[36,128]{1,0:T(8,128)S(1)} collective-permute-done((f32[36,128]{1,0:T(8,128)S(1)}, f32[36,128]{1,0:T(8,128)S(1)}, u32[]{:S(2)}, u32[]{:S(2)}) %collective-permute-start.7) | collective-permute-done | bytes 18464 | tf_op jit(solution)/shard_map/ppermute | solution.py:345
  167.1 0.6 maximum_bitcast_fusion
  (8 shorter events, 0.0 us)
Async XLA Ops:
  3.1 0.9 copy-start.2
  4.1 0.7 copy-start.3
  6.1 22.4 %all-to-all-start = ((bf16[32,8,896]{2,1,0:T(8,128)(2,1)}), bf16[32,8,896]{2,1,0:T(8,128)(2,1)S(1)}, u32[]{:S(2)}, u32[]{:S(2)}) async-start(bf16[32,8,896]{2,1,0:T(8,128)(2,1)} %get-tuple-element.9), calls=%async_computation | async-start | bytes 917504 | tf_op jit(solution)/shard_map/all_to_all | solution.py:294
  13.5 1.0 copy-start.5
  24.4 4.2 %copy-start = (bf16[16,896,384]{2,1,0:T(8,128)(2,1)}, bf16[16,896,384]{2,1,0:T(8,128)(2,1)S(1)}, u32[]{:S(2)}) copy-start(bf16[16,896,384]{2,1,0:T(8,128)(2,1)S(1)} %get-tuple-element.10.xs_ref) | copy-start | bytes 33030148
  28.6 4.1 %copy-start.1 = (bf16[16,896,384]{2,1,0:T(8,128)(2,1)S(1)}, bf16[16,896,384]{2,1,0:T(8,128)(2,1)}, u32[]{:S(2)}) copy-start(bf16[16,896,384]{2,1,0:T(8,128)(2,1)} %copy-done) | copy-start | bytes 33030148
  71.1 37.1 %copy-start.4 = (s32[8]{0:T(128)S(1)}, s32[8]{0:T(128)}, u32[]{:S(2)}) copy-start(s32[8]{0:T(128)} %count_ref.1) | copy-start | bytes 100
  124.9 10.5 %collective-permute-start = (f32[36,128]{1,0:T(8,128)S(1)}, f32[36,128]{1,0:T(8,128)S(1)}, u32[]{:S(2)}, u32[]{:S(2)}) collective-permute-start(f32[36,128]{1,0:T(8,128)S(1)} %reshape_reshape.3), channel_id=1, source_target_pairs={{0,1},{1,0},{2,3},{3,2},{4,5},{5,4},{6,7},{7,6},{8,9},{9,8},{10,11... | collective-permute-start | bytes 55304 | tf_op jit(solution)/shard_map/ppermute | solution.py:345
  135.4 4.7 %collective-permute-start.1 = (f32[36,128]{1,0:T(8,128)S(1)}, f32[36,128]{1,0:T(8,128)S(1)}, u32[]{:S(2)}, u32[]{:S(2)}) collective-permute-start(f32[36,128]{1,0:T(8,128)S(1)} %max.24), channel_id=1, source_target_pairs={{0,2},{1,3},{2,0},{3,1},{4,6},{5,7},{6,4},{7,5},{8,10},{9,11},{10,... | collective-permute-start | bytes 55304 | tf_op jit(solution)/shard_map/ppermute | solution.py:345
  140.1 7.7 %collective-permute-start.2 = (f32[36,128]{1,0:T(8,128)S(1)}, f32[36,128]{1,0:T(8,128)S(1)}, u32[]{:S(2)}, u32[]{:S(2)}) collective-permute-start(f32[36,128]{1,0:T(8,128)S(1)} %max.25), channel_id=1, source_target_pairs={{0,4},{1,5},{2,6},{3,7},{4,0},{5,1},{6,2},{7,3},{8,12},{9,13},{10,... | collective-permute-start | bytes 55304 | tf_op jit(solution)/shard_map/ppermute | solution.py:345
  147.8 1.2 collective-permute-start.3
  149.0 3.8 %collective-permute-start.4 = (f32[36,128]{1,0:T(8,128)S(1)}, f32[36,128]{1,0:T(8,128)S(1)}, u32[]{:S(2)}, u32[]{:S(2)}) collective-permute-start(f32[36,128]{1,0:T(8,128)S(1)} %max.27), channel_id=1, source_target_pairs={{0,16},{8,24},{16,0},{24,8},{32,48},{40,56},{48,32},{56,40},{64,80... | collective-permute-start | bytes 55304 | tf_op jit(solution)/shard_map/ppermute | solution.py:345
  152.8 5.3 %collective-permute-start.5 = (f32[36,128]{1,0:T(8,128)S(1)}, f32[36,128]{1,0:T(8,128)S(1)}, u32[]{:S(2)}, u32[]{:S(2)}) collective-permute-start(f32[36,128]{1,0:T(8,128)S(1)} %max.28), channel_id=1, source_target_pairs={{0,32},{8,40},{16,48},{24,56},{32,0},{40,8},{48,16},{56,24},{64,96... | collective-permute-start | bytes 55304 | tf_op jit(solution)/shard_map/ppermute | solution.py:345
  158.1 3.8 %collective-permute-start.6 = (f32[36,128]{1,0:T(8,128)S(1)}, f32[36,128]{1,0:T(8,128)S(1)}, u32[]{:S(2)}, u32[]{:S(2)}) collective-permute-start(f32[36,128]{1,0:T(8,128)S(1)} %max.29), channel_id=1, source_target_pairs={{0,64},{8,72},{16,80},{24,88},{32,96},{40,104},{48,112},{56,120},{... | collective-permute-start | bytes 55304 | tf_op jit(solution)/shard_map/ppermute | solution.py:345
  161.8 5.3 %collective-permute-start.7 = (f32[36,128]{1,0:T(8,128)S(1)}, f32[36,128]{1,0:T(8,128)S(1)}, u32[]{:S(2)}, u32[]{:S(2)}) collective-permute-start(f32[36,128]{1,0:T(8,128)S(1)} %max.30), channel_id=1, source_target_pairs={{0,128},{8,136},{16,144},{24,152},{32,160},{40,168},{48,176},{56,1... | collective-permute-start | bytes 55304 | tf_op jit(solution)/shard_map/ppermute | solution.py:345

commit v2 on v1

v2 whole, which is shorter than its diff:
```python
import functools

import jax
import jax.numpy as jnp
from jax import lax
from jax.experimental import pallas as pl
from jax.experimental.pallas import tpu as pltpu
from jax.sharding import PartitionSpec as P

SLOTS = 20
L = 256
BLOCK = 128
LAG_BLOCKS = 40
MOVE_BLOCKS = 4
EPS = 1e-06

PHASES = 16
COLS = LAG_BLOCKS * BLOCK // PHASES
KEPT = (LAG_BLOCKS - MOVE_BLOCKS) * BLOCK // PHASES
WIDE = 384
REACH = L // PHASES
DEPTH = 3 * L + BLOCK
CHUNK = 8
CAP = 6
ROWS = 8
BLOCKS = 14

FINE = 8.0
FULL = 32700.0
NT = (((1,), (1,)), ((), ()))


def iota(shape, dim):
    return lax.broadcasted_iota(jnp.int32, shape, dim)


def dot(a, b, dims=None):
    if dims is None:
        dims = (((1,), (0,)), ((), ()))
    return lax.dot_general(a, b, dims, preferred_element_type=jnp.float32)


def pack_kernel(
    stations_hbm, moves_hbm, counts_hbm, home_hbm, templates_hbm, send_ref, dest_ref,
    stations_ref, moves_ref, counts_ref, home_ref, templates_ref, sems,
):
    copies = [
        pltpu.make_async_copy(src, dst, sems.at[i])
        for i, (src, dst) in enumerate(
            (
                (stations_hbm, stations_ref),
                (moves_hbm, moves_ref),
                (counts_hbm, counts_ref),
                (home_hbm, home_ref),
                (templates_hbm, templates_ref),
            )
        )
    ]
    for copy in copies:
        copy.start()
    tpl_dev, slots = stations_ref.shape
    total = tpl_dev * slots
    width = send_ref.shape[0]
    parts = home_ref.shape[0]
    sta_dev = parts * BLOCK // width
    place = iota((1, total), 1)
    of_template = place % tpl_dev
    for copy in copies[:4]:
        copy.wait()
    stations = stations_ref[...]
    high = stations // 16
    fields = jnp.concatenate([high, stations - 16 * high, moves_ref[...]], axis=0)
    expand = (iota((slots, total), 1) // tpl_dev == iota((slots, total), 0)).astype(jnp.bfloat16)
    spread = dot(fields.astype(jnp.float32).astype(jnp.bfloat16), expand)
    mine = iota((tpl_dev, total), 0) == of_template
    rows = [
        jnp.sum(jnp.where(mine, spread[i * tpl_dev : (i + 1) * tpl_dev], 0.0), axis=0, keepdims=True)
        for i in range(3)
    ]
    station = (rows[0] * 16.0 + rows[1]).astype(jnp.int32)
    moves = rows[2]
    counts = jnp.zeros((1, total), jnp.int32)
    for t in range(tpl_dev):
        counts = jnp.where(of_template == t, counts_ref[t], counts)
    home = home_ref[...]
    owners = home // sta_dev
    table = jnp.concatenate([owners, home - owners * sta_dev], axis=0)
    hit = (iota((BLOCK, total), 0) == station % BLOCK).astype(jnp.bfloat16)
    found = dot(table.astype(jnp.float32).astype(jnp.bfloat16), hit)
    part = iota((parts, total), 0) == station // BLOCK
    owner = jnp.sum(jnp.where(part, found[:parts], 0.0), axis=0, keepdims=True).astype(jnp.int32)
    local = jnp.sum(jnp.where(part, found[parts:], 0.0), axis=0, keepdims=True)
    live = place // tpl_dev < counts
    at_owner = jnp.where((iota((width, total), 0) == owner) & live, 1.0, 0.0)
    before = (iota((total, total), 0) < iota((total, total), 1)).astype(jnp.bfloat16)
    rank = jnp.sum(at_owner * dot(at_owner.astype(jnp.bfloat16), before), axis=0, keepdims=True)
    dest = jnp.where(live, owner * ROWS + rank.astype(jnp.int32), -1)
    dest_ref[...] = dest
    pick = (iota((width * ROWS, total), 0) == dest).astype(jnp.bfloat16)
    kind = iota((BLOCK, total), 0)
    fields = jnp.where(
        kind == 0, local, jnp.where(kind == 1, moves, jnp.where(kind == 2, 1.0, 0.0))
    ).astype(jnp.bfloat16)
    tail = dot(pick, fields, NT).astype(jnp.bfloat16)
    copies[4].wait()
    send = dot(pick, templates_ref[...].reshape(total, 3 * L)).astype(jnp.bfloat16)
    send_ref[:, :, : 3 * L] = send.reshape(width, ROWS, 3 * L)
    send_ref[:, :, 3 * L :] = tail.reshape(width, ROWS, BLOCK)


def prep_kernel(wave_ref, xs_ref, inv_ref, wide_ref):
    tiles = wave_ref.shape[2] // BLOCK

    @pl.when(pl.program_id(0) == 0)
    def _():
        wide_ref[...] = wave_ref[...].astype(jnp.float32)

    lane = iota((8, BLOCK), 1)
    own = (lane // PHASES == iota((8, BLOCK), 0)).astype(jnp.float32)
    spread = (
        (iota((3 * PHASES, 3 * BLOCK), 1) // BLOCK == iota((3 * PHASES, 3 * BLOCK), 0) // PHASES)
        & (iota((3 * PHASES, 3 * BLOCK), 1) % PHASES == iota((3 * PHASES, 3 * BLOCK), 0) % PHASES)
    ).astype(jnp.bfloat16)
    sub = iota((PHASES, WIDE), 0)
    s = pl.program_id(0)

    def one_station():
        comps = []
        for c in range(3):
            parts = []
            group = wide_ref[c, pl.ds(pl.multiple_of(s // 8 * 8, 8), 8), :]
            line = pltpu.roll(group, (8 - s % 8) % 8, 0)[0:1, :]
            for r in range(tiles):
                row = line[:, r * BLOCK : (r + 1) * BLOCK]
                parts.append(jnp.broadcast_to(row, (8, BLOCK)) * own)
            parts.append(jnp.zeros((WIDE - 8 * tiles, BLOCK), jnp.float32))
            comps.append(jnp.concatenate(parts, axis=0).astype(jnp.bfloat16))
        grid = jnp.concatenate(comps, axis=1)
        phases = dot(spread, grid, NT)
        squares = jnp.zeros((PHASES, WIDE), jnp.float32)
        for c in range(3):
            x = phases[c * PHASES : (c + 1) * PHASES]
            squares = squares + x * x
            for r in range(REACH + 1):
                moved = x if r == 0 else pltpu.roll(x, WIDE - r, 1)
                at = c * L + r * PHASES if r < REACH else 3 * L + c * PHASES
                xs_ref[0, at : at + PHASES, :] = moved.astype(jnp.bfloat16)
        xs_ref[0, 3 * L + 3 * PHASES :, :] = jnp.zeros((DEPTH - 3 * L - 3 * PHASES, WIDE), jnp.bfloat16)
        up = squares
        down = jnp.where(sub >= 1, pltpu.roll(squares, 1, 0), 0.0)
        for step in (1, 2, 4, 8):
            up = up + jnp.where(sub < PHASES - step, pltpu.roll(up, PHASES - step, 0), 0.0)
            down = down + jnp.where(sub >= step, pltpu.roll(down, step, 0), 0.0)
        whole = jnp.broadcast_to(up[0:1, :], (PHASES, WIDE))
        two = whole + pltpu.roll(whole, WIDE - 1, 1)
        four = two + pltpu.roll(two, WIDE - 2, 1)
        eight = four + pltpu.roll(four, WIDE - 4, 1)
        fifteen = (
            pltpu.roll(eight, WIDE - 1, 1)
            + pltpu.roll(four, WIDE - 9, 1)
            + pltpu.roll(two, WIDE - 13, 1)
            + pltpu.roll(whole, WIDE - 15, 1)
        )
        power = (up + fifteen + pltpu.roll(down, WIDE - REACH, 1)) / (3.0 * L)
        inv_ref[0] = 1.0 / (3.0 * L * jnp.sqrt(power + EPS))

    one_station()


def correlate_kernel(
    got_ref, xs_hbm, inv_ref, out_ref, xs_ref, sorted_ref, order_ref, held_ref, table_ref, sem, xs_sems
):
    width = got_ref.shape[0]
    stations = xs_ref.shape[0]
    total = width * ROWS
    room = sorted_ref.shape[0]
    loads = [pltpu.make_async_copy(xs_hbm.at[s], xs_ref.at[s], xs_sems.at[s]) for s in range(stations)]
    for load in loads:
        load.start()
    got = got_ref[...].reshape(total, DEPTH)
    pieces = got[:, : 3 * L]
    eye = (iota((8, BLOCK), 0) == iota((8, BLOCK), 1)).astype(jnp.bfloat16)
    fields = dot(eye, got[:, 3 * L :], NT)
    live = fields[2:3, :] > 0.5
    at_station = jnp.where(
        (iota((stations, total), 0) == fields[0:1, :].astype(jnp.int32)) & live, 1.0, 0.0
    )
    before = (iota((total, total), 0) < iota((total, total), 1)).astype(jnp.bfloat16)
    rank = dot(at_station.astype(jnp.bfloat16), before)
    chunks = jnp.floor((jnp.sum(at_station, axis=1, keepdims=True) + (CHUNK - 1)) / CHUNK)
    earlier = (iota((stations, stations), 1) < iota((stations, stations), 0)).astype(jnp.bfloat16)
    start = dot(earlier, jnp.broadcast_to(chunks, (stations, BLOCK)).astype(jnp.bfloat16))[:, 0:1]
    place = jnp.sum(at_station * (start * CHUNK + rank), axis=0, keepdims=True).astype(jnp.int32)
    place = jnp.where(live, place, -1)
    pick = (iota((room, total), 0) == place).astype(jnp.bfloat16)
    kind = iota((8, total), 0)
    rows = jnp.where(
        kind == 3, iota((8, total), 1).astype(jnp.float32), jnp.where(kind < 3, fields, 0.0)
    ).astype(jnp.bfloat16)
    table = dot(rows, pick, NT)
    kind = iota((8, room), 0)
    table = jnp.where((kind == 3) & (table[2:3, :] < 0.5), float(total), table)
    table = jnp.where(kind == 4, jnp.sum(chunks), table)
    order_ref[...] = table.astype(jnp.int32)
    copy = pltpu.make_async_copy(order_ref, table_ref, sem)
    copy.start()
    sorted_ref[...] = dot(pick, pieces)
    copy.wait()
    for load in loads:
        load.wait()

    sub = iota((PHASES, BLOCK), 0)
    lane = iota((PHASES, BLOCK), 1)
    late = lane >= sub

    def toeplitz(slot):
        bands = []
        for k in range(CHUNK):
            tail = jnp.zeros((PHASES, BLOCK), jnp.float32)
            band = []
            for c in range(3):
                turned = []
                for h in range(2):
                    at = c * L + h * BLOCK
                    row = jnp.broadcast_to(slot[k : k + 1, at : at + BLOCK], (PHASES, BLOCK))
                    turned.append(pltpu.roll(row, 0, 1, stride=1, stride_axis=0))
                band.append(jnp.where(late, turned[0], 0.0).astype(jnp.bfloat16))
                band.append(jnp.where(late, turned[1], turned[0]).astype(jnp.bfloat16))
                rest = jnp.where(late, 0.0, turned[1])
                tail = tail + (rest if c == 0 else pltpu.roll(rest, c * PHASES, 1))
            band.append(tail.astype(jnp.bfloat16))
            bands.append(jnp.concatenate(band, axis=1))
        return jnp.concatenate(bands, axis=0)

    def chunk(i):
        first = pl.multiple_of(i * CHUNK, CHUNK)
        s = table_ref[0, first]
        slot = sorted_ref[pl.ds(first, CHUNK), :]
        mean = jnp.sum(slot * slot, axis=1, keepdims=True) / (3.0 * L)
        unit = 1.0 / jnp.sqrt(mean + EPS)
        corr = dot(toeplitz(slot), xs_ref[s])
        inv = inv_ref[s]
        for k in range(CHUNK):
            y = corr[k * PHASES : (k + 1) * PHASES] * (inv * unit[k : k + 1, :])
            move = table_ref[1, first + k] * (BLOCK // PHASES)
            turned = [
                pltpu.roll(y[:, b * BLOCK : (b + 1) * BLOCK], (BLOCK - move) % BLOCK, 1) for b in range(3)
            ]
            stay = lane < BLOCK - move
            target = table_ref[3, first + k]
            held_ref[target, :, :BLOCK] = jnp.where(stay, turned[0], turned[1])
            held_ref[target, :, BLOCK : 2 * BLOCK] = jnp.where(stay, turned[1], turned[2])
            held_ref[target, :, 2 * BLOCK :] = turned[2]

    @pl.loop(0, (table_ref[4, 0] + 1) // 2)
    def _(i):
        chunk(2 * i)
        chunk(2 * i + 1)

    end = KEPT - 2 * BLOCK

    @pl.loop(0, width)
    def _(o):
        tails, powers = [], []
        for r in range(CAP):
            y = held_ref[o * ROWS + r]
            a, b = y[:, :BLOCK], y[:, BLOCK : 2 * BLOCK]
            c = jnp.where(lane < end, y[:, 2 * BLOCK :], 0.0)
            top = jnp.maximum(jnp.maximum(jnp.abs(a), jnp.abs(b)), jnp.abs(c))
            top = jnp.maximum(jnp.max(top, axis=1, keepdims=True), 2.0**-110)
            power = jnp.ceil(FINE * jnp.log2(jnp.broadcast_to(top, (PHASES, BLOCK))))
            scale = FULL * jnp.exp2(power * (-1.0 / FINE))
            out_ref[o, 2 * r] = jnp.round(a * scale).astype(jnp.int32).astype(jnp.int16)
            out_ref[o, 2 * r + 1] = jnp.round(b * scale).astype(jnp.int32).astype(jnp.int16)
            c = jnp.round(c * scale)
            tails.append(c if r % 4 == 0 else pltpu.roll(c, end * (r % 4), 1))
            powers.append(power)
        first = jnp.where(
            lane < end, tails[0], jnp.where(lane < 2 * end, tails[1], jnp.where(lane < 3 * end, tails[2], tails[3]))
        )
        second = jnp.where(lane < end, tails[4], jnp.where(lane < 2 * end, tails[5], 0.0))
        for r in range(CAP):
            second = jnp.where(lane == 2 * end + r, powers[r], second)
        out_ref[o, 12] = first.astype(jnp.int32).astype(jnp.int16)
        out_ref[o, 13] = second.astype(jnp.int32).astype(jnp.int16)


def add_kernel(dest_ref, count_ref, back_ref, stack_ref, best_ref, scale_ref, tail_ref):
    width = back_ref.shape[0]
    end = KEPT - 2 * BLOCK

    def wide(x):
        return x.astype(jnp.int32).astype(jnp.float32)

    @pl.loop(0, width)
    def _(o):
        first, second = wide(back_ref[o, 12]), wide(back_ref[o, 13])
        scales = jnp.exp2(second * (1.0 / FINE)) * (1.0 / FULL)
        for r in range(CAP):
            scale = jnp.broadcast_to(scales[:, 2 * end + r : 2 * end + r + 1], (PHASES, BLOCK))
            tail = first if r < 4 else second
            tail = tail if r % 4 == 0 else pltpu.roll(tail, BLOCK - end * (r % 4), 1)
            scale_ref[o * ROWS + r] = scale
            tail_ref[o * ROWS + r] = tail

    def one_template(t, best):
        count = count_ref[t]

        def four_slots(g, total):
            for i in range(4):
                k = 4 * g + i
                dest = jnp.maximum(dest_ref[0, k * 8 + t], 0)
                o = dest // ROWS
                r = dest % ROWS
                scale = jnp.where(k < count, scale_ref[dest], 0.0)
                parts = (wide(back_ref[o, 2 * r]), wide(back_ref[o, 2 * r + 1]), tail_ref[dest])
                total = tuple(a + p * scale for a, p in zip(total, parts))
            return total

        zero = jnp.zeros((PHASES, BLOCK), jnp.float32)
        total = lax.fori_loop(0, (count + 3) // 4, four_slots, (zero, zero, zero))
        factor = jnp.sqrt(3.0 * L / jnp.full((1, 1), count, jnp.int32).astype(jnp.float32))
        whole = jnp.concatenate(total, axis=1) * factor
        stack_ref[t] = whole[:, :KEPT]
        return jnp.maximum(best, whole)

    start = jnp.full((PHASES, WIDE), -jnp.inf, jnp.float32)
    best = lax.fori_loop(0, stack_ref.shape[0], one_template, start)
    best_ref[...] = best[:, :KEPT]


VMEM = pl.BlockSpec(memory_space=pltpu.VMEM)
ANY = pl.BlockSpec(memory_space=pl.ANY)
SMEM = pl.BlockSpec(memory_space=pltpu.SMEM)


def params(mib):
    return pltpu.CompilerParams(vmem_limit_bytes=mib * 2**20)


def body(waveforms, station_home, templates, template_stations, station_counts, moveouts):
    stations, _, samples = waveforms.shape
    tpl_dev = templates.shape[0]
    width = lax.axis_size("sta")
    total = tpl_dev * SLOTS
    parts = station_home.shape[0] // BLOCK
    send, dest = pl.pallas_call(
        pack_kernel,
        out_shape=(
            jax.ShapeDtypeStruct((width, ROWS, DEPTH), jnp.bfloat16),
            jax.ShapeDtypeStruct((1, total), jnp.int32),
        ),
        in_specs=[ANY] * 5,
        out_specs=(VMEM, VMEM),
        scratch_shapes=[
            pltpu.VMEM((tpl_dev, SLOTS), jnp.int32),
            pltpu.VMEM((tpl_dev, SLOTS), jnp.int32),
            pltpu.SMEM((tpl_dev,), jnp.int32),
            pltpu.VMEM((parts, BLOCK), jnp.int32),
            pltpu.VMEM((SLOTS, tpl_dev, 3 * L), jnp.bfloat16),
            pltpu.SemaphoreType.DMA((5,)),
        ],
        compiler_params=params(60),
    )(
        template_stations,
        moveouts,
        station_counts,
        station_home.reshape(parts, BLOCK),
        templates.transpose(1, 0, 2),
    )
    got = lax.all_to_all(send, "sta", split_axis=0, concat_axis=0, tiled=True)
    xs, inv = pl.pallas_call(
        prep_kernel,
        grid=(stations,),
        out_shape=(
            jax.ShapeDtypeStruct((stations, DEPTH, WIDE), jnp.bfloat16),
            jax.ShapeDtypeStruct((stations, PHASES, WIDE), jnp.float32),
        ),
        in_specs=[pl.BlockSpec((3, stations, samples), lambda s: (0, 0, 0))],
        out_specs=(
            pl.BlockSpec((1, DEPTH, WIDE), lambda s: (s, 0, 0)),
            pl.BlockSpec((1, PHASES, WIDE), lambda s: (s, 0, 0)),
        ),
        scratch_shapes=[pltpu.VMEM((3, stations, samples), jnp.float32)],
        compiler_params=params(50),
        cost_estimate=pl.CostEstimate(flops=2 * 10**9, bytes_accessed=12 * 2**20, transcendentals=0),
    )(waveforms.transpose(1, 0, 2))
    room = 8 * (width * CAP // CHUNK + stations)
    traces = pl.pallas_call(
        correlate_kernel,
        out_shape=jax.ShapeDtypeStruct((width, BLOCKS, PHASES, BLOCK), jnp.int16),
        in_specs=[VMEM, ANY, VMEM],
        out_specs=VMEM,
        scratch_shapes=[
            pltpu.VMEM((stations, DEPTH, WIDE), jnp.bfloat16),
            pltpu.VMEM((room, 3 * L), jnp.float32),
            pltpu.VMEM((8, room), jnp.int32),
            pltpu.VMEM((width * ROWS + 1, PHASES, WIDE), jnp.float32),
            pltpu.SMEM((8, room), jnp.int32),
            pltpu.SemaphoreType.DMA,
            pltpu.SemaphoreType.DMA((stations,)),
        ],
        compiler_params=params(54),
    )(got, xs, inv)
    back = lax.all_to_all(traces, "sta", split_axis=0, concat_axis=0, tiled=True)
    stack, best = pl.pallas_call(
        add_kernel,
        out_shape=(
            jax.ShapeDtypeStruct((tpl_dev, PHASES, KEPT), jnp.float32),
            jax.ShapeDtypeStruct((PHASES, KEPT), jnp.float32),
        ),
        in_specs=[SMEM, SMEM, VMEM],
        out_specs=(VMEM, VMEM),
        scratch_shapes=[
            pltpu.VMEM((width * ROWS, PHASES, BLOCK), jnp.float32),
            pltpu.VMEM((width * ROWS, PHASES, BLOCK), jnp.float32),
        ],
        compiler_params=params(32),
    )(dest, station_counts, back)
    stack = stack.transpose(0, 2, 1).reshape(tpl_dev, PHASES * KEPT)
    best = best.T.reshape(PHASES * KEPT)
    network = best_of_all(best.reshape(-1, BLOCK)).reshape(PHASES * KEPT)
    return (stack, network)


def best_of_all(best):
    for axis in ("tpl", "sta"):
        size = lax.axis_size(axis)
        step = 1
        while step < size:
            other = lax.ppermute(best, axis, [(i, i ^ step) for i in range(size)])
            best = jnp.maximum(best, other)
            step *= 2
    return best


def solution(mesh):
    in_specs = (
        P("sta", None, None),
        P(),
        P(("sta", "tpl"), None, None),
        P(("sta", "tpl"), None),
        P(("sta", "tpl")),
        P(("sta", "tpl"), None),
    )
    out_specs = (P(("sta", "tpl"), None), P())
    return jax.shard_map(body, mesh=mesh, in_specs=in_specs, out_specs=out_specs, check_vma=False)
```

time: 169 us -> 120 us (0.71)
  Pallas kernels: 66.1 us -> 38.8 us
  local copies, waits for them, and re-layouts: 15.4 us -> 4.53 us
  waiting for transfers between devices: 30.3 us -> 19.8 us
  starting transfers between devices: 17.5 us -> 22.6 us
  blocking collectives: 37.1 us -> 33.1 us
    pallas_call x1, Pallas kernels: 38.4 us -> 19.1 us  [body(): pl.pallas_call(correlate_kernel, out_shape=jax.ShapeDtypeStruct((width, B...]
    pallas_call x1, Pallas kernels: 16.4 us -> 4.67 us  [body(): pl.pallas_call(add_kernel, out_shape=(jax.ShapeDtypeStruct((tpl_dev, PHAS...]
    ppermute x8, waiting for transfers between devices: 30.3 us -> 19.8 us  [best_of_all(): other = lax.ppermute(best, axis, [(i, i ^ step) for i in range(size)])]
    unnamed x12 -> x10, local copies, waits for them, and re-layouts: 11 us -> 2.6 us
    ppermute x8, starting transfers between devices: 10.2 us -> 15.2 us  [best_of_all(): other = lax.ppermute(best, axis, [(i, i ^ step) for i in range(size)])]
    all_to_all x1, blocking collectives: 37.1 us -> 33.1 us  [body(): lax.all_to_all(traces, 'sta', split_axis=0, concat_axis=0, tiled=True)]
    pallas_call x1, Pallas kernels: 9.87 us -> 12.5 us  [body(): pl.pallas_call(prep_kernel, grid=(stations,), out_shape=(jax.ShapeDtypeSt...]
  transfers between devices with their start and end apart: 9 -> 9, of which waited for: 8 -> 8; matrix products, arithmetic and copies ran while one was open for 1% -> 1% of each run, Pallas kernels for 6% -> 10%
where the time goes in v2:
time: 120 us
  Pallas kernels  38.8 us (32%)
  blocking collectives  33.1 us (28%)
  starting transfers between devices  22.6 us (19%)
  waiting for transfers between devices  19.8 us (16%)
  local copies, waits for them, and re-layouts  4.53 us (4%)
    all_to_all x1, blocking collectives, body(): lax.all_to_all(traces, 'sta', split_axis=0, concat_axis=0, tiled=True)  33.1 us
    ppermute x8, waiting for transfers between devices, best_of_all(): other = lax.ppermute(best, axis, [(i, i ^ step) for i in range(size)])  19.8 us
    pallas_call x1, Pallas kernels, body(): pl.pallas_call(correlate_kernel, out_shape=jax.ShapeDtypeStruct((width, B...  19.1 us
    ppermute x8, starting transfers between devices, best_of_all(): other = lax.ppermute(best, axis, [(i, i ^ step) for i in range(size)])  15.2 us
    pallas_call x1, Pallas kernels, body(): pl.pallas_call(prep_kernel, grid=(stations,), out_shape=(jax.ShapeDtypeSt...  12.5 us
    all_to_all x1, starting transfers between devices, body(): got = lax.all_to_all(send, 'sta', split_axis=0, concat_axis=0, tiled=True)  7.33 us
    pallas_call x1, Pallas kernels, body(): pl.pallas_call(add_kernel, out_shape=(jax.ShapeDtypeStruct((tpl_dev, PHAS...  4.67 us
    unnamed x10, local copies, waits for them, and re-layouts  2.6 us
  transfers between devices with their start and end apart: 9, of which 8 were waited for; matrix products, arithmetic and copies ran while one was open for 1% of the time, Pallas kernels for 10%

profile of v2, /device:TPU:32, one launch (start us, length us, event | category | flops | bytes accessed | tf_op | source)
XLA Modules:
  0.0 120.1 jit_solution(1561848298132920072)
XLA Ops:
  0.6 2.5 %shard_map.77 = (bf16[32,8,896]{2,1,0:T(8,128)(2,1)}, s32[1,160]{1,0:T(1,128)}) custom-call(s32[8,20]{1,0:T(8,128)} %stations_hbm.1, s32[8,20]{1,0:T(8,128)} %moves_hbm.1, s32[8]{0:T(128)} %count_ref.1, s32[4,128]{1,0:T(4,128)} %bitcast.11, bf16[20,8,768]{2,1,0:T(8,128)(2,1)} %bitcast.10), custom_call_target="tpu_custom_call" | custom-call | tf_op jit(solution)/shard_map/pallas_call | solution.py:347
  3.1 7.3 %all-to-all-start = ((bf16[32,8,896]{2,1,0:T(8,128)(2,1)}), bf16[32,8,896]{2,1,0:T(8,128)(2,1)S(1)}, u32[]{:S(2)}, u32[]{:S(2)}) async-start(bf16[32,8,896]{2,1,0:T(8,128)(2,1)} %get-tuple-element.9), calls=%async_computation | async-start | bytes 917504 | tf_op jit(solution)/shard_map/all_to_all | solution.py:371
  10.5 0.0 copy-start.3
  10.5 1.0 copy-done.3
  11.5 12.5 %shard_map.78 = (bf16[16,896,384]{2,1,0:T(8,128)(2,1)}, f32[16,16,384]{2,1,0:T(8,128)S(1)}) custom-call(bf16[3,16,5376]{2,1,0:T(8,128)(2,1)S(1)} %bitcast.9), custom_call_target="tpu_custom_call" | custom-call | flops 2000000000 | bytes 12582912 | tf_op jit(solution)/shard_map/pallas_call | solution.py:372
  24.0 0.0 copy-start
  24.0 0.7 copy-done
  24.7 0.0 all-to-all-done.got_ref
  24.7 0.0 copy-start.4
  24.7 0.8 copy-done.4
  25.5 19.1 %shard_map.79 = s16[32,14,16,128]{3,2,1,0:T(8,128)(2,1)} custom-call(bf16[32,8,896]{2,1,0:T(8,128)(2,1)} %copy-done.4, bf16[16,896,384]{2,1,0:T(8,128)(2,1)} %get-tuple-element.10.xs_hbm, f32[16,16,384]{2,1,0:T(8,128)} %copy-done), custom_call_target="tpu_custom_call" | custom-call | tf_op jit(solution)/shard_map/pallas_call | solution.py:389
  44.7 0.0 copy-start.1
  44.7 0.0 copy-start.2
  44.7 33.1 %all_to_all.10.back_ref = s16[32,14,16,128]{3,2,1,0:T(8,128)(2,1)S(1)} all-to-all(s16[32,14,16,128]{3,2,1,0:T(8,128)(2,1)} %shard_map.79), channel_id=1, replica_groups=mesh['sta'=32,'tpl'=8] {'sta'}, dimensions={0} | all-to-all | bytes 3670016 | tf_op jit(solution)/shard_map/all_to_all | solution.py:405
  77.8 0.0 copy-done.1
  77.8 0.0 copy-done.2
  77.8 4.7 %shard_map.80 = (f32[8,16,288]{2,1,0:T(8,128)S(1)}, f32[16,288]{1,0:T(8,128)S(1)}) custom-call(s32[1,160]{1,0:T(1,128)S(1)} %copy-done.2, s32[8]{0:T(128)S(1)} %copy-done.1, s16[32,14,16,128]{3,2,1,0:T(8,128)(2,1)S(1)} %all_to_all.10.back_ref), custom_call_target="tpu_custom_call" | custom-call | tf_op jit(solution)/shard_map/pallas_call | solution.py:406
  82.5 0.1 copy.9
  82.6 0.1 reshape_reshape.3
  82.7 1.1 collective-permute-start
  83.8 2.8 %collective-permute-done = f32[36,128]{1,0:T(8,128)S(1)} collective-permute-done((f32[36,128]{1,0:T(8,128)S(1)}, f32[36,128]{1,0:T(8,128)S(1)}, u32[]{:S(2)}, u32[]{:S(2)}) %collective-permute-start) | collective-permute-done | bytes 18464 | tf_op jit(solution)/shard_map/ppermute | solution.py:431
  86.6 2.7 %collective-permute-start.1 = (f32[36,128]{1,0:T(8,128)S(1)}, f32[36,128]{1,0:T(8,128)S(1)}, u32[]{:S(2)}, u32[]{:S(2)}) collective-permute-start(f32[36,128]{1,0:T(8,128)S(1)} %max.24), channel_id=1, source_target_pairs={{0,2},{1,3},{2,0},{3,1},{4,6},{5,7},{6,4},{7,5},{8,10},{9,11},{10,... | collective-permute-start | bytes 55304 | tf_op jit(solution)/shard_map/ppermute | solution.py:431
  89.3 2.0 %collective-permute-done.1 = f32[36,128]{1,0:T(8,128)S(1)} collective-permute-done((f32[36,128]{1,0:T(8,128)S(1)}, f32[36,128]{1,0:T(8,128)S(1)}, u32[]{:S(2)}, u32[]{:S(2)}) %collective-permute-start.1) | collective-permute-done | bytes 18464 | tf_op jit(solution)/shard_map/ppermute | solution.py:431
  91.3 7.1 %collective-permute-start.2 = (f32[36,128]{1,0:T(8,128)S(1)}, f32[36,128]{1,0:T(8,128)S(1)}, u32[]{:S(2)}, u32[]{:S(2)}) collective-permute-start(f32[36,128]{1,0:T(8,128)S(1)} %max.25), channel_id=1, source_target_pairs={{0,4},{1,5},{2,6},{3,7},{4,0},{5,1},{6,2},{7,3},{8,12},{9,13},{10,... | collective-permute-start | bytes 55304 | tf_op jit(solution)/shard_map/ppermute | solution.py:431
  98.4 1.8 %collective-permute-done.2 = f32[36,128]{1,0:T(8,128)S(1)} collective-permute-done((f32[36,128]{1,0:T(8,128)S(1)}, f32[36,128]{1,0:T(8,128)S(1)}, u32[]{:S(2)}, u32[]{:S(2)}) %collective-permute-start.2) | collective-permute-done | bytes 18464 | tf_op jit(solution)/shard_map/ppermute | solution.py:431
  100.2 0.0 collective-permute-start.3
  100.2 1.2 collective-permute-done.3
  101.4 0.9 collective-permute-start.4
  102.3 2.9 %collective-permute-done.4 = f32[36,128]{1,0:T(8,128)S(1)} collective-permute-done((f32[36,128]{1,0:T(8,128)S(1)}, f32[36,128]{1,0:T(8,128)S(1)}, u32[]{:S(2)}, u32[]{:S(2)}) %collective-permute-start.4) | collective-permute-done | bytes 18464 | tf_op jit(solution)/shard_map/ppermute | solution.py:431
  105.1 1.9 %collective-permute-start.5 = (f32[36,128]{1,0:T(8,128)S(1)}, f32[36,128]{1,0:T(8,128)S(1)}, u32[]{:S(2)}, u32[]{:S(2)}) collective-permute-start(f32[36,128]{1,0:T(8,128)S(1)} %max.28), channel_id=1, source_target_pairs={{0,32},{8,40},{16,48},{24,56},{32,0},{40,8},{48,16},{56,24},{64,96... | collective-permute-start | bytes 55304 | tf_op jit(solution)/shard_map/ppermute | solution.py:431
  107.0 3.4 %collective-permute-done.5 = f32[36,128]{1,0:T(8,128)S(1)} collective-permute-done((f32[36,128]{1,0:T(8,128)S(1)}, f32[36,128]{1,0:T(8,128)S(1)}, u32[]{:S(2)}, u32[]{:S(2)}) %collective-permute-start.5) | collective-permute-done | bytes 18464 | tf_op jit(solution)/shard_map/ppermute | solution.py:431
  110.4 0.0 collective-permute-start.6
  110.4 3.8 %collective-permute-done.6 = f32[36,128]{1,0:T(8,128)S(1)} collective-permute-done((f32[36,128]{1,0:T(8,128)S(1)}, f32[36,128]{1,0:T(8,128)S(1)}, u32[]{:S(2)}, u32[]{:S(2)}) %collective-permute-start.6) | collective-permute-done | bytes 18464 | tf_op jit(solution)/shard_map/ppermute | solution.py:431
  114.2 1.6 %collective-permute-start.7 = (f32[36,128]{1,0:T(8,128)S(1)}, f32[36,128]{1,0:T(8,128)S(1)}, u32[]{:S(2)}, u32[]{:S(2)}) collective-permute-start(f32[36,128]{1,0:T(8,128)S(1)} %max.30), channel_id=1, source_target_pairs={{0,128},{8,136},{16,144},{24,152},{32,160},{40,168},{48,176},{56,1... | collective-permute-start | bytes 55304 | tf_op jit(solution)/shard_map/ppermute | solution.py:431
  115.8 0.4 copy.8
  116.2 1.4 %reshape.14 = f32[8,4608]{1,0:T(8,128)} reshape(f32[8,288,16]{2,1,0:T(8,128)S(1)} %copy.8) | data formatting | bytes 294912 | tf_op jit(solution)/shard_map/reshape | solution.py:420
  117.5 2.0 %collective-permute-done.7 = f32[36,128]{1,0:T(8,128)S(1)} collective-permute-done((f32[36,128]{1,0:T(8,128)S(1)}, f32[36,128]{1,0:T(8,128)S(1)}, u32[]{:S(2)}, u32[]{:S(2)}) %collective-permute-start.7) | collective-permute-done | bytes 18464 | tf_op jit(solution)/shard_map/ppermute | solution.py:431
  119.5 0.6 maximum_bitcast_fusion
  (7 shorter events, 0.0 us)
Async XLA Ops:
  3.1 21.6 %all-to-all-start = ((bf16[32,8,896]{2,1,0:T(8,128)(2,1)}), bf16[32,8,896]{2,1,0:T(8,128)(2,1)S(1)}, u32[]{:S(2)}, u32[]{:S(2)}) async-start(bf16[32,8,896]{2,1,0:T(8,128)(2,1)} %get-tuple-element.9), calls=%async_computation | async-start | bytes 917504 | tf_op jit(solution)/shard_map/all_to_all | solution.py:371
  10.5 1.0 copy-start.3
  24.0 0.7 copy-start
  24.7 0.8 copy-start.4
  44.7 33.1 %copy-start.1 = (s32[8]{0:T(128)S(1)}, s32[8]{0:T(128)}, u32[]{:S(2)}) copy-start(s32[8]{0:T(128)} %count_ref.1) | copy-start | bytes 100
  44.7 33.1 %copy-start.2 = (s32[1,160]{1,0:T(1,128)S(1)}, s32[1,160]{1,0:T(1,128)}, u32[]{:S(2)}) copy-start(s32[1,160]{1,0:T(1,128)} %get-tuple-element.8.dest_ref) | copy-start | bytes 1924
  82.7 3.9 %collective-permute-start = (f32[36,128]{1,0:T(8,128)S(1)}, f32[36,128]{1,0:T(8,128)S(1)}, u32[]{:S(2)}, u32[]{:S(2)}) collective-permute-start(f32[36,128]{1,0:T(8,128)S(1)} %reshape_reshape.3), channel_id=1, source_target_pairs={{0,1},{1,0},{2,3},{3,2},{4,5},{5,4},{6,7},{7,6},{8,9},{9,8},{10,11... | collective-permute-start | bytes 55304 | tf_op jit(solution)/shard_map/ppermute | solution.py:431
  86.6 4.7 %collective-permute-start.1 = (f32[36,128]{1,0:T(8,128)S(1)}, f32[36,128]{1,0:T(8,128)S(1)}, u32[]{:S(2)}, u32[]{:S(2)}) collective-permute-start(f32[36,128]{1,0:T(8,128)S(1)} %max.24), channel_id=1, source_target_pairs={{0,2},{1,3},{2,0},{3,1},{4,6},{5,7},{6,4},{7,5},{8,10},{9,11},{10,... | collective-permute-start | bytes 55304 | tf_op jit(solution)/shard_map/ppermute | solution.py:431
  91.3 8.8 %collective-permute-start.2 = (f32[36,128]{1,0:T(8,128)S(1)}, f32[36,128]{1,0:T(8,128)S(1)}, u32[]{:S(2)}, u32[]{:S(2)}) collective-permute-start(f32[36,128]{1,0:T(8,128)S(1)} %max.25), channel_id=1, source_target_pairs={{0,4},{1,5},{2,6},{3,7},{4,0},{5,1},{6,2},{7,3},{8,12},{9,13},{10,... | collective-permute-start | bytes 55304 | tf_op jit(solution)/shard_map/ppermute | solution.py:431
  100.2 1.2 collective-permute-start.3
  101.4 3.8 %collective-permute-start.4 = (f32[36,128]{1,0:T(8,128)S(1)}, f32[36,128]{1,0:T(8,128)S(1)}, u32[]{:S(2)}, u32[]{:S(2)}) collective-permute-start(f32[36,128]{1,0:T(8,128)S(1)} %max.27), channel_id=1, source_target_pairs={{0,16},{8,24},{16,0},{24,8},{32,48},{40,56},{48,32},{56,40},{64,80... | collective-permute-start | bytes 55304 | tf_op jit(solution)/shard_map/ppermute | solution.py:431
  105.1 5.3 %collective-permute-start.5 = (f32[36,128]{1,0:T(8,128)S(1)}, f32[36,128]{1,0:T(8,128)S(1)}, u32[]{:S(2)}, u32[]{:S(2)}) collective-permute-start(f32[36,128]{1,0:T(8,128)S(1)} %max.28), channel_id=1, source_target_pairs={{0,32},{8,40},{16,48},{24,56},{32,0},{40,8},{48,16},{56,24},{64,96... | collective-permute-start | bytes 55304 | tf_op jit(solution)/shard_map/ppermute | solution.py:431
  110.4 3.8 %collective-permute-start.6 = (f32[36,128]{1,0:T(8,128)S(1)}, f32[36,128]{1,0:T(8,128)S(1)}, u32[]{:S(2)}, u32[]{:S(2)}) collective-permute-start(f32[36,128]{1,0:T(8,128)S(1)} %max.29), channel_id=1, source_target_pairs={{0,64},{8,72},{16,80},{24,88},{32,96},{40,104},{48,112},{56,120},{... | collective-permute-start | bytes 55304 | tf_op jit(solution)/shard_map/ppermute | solution.py:431
  114.2 5.3 %collective-permute-start.7 = (f32[36,128]{1,0:T(8,128)S(1)}, f32[36,128]{1,0:T(8,128)S(1)}, u32[]{:S(2)}, u32[]{:S(2)}) collective-permute-start(f32[36,128]{1,0:T(8,128)S(1)} %max.30), channel_id=1, source_target_pairs={{0,128},{8,136},{16,144},{24,152},{32,160},{40,168},{48,176},{56,1... | collective-permute-start | bytes 55304 | tf_op jit(solution)/shard_map/ppermute | solution.py:431

commit v3 on v2

--- a/solution.py
+++ b/solution.py
@@ -23,7 +23,8 @@
 CHUNK = 8
 CAP = 6
 ROWS = 8
-BLOCKS = 14
+HALF = 3
+BLOCKS = 7
 
 FINE = 8.0
 FULL = 32700.0
@@ -41,7 +42,7 @@
 
 
 def pack_kernel(
-    stations_hbm, moves_hbm, counts_hbm, home_hbm, templates_hbm, send_ref, dest_ref,
+    stations_hbm, moves_hbm, counts_hbm, home_hbm, templates_hbm, send_ref, list_ref,
     stations_ref, moves_ref, counts_ref, home_ref, templates_ref, sems,
 ):
     copies = [
@@ -91,17 +92,35 @@
     owner = jnp.sum(jnp.where(part, found[:parts], 0.0), axis=0, keepdims=True).astype(jnp.int32)
     local = jnp.sum(jnp.where(part, found[parts:], 0.0), axis=0, keepdims=True)
     live = place // tpl_dev < counts
+    before = (iota((total, total), 0) < iota((total, total), 1)).astype(jnp.bfloat16)
+    pairs = width * tpl_dev
+    of_pair = jnp.where((iota((pairs, total), 0) == owner * tpl_dev + of_template) & live, 1.0, 0.0)
+    earlier = jnp.sum(of_pair * dot(of_pair.astype(jnp.bfloat16), before), axis=0, keepdims=True)
+    first = live & (earlier < 0.5)
+    present = jnp.minimum(jnp.sum(of_pair, axis=1, keepdims=True), 1.0)
+    row, col = iota((pairs, pairs), 0), iota((pairs, pairs), 1)
+    lower = ((row // tpl_dev == col // tpl_dev) & (col < row)).astype(jnp.bfloat16)
+    order = dot(lower, jnp.broadcast_to(present, (pairs, BLOCK)).astype(jnp.bfloat16))[:, 0:1]
+    turn = jnp.sum(of_pair * order, axis=0, keepdims=True)
+    over = jnp.max(jnp.where(live & (turn > HALF - 0.5), 1.0, 0.0))
+    late = turn > HALF - 0.5
+    home_of = (jnp.where(late, width, 0) + owner) * 4 + jnp.where(late, turn - HALF, turn).astype(jnp.int32)
+    own_first = jnp.where((iota((tpl_dev, total), 0) == of_template) & first, 1.0, 0.0)
+    nth = dot(own_first.astype(jnp.bfloat16), before)
+    nth = jnp.sum(own_first * nth, axis=0, keepdims=True).astype(jnp.int32)
+    entry = (iota((BLOCK, total), 0) == nth).astype(jnp.bfloat16)
+    listed = dot((own_first * home_of.astype(jnp.float32)).astype(jnp.bfloat16), entry, NT)
+    number = jnp.sum(own_first, axis=1, keepdims=True)
+    list_ref[...] = jnp.where(iota((tpl_dev, BLOCK), 1) == BLOCK - 1, number, listed).astype(jnp.int32)
     at_owner = jnp.where((iota((width, total), 0) == owner) & live, 1.0, 0.0)
-    before = (iota((total, total), 0) < iota((total, total), 1)).astype(jnp.bfloat16)
     rank = jnp.sum(at_owner * dot(at_owner.astype(jnp.bfloat16), before), axis=0, keepdims=True)
     dest = jnp.where(live, owner * ROWS + rank.astype(jnp.int32), -1)
-    dest_ref[...] = dest
     pick = (iota((width * ROWS, total), 0) == dest).astype(jnp.bfloat16)
     kind = iota((BLOCK, total), 0)
-    fields = jnp.where(
-        kind == 0, local, jnp.where(kind == 1, moves, jnp.where(kind == 2, 1.0, 0.0))
-    ).astype(jnp.bfloat16)
-    tail = dot(pick, fields, NT).astype(jnp.bfloat16)
+    fields = jnp.where(kind == 0, local, jnp.where(kind == 1, moves, jnp.where(kind == 2, 1.0, 0.0)))
+    fields = jnp.where(kind == 3, turn, fields).astype(jnp.bfloat16)
+    tail = dot(pick, fields, NT)
+    tail = jnp.where(iota(tail.shape, 1) == 4, over, tail).astype(jnp.bfloat16)
     copies[4].wait()
     send = dot(pick, templates_ref[...].reshape(total, 3 * L)).astype(jnp.bfloat16)
     send_ref[:, :, : 3 * L] = send.reshape(width, ROWS, 3 * L)
@@ -168,7 +187,7 @@
 
 
 def correlate_kernel(
-    got_ref, xs_hbm, inv_ref, out_ref, xs_ref, sorted_ref, order_ref, held_ref, table_ref, sem, xs_sems
+    got_ref, xs_hbm, inv_ref, out_ref, more_ref, flag_ref, xs_ref, sorted_ref, order_ref, held_ref, table_ref, sem, xs_sems
 ):
     width = got_ref.shape[0]
     stations = xs_ref.shape[0]
@@ -194,20 +213,33 @@
     place = jnp.where(live, place, -1)
     pick = (iota((room, total), 0) == place).astype(jnp.bfloat16)
     kind = iota((8, total), 0)
-    rows = jnp.where(
-        kind == 3, iota((8, total), 1).astype(jnp.float32), jnp.where(kind < 3, fields, 0.0)
-    ).astype(jnp.bfloat16)
+    late = fields[3:4, :] > HALF - 0.5
+    source = iota((1, total), 1) // ROWS
+    turn = jnp.where(late, fields[3:4, :] - HALF, fields[3:4, :]).astype(jnp.int32)
+    target = ((jnp.where(late, width, 0) + source) * 4 + turn).astype(jnp.float32)
+    rows = jnp.where(kind == 3, target, jnp.where(kind < 3, fields, 0.0)).astype(jnp.bfloat16)
     table = dot(rows, pick, NT)
+    over = jnp.max(fields[4:5, :])
     kind = iota((8, room), 0)
-    table = jnp.where((kind == 3) & (table[2:3, :] < 0.5), float(total), table)
-    table = jnp.where(kind == 4, jnp.sum(chunks), table)
+    table = jnp.where((kind == 3) & (table[2:3, :] < 0.5), float(held_ref.shape[0] - 1), table)
+    table = jnp.where(kind == 4, jnp.sum(chunks), jnp.where(kind == 5, over, table))
     order_ref[...] = table.astype(jnp.int32)
     copy = pltpu.make_async_copy(order_ref, table_ref, sem)
     copy.start()
+    flag_ref[...] = jnp.full(flag_ref.shape, over, jnp.float32).astype(jnp.int32)
     sorted_ref[...] = dot(pick, pieces)
+    blank = jnp.zeros((PHASES, WIDE), jnp.float32)
+
+    @pl.loop(0, held_ref.shape[0] // 8)
+    def _(i):
+        for r in range(8):
+            held_ref[8 * i + r] = blank
+
     copy.wait()
-    for load in loads:
-        load.wait()
+
+    def arrive(s, carry):
+        pltpu.make_async_copy(xs_hbm.at[s], xs_ref.at[s], xs_sems.at[s]).wait()
+        return carry
 
     sub = iota((PHASES, BLOCK), 0)
     lane = iota((PHASES, BLOCK), 1)
@@ -248,77 +280,82 @@
             ]
             stay = lane < BLOCK - move
             target = table_ref[3, first + k]
-            held_ref[target, :, :BLOCK] = jnp.where(stay, turned[0], turned[1])
-            held_ref[target, :, BLOCK : 2 * BLOCK] = jnp.where(stay, turned[1], turned[2])
-            held_ref[target, :, 2 * BLOCK :] = turned[2]
-
-    @pl.loop(0, (table_ref[4, 0] + 1) // 2)
-    def _(i):
+            held_ref[target, :, :BLOCK] += jnp.where(stay, turned[0], turned[1])
+            held_ref[target, :, BLOCK : 2 * BLOCK] += jnp.where(stay, turned[1], turned[2])
+            held_ref[target, :, 2 * BLOCK :] += turned[2]
+
+    def two_chunks(i, ready):
+        last = jnp.maximum(table_ref[0, 16 * i], table_ref[0, 16 * i + 8]) + 1
+        lax.fori_loop(ready, last, arrive, 0)
         chunk(2 * i)
         chunk(2 * i + 1)
-
+        return jnp.maximum(ready, last)
+
+    ready = lax.fori_loop(0, (table_ref[4, 0] + 1) // 2, two_chunks, 0)
+    lax.fori_loop(ready, stations, arrive, 0)
     end = KEPT - 2 * BLOCK
 
-    @pl.loop(0, width)
-    def _(o):
-        tails, powers = [], []
-        for r in range(CAP):
-            y = held_ref[o * ROWS + r]
+    def finish(ref, o, at):
+        last = jnp.zeros((PHASES, BLOCK), jnp.float32)
+        for r in range(HALF):
+            y = held_ref[at * 4 + r]
             a, b = y[:, :BLOCK], y[:, BLOCK : 2 * BLOCK]
             c = jnp.where(lane < end, y[:, 2 * BLOCK :], 0.0)
             top = jnp.maximum(jnp.maximum(jnp.abs(a), jnp.abs(b)), jnp.abs(c))
             top = jnp.maximum(jnp.max(top, axis=1, keepdims=True), 2.0**-110)
             power = jnp.ceil(FINE * jnp.log2(jnp.broadcast_to(top, (PHASES, BLOCK))))
             scale = FULL * jnp.exp2(power * (-1.0 / FINE))
-            out_ref[o, 2 * r] = jnp.round(a * scale).astype(jnp.int32).astype(jnp.int16)
-            out_ref[o, 2 * r + 1] = jnp.round(b * scale).astype(jnp.int32).astype(jnp.int16)
+            ref[o, 2 * r] = jnp.round(a * scale).astype(jnp.int32).astype(jnp.int16)
+            ref[o, 2 * r + 1] = jnp.round(b * scale).astype(jnp.int32).astype(jnp.int16)
             c = jnp.round(c * scale)
-            tails.append(c if r % 4 == 0 else pltpu.roll(c, end * (r % 4), 1))
-            powers.append(power)
-        first = jnp.where(
-            lane < end, tails[0], jnp.where(lane < 2 * end, tails[1], jnp.where(lane < 3 * end, tails[2], tails[3]))
-        )
-        second = jnp.where(lane < end, tails[4], jnp.where(lane < 2 * end, tails[5], 0.0))
-        for r in range(CAP):
-            second = jnp.where(lane == 2 * end + r, powers[r], second)
-        out_ref[o, 12] = first.astype(jnp.int32).astype(jnp.int16)
-        out_ref[o, 13] = second.astype(jnp.int32).astype(jnp.int16)
-
-
-def add_kernel(dest_ref, count_ref, back_ref, stack_ref, best_ref, scale_ref, tail_ref):
-    width = back_ref.shape[0]
+            last = last + (c if r == 0 else pltpu.roll(c, end * r, 1))
+            last = jnp.where(lane == HALF * end + r, power, last)
+        ref[o, 2 * HALF] = last.astype(jnp.int32).astype(jnp.int16)
+
+    @pl.loop(0, width // 2)
+    def _(i):
+        finish(out_ref, 2 * i, 2 * i)
+        finish(out_ref, 2 * i + 1, 2 * i + 1)
+
+    @pl.when(table_ref[5, 0] > 0)
+    def _():
+        @pl.loop(0, width)
+        def _(o):
+            finish(more_ref, o, width + o)
+
+
+def add_kernel(list_ref, count_ref, back_ref, stack_ref, best_ref, scale_ref, tail_ref):
     end = KEPT - 2 * BLOCK
 
     def wide(x):
         return x.astype(jnp.int32).astype(jnp.float32)
 
-    @pl.loop(0, width)
-    def _(o):
-        first, second = wide(back_ref[o, 12]), wide(back_ref[o, 13])
-        scales = jnp.exp2(second * (1.0 / FINE)) * (1.0 / FULL)
-        for r in range(CAP):
-            scale = jnp.broadcast_to(scales[:, 2 * end + r : 2 * end + r + 1], (PHASES, BLOCK))
-            tail = first if r < 4 else second
-            tail = tail if r % 4 == 0 else pltpu.roll(tail, BLOCK - end * (r % 4), 1)
-            scale_ref[o * ROWS + r] = scale
-            tail_ref[o * ROWS + r] = tail
+    @pl.loop(0, back_ref.shape[0] // 2)
+    def _(i):
+        for o in (2 * i, 2 * i + 1):
+            last = wide(back_ref[o, 2 * HALF])
+            scales = jnp.exp2(last * (1.0 / FINE)) * (1.0 / FULL)
+            for r in range(HALF):
+                at = HALF * end + r
+                scale_ref[o * 4 + r] = jnp.broadcast_to(scales[:, at : at + 1], (PHASES, BLOCK))
+                tail_ref[o * 4 + r] = last if r == 0 else pltpu.roll(last, BLOCK - end * r, 1)
 
     def one_template(t, best):
         count = count_ref[t]
-
-        def four_slots(g, total):
+        number = list_ref[t, BLOCK - 1]
+
+        def four_traces(g, total):
             for i in range(4):
-                k = 4 * g + i
-                dest = jnp.maximum(dest_ref[0, k * 8 + t], 0)
-                o = dest // ROWS
-                r = dest % ROWS
-                scale = jnp.where(k < count, scale_ref[dest], 0.0)
-                parts = (wide(back_ref[o, 2 * r]), wide(back_ref[o, 2 * r + 1]), tail_ref[dest])
+                entry = list_ref[t, 4 * g + i]
+                o = entry // 4
+                r = entry % 4
+                scale = jnp.where(4 * g + i < number, scale_ref[entry], 0.0)
+                parts = (wide(back_ref[o, 2 * r]), wide(back_ref[o, 2 * r + 1]), tail_ref[entry])
                 total = tuple(a + p * scale for a, p in zip(total, parts))
             return total
 
         zero = jnp.zeros((PHASES, BLOCK), jnp.float32)
-        total = lax.fori_loop(0, (count + 3) // 4, four_slots, (zero, zero, zero))
+        total = lax.fori_loop(0, (number + 3) // 4, four_traces, (zero, zero, zero))
         factor = jnp.sqrt(3.0 * L / jnp.full((1, 1), count, jnp.int32).astype(jnp.float32))
         whole = jnp.concatenate(total, axis=1) * factor
         stack_ref[t] = whole[:, :KEPT]
@@ -338,17 +375,60 @@
     return pltpu.CompilerParams(vmem_limit_bytes=mib * 2**20)
 
 
+def correlate_call(got, xs, inv):
+    width = got.shape[0]
+    stations = xs.shape[0]
+    room = 8 * (width * CAP // CHUNK + stations)
+    return pl.pallas_call(
+        correlate_kernel,
+        out_shape=(
+            jax.ShapeDtypeStruct((width, BLOCKS, PHASES, BLOCK), jnp.int16),
+            jax.ShapeDtypeStruct((width, BLOCKS, PHASES, BLOCK), jnp.int16),
+            jax.ShapeDtypeStruct((1, BLOCK), jnp.int32),
+        ),
+        in_specs=[VMEM, ANY, VMEM],
+        out_specs=(VMEM, VMEM, VMEM),
+        scratch_shapes=[
+            pltpu.VMEM((stations, DEPTH, WIDE), jnp.bfloat16),
+            pltpu.VMEM((room, 3 * L), jnp.float32),
+            pltpu.VMEM((8, room), jnp.int32),
+            pltpu.VMEM((8 * width + 8, PHASES, WIDE), jnp.float32),
+            pltpu.SMEM((8, room), jnp.int32),
+            pltpu.SemaphoreType.DMA,
+            pltpu.SemaphoreType.DMA((stations,)),
+        ],
+        compiler_params=params(54),
+    )(got, xs, inv)
+
+
+def add_call(listed, counts, back):
+    tpl_dev = counts.shape[0]
+    return pl.pallas_call(
+        add_kernel,
+        out_shape=(
+            jax.ShapeDtypeStruct((tpl_dev, PHASES, KEPT), jnp.float32),
+            jax.ShapeDtypeStruct((PHASES, KEPT), jnp.float32),
+        ),
+        in_specs=[SMEM, SMEM, VMEM],
+        out_specs=(VMEM, VMEM),
+        scratch_shapes=[
+            pltpu.VMEM((back.shape[0] * 4, PHASES, BLOCK), jnp.float32),
+            pltpu.VMEM((back.shape[0] * 4, PHASES, BLOCK), jnp.float32),
+        ],
+        compiler_params=params(32),
+    )(listed, counts, back)
+
+
 def body(waveforms, station_home, templates, template_stations, station_counts, moveouts):
     stations, _, samples = waveforms.shape
     tpl_dev = templates.shape[0]
     width = lax.axis_size("sta")
-    total = tpl_dev * SLOTS
     parts = station_home.shape[0] // BLOCK
-    send, dest = pl.pallas_call(
+    send, listed = pl.pallas_call(
         pack_kernel,
         out_shape=(
             jax.ShapeDtypeStruct((width, ROWS, DEPTH), jnp.bfloat16),
-            jax.ShapeDtypeStruct((1, total), jnp.int32),
+            jax.ShapeDtypeStruct((tpl_dev, BLOCK), jnp.int32),
         ),
         in_specs=[ANY] * 5,
         out_specs=(VMEM, VMEM),
@@ -385,38 +465,18 @@
         compiler_params=params(50),
         cost_estimate=pl.CostEstimate(flops=2 * 10**9, bytes_accessed=12 * 2**20, transcendentals=0),
     )(waveforms.transpose(1, 0, 2))
-    room = 8 * (width * CAP // CHUNK + stations)
-    traces = pl.pallas_call(
-        correlate_kernel,
-        out_shape=jax.ShapeDtypeStruct((width, BLOCKS, PHASES, BLOCK), jnp.int16),
-        in_specs=[VMEM, ANY, VMEM],
-        out_specs=VMEM,
-        scratch_shapes=[
-            pltpu.VMEM((stations, DEPTH, WIDE), jnp.bfloat16),
-            pltpu.VMEM((room, 3 * L), jnp.float32),
-            pltpu.VMEM((8, room), jnp.int32),
-            pltpu.VMEM((width * ROWS + 1, PHASES, WIDE), jnp.float32),
-            pltpu.SMEM((8, room), jnp.int32),
-            pltpu.SemaphoreType.DMA,
-            pltpu.SemaphoreType.DMA((stations,)),
-        ],
-        compiler_params=params(54),
-    )(got, xs, inv)
-    back = lax.all_to_all(traces, "sta", split_axis=0, concat_axis=0, tiled=True)
-    stack, best = pl.pallas_call(
-        add_kernel,
-        out_shape=(
-            jax.ShapeDtypeStruct((tpl_dev, PHASES, KEPT), jnp.float32),
-            jax.ShapeDtypeStruct((PHASES, KEPT), jnp.float32),
-        ),
-        in_specs=[SMEM, SMEM, VMEM],
-        out_specs=(VMEM, VMEM),
-        scratch_shapes=[
-            pltpu.VMEM((width * ROWS, PHASES, BLOCK), jnp.float32),
-            pltpu.VMEM((width * ROWS, PHASES, BLOCK), jnp.float32),
-        ],
-        compiler_params=params(32),
-    )(dest, station_counts, back)
+    traces, more, flag = correlate_call(got, xs, inv)
+
+    def home(x):
+        return lax.all_to_all(x, "sta", split_axis=0, concat_axis=0, tiled=True)
+
+    def one_exchange(traces, more):
+        return add_call(listed, station_counts, home(traces))
+
+    def two_exchanges(traces, more):
+        return add_call(listed, station_counts, jnp.concatenate([home(traces), home(more)]))
+
+    stack, best = lax.cond(flag[0, 0] > 0, two_exchanges, one_exchange, traces, more)
     stack = stack.transpose(0, 2, 1).reshape(tpl_dev, PHASES * KEPT)
     best = best.T.reshape(PHASES * KEPT)
     network = best_of_all(best.reshape(-1, BLOCK)).reshape(PHASES * KEPT)

time: 120 us -> 103 us (0.86)
  blocking collectives: 33.1 us -> 23.2 us
  Pallas kernels: 38.8 us -> 31.1 us
  starting transfers between devices: 22.6 us -> 20.7 us
    all_to_all x1, blocking collectives: 33.1 us -> 23.2 us  [home(): return lax.all_to_all(x, 'sta', split_axis=0, concat_axis=0, tiled=True)]
    pallas_call x2, Pallas kernels: 23.8 us -> 15.8 us  [the longest x1 12.7 us: correlate_call(): pl.pallas_call(correlate_kernel, out_shape=(jax.ShapeDtypeStruct((width,...]
    ppermute x8, starting transfers between devices: 15.2 us -> 13.4 us  [best_of_all(): other = lax.ppermute(best, axis, [(i, i ^ step) for i in range(size)])]
    unnamed x10 -> x8, local copies, waits for them, and re-layouts: 2.6 us -> 2.56 us
  transfers between devices with their start and end apart: 9 -> 9, of which waited for: 8 -> 8; matrix products, arithmetic and copies ran while one was open for 1% -> 2% of each run, Pallas kernels for 10% -> 12%
where the time goes in v3:
time: 103 us; the launch traced here: 102 us
  Pallas kernels  31.1 us (30%)
  blocking collectives  23.2 us (23%)
  waiting for transfers between devices  20.8 us (20%)
  starting transfers between devices  20.7 us (20%)
  local copies, waits for them, and re-layouts  4.49 us (4%)
  between operations  1.38 us (1%)
    all_to_all x1, blocking collectives, home(): return lax.all_to_all(x, 'sta', split_axis=0, concat_axis=0, tiled=True)  23.2 us
    ppermute x8, waiting for transfers between devices, best_of_all(): other = lax.ppermute(best, axis, [(i, i ^ step) for i in range(size)])  20.8 us
    ppermute x8, starting transfers between devices, best_of_all(): other = lax.ppermute(best, axis, [(i, i ^ step) for i in range(size)])  13.4 us
    pallas_call x1, Pallas kernels, correlate_call(): pl.pallas_call(correlate_kernel, out_shape=(jax.ShapeDtypeStruct((width,...  12.7 us
    pallas_call x1, Pallas kernels, body(): pl.pallas_call(prep_kernel, grid=(stations,), out_shape=(jax.ShapeDtypeSt...  12.6 us
    all_to_all x1, starting transfers between devices, body(): got = lax.all_to_all(send, 'sta', split_axis=0, concat_axis=0, tiled=True)  7.33 us
    pallas_call x1, Pallas kernels, add_call(): pl.pallas_call(add_kernel, out_shape=(jax.ShapeDtypeStruct((tpl_dev, PHAS...  3.14 us
    pallas_call x1, Pallas kernels, body(): pl.pallas_call(pack_kernel, out_shape=(jax.ShapeDtypeStruct((width, ROWS,...  2.75 us
  transfers between devices with their start and end apart: 9, of which 8 were waited for; matrix products, arithmetic and copies ran while one was open for 2% of the time, Pallas kernels for 12%

profile of v3, /device:TPU:32, one launch (start us, length us, event | category | flops | bytes accessed | tf_op | source)
XLA Modules:
  0.0 102.3 jit_solution(9965296868892568954)
XLA Ops:
  0.6 2.7 %shard_map.77 = (bf16[32,8,896]{2,1,0:T(8,128)(2,1)}, s32[8,128]{1,0:T(8,128)S(1)}) custom-call(s32[8,20]{1,0:T(8,128)} %stations_hbm.1, s32[8,20]{1,0:T(8,128)} %moves_hbm.1, s32[8]{0:T(128)} %counts_hbm.1, s32[4,128]{1,0:T(4,128)} %bitcast.13, bf16[20,8,768]{2,1,0:T(8,128)(2,1)} %bitcast.10), custom_call_target="tpu_custom_call" | custom-call | tf_op jit(solution)/shard_map/pallas_call | solution.py:427
  3.4 7.3 %all-to-all-start.3 = ((bf16[32,8,896]{2,1,0:T(8,128)(2,1)}), bf16[32,8,896]{2,1,0:T(8,128)(2,1)S(1)}, u32[]{:S(2)}, u32[]{:S(2)}) async-start(bf16[32,8,896]{2,1,0:T(8,128)(2,1)} %get-tuple-element.32), calls=%async_computation.3 | async-start | bytes 917504 | tf_op jit(solution)/shard_map/all_to_all | solution.py:451
  10.7 0.0 copy-start.1
  10.7 1.0 %copy-done.1 = bf16[16,3,5376]{2,0,1:T(8,128)(2,1)S(1)} copy-done((bf16[16,3,5376]{2,0,1:T(8,128)(2,1)S(1)}, bf16[16,3,5376]{2,0,1:T(8,128)(2,1)}, u32[]{:S(2)}) %copy-start.1) | copy-done | bytes 516120
  11.8 12.6 %shard_map.78 = (bf16[16,896,384]{2,1,0:T(8,128)(2,1)}, f32[16,16,384]{2,1,0:T(8,128)S(1)}) custom-call(bf16[3,16,5376]{2,1,0:T(8,128)(2,1)S(1)} %bitcast.9), custom_call_target="tpu_custom_call" | custom-call | flops 2000000000 | bytes 12582912 | tf_op jit(solution)/shard_map/pallas_call | solution.py:452
  24.3 0.0 copy-start
  24.3 0.8 copy-done
  25.1 0.0 all-to-all-done.3.got_ref
  25.1 0.0 copy-start.2
  25.1 0.8 copy-done.2
  25.8 0.0 copy-start.3
  25.8 12.7 %shard_map.79 = (s16[32,7,16,128]{3,2,1,0:T(8,128)(2,1)S(1)}, s16[32,7,16,128]{3,2,1,0:T(8,128)(2,1)S(1)}, s32[1,128]{1,0:T(1,128)}) custom-call(bf16[32,8,896]{2,1,0:T(8,128)(2,1)} %copy-done.2, bf16[16,896,384]{2,1,0:T(8,128)(2,1)} %get-tuple-element.33.xs_hbm, f32[16,16,384]{2,1,0:T(8,128)} %copy-done), custom_call_target="tpu_custom_call" | custom-call | tf_op jit(solution)/shard_map/pallas_call | solution.py:382
  39.2 0.0 copy-done.3
  39.2 26.3 %conditional.1 = ((f32[8,16,288]{2,1,0:T(8,128)S(1)}, f32[16,288]{1,0:T(8,128)S(1)})) conditional(s32[]{:T(128)} %bitcast.3, (s16[32,7,16,128]{3,2,1,0:T(8,128)(2,1)S(1)}, s32[8,128]{1,0:T(8,128)S(1)}, s32[8]{0:T(128)S(1)}) %tuple.21, (s16[32,7,16,128]{3,2,1,0:T(8,128)(2,1)S(1)}, s16[32,7,16,128]{3,2,1,0:T(8,128)(2,1)S(1)}, s32[8,128]{1,0:T(8,128)S(1)}, ...), branch_computations={%region_0.0_spmd, %region_1.0_spmd} | conditional | flops 917504 | bytes 7340040 | solution.py:479
  39.2 23.2 %all_to_all.17.back_ref = s16[32,7,16,128]{3,2,1,0:T(8,128)(2,1)S(1)} all-to-all(s16[32,7,16,128]{3,2,1,0:T(8,128)(2,1)S(1)} %get-tuple-element.16), channel_id=1, replica_groups=mesh['sta'=32,'tpl'=8] {'sta'}, dimensions={0} | all-to-all | bytes 1835008 | tf_op jit(solution)/shard_map/cond/branch_0_fun/all_to_all | solution.py:471
  62.4 3.1 %branch_0_fun.1 = (f32[8,16,288]{2,1,0:T(8,128)S(1)}, f32[16,288]{1,0:T(8,128)S(1)}) custom-call(s32[8,128]{1,0:T(8,128)S(1)} %get-tuple-element.14.list_ref, s32[8]{0:T(128)S(1)} %get-tuple-element.15.count_ref, s16[32,7,16,128]{3,2,1,0:T(8,128)(2,1)S(1)} %all_to_all.17.back_ref), custom_call_target="tpu_custom_call" | custom-call | tf_op jit(solution)/shard_map/cond/branch_0_fun/pallas_call | solution.py:406
  65.5 0.1 copy.10
  65.6 0.1 reshape_reshape.3
  65.7 0.1 collective-permute-start
  65.8 3.8 %collective-permute-done = f32[36,128]{1,0:T(8,128)S(1)} collective-permute-done((f32[36,128]{1,0:T(8,128)S(1)}, f32[36,128]{1,0:T(8,128)S(1)}, u32[]{:S(2)}, u32[]{:S(2)}) %collective-permute-start) | collective-permute-done | bytes 18464 | tf_op jit(solution)/shard_map/ppermute | solution.py:491
  69.6 3.2 %collective-permute-start.1 = (f32[36,128]{1,0:T(8,128)S(1)}, f32[36,128]{1,0:T(8,128)S(1)}, u32[]{:S(2)}, u32[]{:S(2)}) collective-permute-start(f32[36,128]{1,0:T(8,128)S(1)} %max.24), channel_id=1, source_target_pairs={{0,2},{1,3},{2,0},{3,1},{4,6},{5,7},{6,4},{7,5},{8,10},{9,11},{10,... | collective-permute-start | bytes 55304 | tf_op jit(solution)/shard_map/ppermute | solution.py:491
  72.8 1.8 %collective-permute-done.1 = f32[36,128]{1,0:T(8,128)S(1)} collective-permute-done((f32[36,128]{1,0:T(8,128)S(1)}, f32[36,128]{1,0:T(8,128)S(1)}, u32[]{:S(2)}, u32[]{:S(2)}) %collective-permute-start.1) | collective-permute-done | bytes 18464 | tf_op jit(solution)/shard_map/ppermute | solution.py:491
  74.5 6.0 %collective-permute-start.2 = (f32[36,128]{1,0:T(8,128)S(1)}, f32[36,128]{1,0:T(8,128)S(1)}, u32[]{:S(2)}, u32[]{:S(2)}) collective-permute-start(f32[36,128]{1,0:T(8,128)S(1)} %max.25), channel_id=1, source_target_pairs={{0,4},{1,5},{2,6},{3,7},{4,0},{5,1},{6,2},{7,3},{8,12},{9,13},{10,... | collective-permute-start | bytes 55304 | tf_op jit(solution)/shard_map/ppermute | solution.py:491
  80.5 1.8 %collective-permute-done.2 = f32[36,128]{1,0:T(8,128)S(1)} collective-permute-done((f32[36,128]{1,0:T(8,128)S(1)}, f32[36,128]{1,0:T(8,128)S(1)}, u32[]{:S(2)}, u32[]{:S(2)}) %collective-permute-start.2) | collective-permute-done | bytes 18464 | tf_op jit(solution)/shard_map/ppermute | solution.py:491
  82.3 0.0 collective-permute-start.3
  82.3 1.2 %collective-permute-done.3 = f32[36,128]{1,0:T(8,128)S(1)} collective-permute-done((f32[36,128]{1,0:T(8,128)S(1)}, f32[36,128]{1,0:T(8,128)S(1)}, u32[]{:S(2)}, u32[]{:S(2)}) %collective-permute-start.3) | collective-permute-done | bytes 18464 | tf_op jit(solution)/shard_map/ppermute | solution.py:491
  83.5 0.8 collective-permute-start.4
  84.3 3.0 %collective-permute-done.4 = f32[36,128]{1,0:T(8,128)S(1)} collective-permute-done((f32[36,128]{1,0:T(8,128)S(1)}, f32[36,128]{1,0:T(8,128)S(1)}, u32[]{:S(2)}, u32[]{:S(2)}) %collective-permute-start.4) | collective-permute-done | bytes 18464 | tf_op jit(solution)/shard_map/ppermute | solution.py:491
  87.3 2.0 %collective-permute-start.5 = (f32[36,128]{1,0:T(8,128)S(1)}, f32[36,128]{1,0:T(8,128)S(1)}, u32[]{:S(2)}, u32[]{:S(2)}) collective-permute-start(f32[36,128]{1,0:T(8,128)S(1)} %max.28), channel_id=1, source_target_pairs={{0,32},{8,40},{16,48},{24,56},{32,0},{40,8},{48,16},{56,24},{64,96... | collective-permute-start | bytes 55304 | tf_op jit(solution)/shard_map/ppermute | solution.py:491
  89.3 3.3 %collective-permute-done.5 = f32[36,128]{1,0:T(8,128)S(1)} collective-permute-done((f32[36,128]{1,0:T(8,128)S(1)}, f32[36,128]{1,0:T(8,128)S(1)}, u32[]{:S(2)}, u32[]{:S(2)}) %collective-permute-start.5) | collective-permute-done | bytes 18464 | tf_op jit(solution)/shard_map/ppermute | solution.py:491
  92.6 0.0 collective-permute-start.6
  92.6 3.8 %collective-permute-done.6 = f32[36,128]{1,0:T(8,128)S(1)} collective-permute-done((f32[36,128]{1,0:T(8,128)S(1)}, f32[36,128]{1,0:T(8,128)S(1)}, u32[]{:S(2)}, u32[]{:S(2)}) %collective-permute-start.6) | collective-permute-done | bytes 18464 | tf_op jit(solution)/shard_map/ppermute | solution.py:491
  96.4 1.4 %collective-permute-start.7 = (f32[36,128]{1,0:T(8,128)S(1)}, f32[36,128]{1,0:T(8,128)S(1)}, u32[]{:S(2)}, u32[]{:S(2)}) collective-permute-start(f32[36,128]{1,0:T(8,128)S(1)} %max.30), channel_id=1, source_target_pairs={{0,128},{8,136},{16,144},{24,152},{32,160},{40,168},{48,176},{56,1... | collective-permute-start | bytes 55304 | tf_op jit(solution)/shard_map/ppermute | solution.py:491
  97.8 0.4 copy.9
  98.2 1.4 %reshape.18 = f32[8,4608]{1,0:T(8,128)} reshape(f32[8,288,16]{2,1,0:T(8,128)S(1)} %copy.9) | data formatting | bytes 294912 | tf_op jit(solution)/shard_map/reshape | solution.py:480
  99.6 2.1 %collective-permute-done.7 = f32[36,128]{1,0:T(8,128)S(1)} collective-permute-done((f32[36,128]{1,0:T(8,128)S(1)}, f32[36,128]{1,0:T(8,128)S(1)}, u32[]{:S(2)}, u32[]{:S(2)}) %collective-permute-start.7) | collective-permute-done | bytes 18464 | tf_op jit(solution)/shard_map/ppermute | solution.py:491
  101.7 0.6 maximum_bitcast_fusion
  (7 shorter events, 0.0 us)
Async XLA Ops:
  3.4 21.7 %all-to-all-start.3 = ((bf16[32,8,896]{2,1,0:T(8,128)(2,1)}), bf16[32,8,896]{2,1,0:T(8,128)(2,1)S(1)}, u32[]{:S(2)}, u32[]{:S(2)}) async-start(bf16[32,8,896]{2,1,0:T(8,128)(2,1)} %get-tuple-element.32), calls=%async_computation.3 | async-start | bytes 917504 | tf_op jit(solution)/shard_map/all_to_all | solution.py:451
  10.7 1.0 %copy-start.1 = (bf16[16,3,5376]{2,0,1:T(8,128)(2,1)S(1)}, bf16[16,3,5376]{2,0,1:T(8,128)(2,1)}, u32[]{:S(2)}) copy-start(bf16[16,3,5376]{2,0,1:T(8,128)(2,1)} %param.8) | copy-start | bytes 1548292
  24.3 0.8 copy-start
  25.1 0.8 copy-start.2
  25.8 13.3 %copy-start.3 = (s32[8]{0:T(128)S(1)}, s32[8]{0:T(128)}, u32[]{:S(2)}) copy-start(s32[8]{0:T(128)} %counts_hbm.1) | copy-start | bytes 100
  65.7 3.9 %collective-permute-start = (f32[36,128]{1,0:T(8,128)S(1)}, f32[36,128]{1,0:T(8,128)S(1)}, u32[]{:S(2)}, u32[]{:S(2)}) collective-permute-start(f32[36,128]{1,0:T(8,128)S(1)} %reshape_reshape.3), channel_id=1, source_target_pairs={{0,1},{1,0},{2,3},{3,2},{4,5},{5,4},{6,7},{7,6},{8,9},{9,8},{10,11... | collective-permute-start | bytes 55304 | tf_op jit(solution)/shard_map/ppermute | solution.py:491
  69.6 4.9 %collective-permute-start.1 = (f32[36,128]{1,0:T(8,128)S(1)}, f32[36,128]{1,0:T(8,128)S(1)}, u32[]{:S(2)}, u32[]{:S(2)}) collective-permute-start(f32[36,128]{1,0:T(8,128)S(1)} %max.24), channel_id=1, source_target_pairs={{0,2},{1,3},{2,0},{3,1},{4,6},{5,7},{6,4},{7,5},{8,10},{9,11},{10,... | collective-permute-start | bytes 55304 | tf_op jit(solution)/shard_map/ppermute | solution.py:491
  74.5 7.8 %collective-permute-start.2 = (f32[36,128]{1,0:T(8,128)S(1)}, f32[36,128]{1,0:T(8,128)S(1)}, u32[]{:S(2)}, u32[]{:S(2)}) collective-permute-start(f32[36,128]{1,0:T(8,128)S(1)} %max.25), channel_id=1, source_target_pairs={{0,4},{1,5},{2,6},{3,7},{4,0},{5,1},{6,2},{7,3},{8,12},{9,13},{10,... | collective-permute-start | bytes 55304 | tf_op jit(solution)/shard_map/ppermute | solution.py:491
  82.3 1.2 %collective-permute-start.3 = (f32[36,128]{1,0:T(8,128)S(1)}, f32[36,128]{1,0:T(8,128)S(1)}, u32[]{:S(2)}, u32[]{:S(2)}) collective-permute-start(f32[36,128]{1,0:T(8,128)S(1)} %max.26), channel_id=1, source_target_pairs={{0,8},{8,0},{16,24},{24,16},{32,40},{40,32},{48,56},{56,48},{64,72... | collective-permute-start | bytes 55304 | tf_op jit(solution)/shard_map/ppermute | solution.py:491
  83.5 3.8 %collective-permute-start.4 = (f32[36,128]{1,0:T(8,128)S(1)}, f32[36,128]{1,0:T(8,128)S(1)}, u32[]{:S(2)}, u32[]{:S(2)}) collective-permute-start(f32[36,128]{1,0:T(8,128)S(1)} %max.27), channel_id=1, source_target_pairs={{0,16},{8,24},{16,0},{24,8},{32,48},{40,56},{48,32},{56,40},{64,80... | collective-permute-start | bytes 55304 | tf_op jit(solution)/shard_map/ppermute | solution.py:491
  87.3 5.3 %collective-permute-start.5 = (f32[36,128]{1,0:T(8,128)S(1)}, f32[36,128]{1,0:T(8,128)S(1)}, u32[]{:S(2)}, u32[]{:S(2)}) collective-permute-start(f32[36,128]{1,0:T(8,128)S(1)} %max.28), channel_id=1, source_target_pairs={{0,32},{8,40},{16,48},{24,56},{32,0},{40,8},{48,16},{56,24},{64,96... | collective-permute-start | bytes 55304 | tf_op jit(solution)/shard_map/ppermute | solution.py:491
  92.6 3.8 %collective-permute-start.6 = (f32[36,128]{1,0:T(8,128)S(1)}, f32[36,128]{1,0:T(8,128)S(1)}, u32[]{:S(2)}, u32[]{:S(2)}) collective-permute-start(f32[36,128]{1,0:T(8,128)S(1)} %max.29), channel_id=1, source_target_pairs={{0,64},{8,72},{16,80},{24,88},{32,96},{40,104},{48,112},{56,120},{... | collective-permute-start | bytes 55304 | tf_op jit(solution)/shard_map/ppermute | solution.py:491
  96.4 5.3 %collective-permute-start.7 = (f32[36,128]{1,0:T(8,128)S(1)}, f32[36,128]{1,0:T(8,128)S(1)}, u32[]{:S(2)}, u32[]{:S(2)}) collective-permute-start(f32[36,128]{1,0:T(8,128)S(1)} %max.30), channel_id=1, source_target_pairs={{0,128},{8,136},{16,144},{24,152},{32,160},{40,168},{48,176},{56,1... | collective-permute-start | bytes 55304 | tf_op jit(solution)/shard_map/ppermute | solution.py:491

commit v4 on v3

--- a/solution.py
+++ b/solution.py
@@ -20,6 +20,7 @@
 WIDE = 384
 REACH = L // PHASES
 DEPTH = 3 * L + BLOCK
+INV = 3 * L + 3 * PHASES
 CHUNK = 8
 CAP = 6
 ROWS = 8
@@ -127,13 +128,9 @@
     send_ref[:, :, 3 * L :] = tail.reshape(width, ROWS, BLOCK)
 
 
-def prep_kernel(wave_ref, xs_ref, inv_ref, wide_ref):
+def prep_kernel(wave_ref, xs_hbm, xs_ref, wide_ref, sems):
     tiles = wave_ref.shape[2] // BLOCK
-
-    @pl.when(pl.program_id(0) == 0)
-    def _():
-        wide_ref[...] = wave_ref[...].astype(jnp.float32)
-
+    wide_ref[...] = wave_ref[...].astype(jnp.float32)
     lane = iota((8, BLOCK), 1)
     own = (lane // PHASES == iota((8, BLOCK), 0)).astype(jnp.float32)
     spread = (
@@ -141,9 +138,8 @@
         & (iota((3 * PHASES, 3 * BLOCK), 1) % PHASES == iota((3 * PHASES, 3 * BLOCK), 0) % PHASES)
     ).astype(jnp.bfloat16)
     sub = iota((PHASES, WIDE), 0)
-    s = pl.program_id(0)
-
-    def one_station():
+
+    def one_station(s):
         comps = []
         for c in range(3):
             parts = []
@@ -163,8 +159,7 @@
             for r in range(REACH + 1):
                 moved = x if r == 0 else pltpu.roll(x, WIDE - r, 1)
                 at = c * L + r * PHASES if r < REACH else 3 * L + c * PHASES
-                xs_ref[0, at : at + PHASES, :] = moved.astype(jnp.bfloat16)
-        xs_ref[0, 3 * L + 3 * PHASES :, :] = jnp.zeros((DEPTH - 3 * L - 3 * PHASES, WIDE), jnp.bfloat16)
+                xs_ref[s, at : at + PHASES, :] = moved.astype(jnp.bfloat16)
         up = squares
         down = jnp.where(sub >= 1, pltpu.roll(squares, 1, 0), 0.0)
         for step in (1, 2, 4, 8):
@@ -181,13 +176,28 @@
             + pltpu.roll(whole, WIDE - 15, 1)
         )
         power = (up + fifteen + pltpu.roll(down, WIDE - REACH, 1)) / (3.0 * L)
-        inv_ref[0] = 1.0 / (3.0 * L * jnp.sqrt(power + EPS))
-
-    one_station()
+        inv = 1.0 / (3.0 * L * jnp.sqrt(power + EPS))
+        for i in range(3):
+            term = inv.astype(jnp.bfloat16)
+            xs_ref[s, INV + i * PHASES : INV + (i + 1) * PHASES, :] = term
+            inv = inv - term.astype(jnp.float32)
+        xs_ref[s, INV + 3 * PHASES :, :] = jnp.zeros((DEPTH - INV - 3 * PHASES, WIDE), jnp.bfloat16)
+
+    @pl.loop(0, wave_ref.shape[1] // 2)
+    def _(i):
+        one_station(2 * i)
+        one_station(2 * i + 1)
+        pair = pl.ds(2 * i, 2)
+        pltpu.make_async_copy(xs_ref.at[pair], xs_hbm.at[pair], sems.at[i]).start()
+
+    @pl.loop(0, wave_ref.shape[1] // 2)
+    def _(i):
+        pair = pl.ds(2 * i, 2)
+        pltpu.make_async_copy(xs_ref.at[pair], xs_hbm.at[pair], sems.at[i]).wait()
 
 
 def correlate_kernel(
-    got_ref, xs_hbm, inv_ref, out_ref, more_ref, flag_ref, xs_ref, sorted_ref, order_ref, held_ref, table_ref, sem, xs_sems
+    got_ref, xs_hbm, out_ref, more_ref, flag_ref, xs_ref, sorted_ref, order_ref, held_ref, table_ref, sem, xs_sems
 ):
     width = got_ref.shape[0]
     stations = xs_ref.shape[0]
@@ -271,7 +281,8 @@
         mean = jnp.sum(slot * slot, axis=1, keepdims=True) / (3.0 * L)
         unit = 1.0 / jnp.sqrt(mean + EPS)
         corr = dot(toeplitz(slot), xs_ref[s])
-        inv = inv_ref[s]
+        parts = [xs_ref[s, INV + i * PHASES : INV + (i + 1) * PHASES, :].astype(jnp.float32) for i in range(3)]
+        inv = (parts[2] + parts[1]) + parts[0]
         for k in range(CHUNK):
             y = corr[k * PHASES : (k + 1) * PHASES] * (inv * unit[k : k + 1, :])
             move = table_ref[1, first + k] * (BLOCK // PHASES)
@@ -375,9 +386,8 @@
     return pltpu.CompilerParams(vmem_limit_bytes=mib * 2**20)
 
 
-def correlate_call(got, xs, inv):
+def correlate_call(got, xs, stations):
     width = got.shape[0]
-    stations = xs.shape[0]
     room = 8 * (width * CAP // CHUNK + stations)
     return pl.pallas_call(
         correlate_kernel,
@@ -386,7 +396,7 @@
             jax.ShapeDtypeStruct((width, BLOCKS, PHASES, BLOCK), jnp.int16),
             jax.ShapeDtypeStruct((1, BLOCK), jnp.int32),
         ),
-        in_specs=[VMEM, ANY, VMEM],
+        in_specs=[VMEM, ANY],
         out_specs=(VMEM, VMEM, VMEM),
         scratch_shapes=[
             pltpu.VMEM((stations, DEPTH, WIDE), jnp.bfloat16),
@@ -397,8 +407,8 @@
             pltpu.SemaphoreType.DMA,
             pltpu.SemaphoreType.DMA((stations,)),
         ],
-        compiler_params=params(54),
-    )(got, xs, inv)
+        compiler_params=params(40),
+    )(got, xs)
 
 
 def add_call(listed, counts, back):
@@ -415,7 +425,7 @@
             pltpu.VMEM((back.shape[0] * 4, PHASES, BLOCK), jnp.float32),
             pltpu.VMEM((back.shape[0] * 4, PHASES, BLOCK), jnp.float32),
         ],
-        compiler_params=params(32),
+        compiler_params=params(40),
     )(listed, counts, back)
 
 
@@ -449,23 +459,20 @@
         templates.transpose(1, 0, 2),
     )
     got = lax.all_to_all(send, "sta", split_axis=0, concat_axis=0, tiled=True)
-    xs, inv = pl.pallas_call(
+    xs = pl.pallas_call(
         prep_kernel,
-        grid=(stations,),
-        out_shape=(
-            jax.ShapeDtypeStruct((stations, DEPTH, WIDE), jnp.bfloat16),
-            jax.ShapeDtypeStruct((stations, PHASES, WIDE), jnp.float32),
-        ),
-        in_specs=[pl.BlockSpec((3, stations, samples), lambda s: (0, 0, 0))],
-        out_specs=(
-            pl.BlockSpec((1, DEPTH, WIDE), lambda s: (s, 0, 0)),
-            pl.BlockSpec((1, PHASES, WIDE), lambda s: (s, 0, 0)),
-        ),
-        scratch_shapes=[pltpu.VMEM((3, stations, samples), jnp.float32)],
-        compiler_params=params(50),
+        out_shape=jax.ShapeDtypeStruct((2 * stations + 4, DEPTH, WIDE), jnp.bfloat16),
+        in_specs=[VMEM],
+        out_specs=ANY,
+        scratch_shapes=[
+            pltpu.VMEM((stations, DEPTH, WIDE), jnp.bfloat16),
+            pltpu.VMEM((3, stations, samples), jnp.float32),
+            pltpu.SemaphoreType.DMA((stations // 2,)),
+        ],
+        compiler_params=params(40),
         cost_estimate=pl.CostEstimate(flops=2 * 10**9, bytes_accessed=12 * 2**20, transcendentals=0),
     )(waveforms.transpose(1, 0, 2))
-    traces, more, flag = correlate_call(got, xs, inv)
+    traces, more, flag = correlate_call(got, xs, stations)
 
     def home(x):
         return lax.all_to_all(x, "sta", split_axis=0, concat_axis=0, tiled=True)
@@ -484,13 +491,11 @@
 
 
 def best_of_all(best):
-    for axis in ("tpl", "sta"):
+    for axis, steps in (("tpl", (1, 2, 6)), ("sta", (1, 2, 6, 8, 24))):
         size = lax.axis_size(axis)
-        step = 1
-        while step < size:
+        for step in steps:
             other = lax.ppermute(best, axis, [(i, i ^ step) for i in range(size)])
             best = jnp.maximum(best, other)
-            step *= 2
     return best
 
 

time: 103 us -> 92.8 us (0.901)
  Pallas kernels: 31.1 us -> 23.7 us
  waiting for transfers between devices: 20.8 us -> 23.1 us
  starting transfers between devices: 20.7 us -> 18.7 us
  local copies, waits for them, and re-layouts: 4.49 us -> 2.97 us
    pallas_call x1, Pallas kernels: 12.6 us -> 7.51 us  [body(): pl.pallas_call(prep_kernel, out_shape=jax.ShapeDtypeStruct((2 * stations...]
    pallas_call x1, Pallas kernels: 12.7 us -> 10.4 us  [correlate_call(): pl.pallas_call(correlate_kernel, out_shape=(jax.ShapeDtypeStruct((width,...]
    ppermute x8, starting transfers between devices: 13.4 us -> 11.4 us  [best_of_all(): other = lax.ppermute(best, axis, [(i, i ^ step) for i in range(size)])]
    all_to_all x1, waiting for transfers between devices: 0.01 us -> 1.98 us  [body(): got = lax.all_to_all(send, 'sta', split_axis=0, concat_axis=0, tiled=True)]
    unnamed x8 -> x4, local copies, waits for them, and re-layouts: 2.56 us -> 1.04 us
  transfers between devices with their start and end apart: 9 -> 9, of which waited for: 8 -> 9; matrix products, arithmetic and copies ran while one was open for 2% -> 2% of each run, Pallas kernels for 12% -> 8%
where the time goes in v4:
time: 92.8 us; the launch traced here: 92.2 us
  Pallas kernels  23.7 us (26%)
  waiting for transfers between devices  23.1 us (25%)
  blocking collectives  22.2 us (24%)
  starting transfers between devices  18.7 us (20%)
  local copies, waits for them, and re-layouts  2.97 us (3%)
    all_to_all x1, blocking collectives, home(): return lax.all_to_all(x, 'sta', split_axis=0, concat_axis=0, tiled=True)  22.2 us
    ppermute x8, waiting for transfers between devices, best_of_all(): other = lax.ppermute(best, axis, [(i, i ^ step) for i in range(size)])  21.1 us
    ppermute x8, starting transfers between devices, best_of_all(): other = lax.ppermute(best, axis, [(i, i ^ step) for i in range(size)])  11.4 us
    pallas_call x1, Pallas kernels, correlate_call(): pl.pallas_call(correlate_kernel, out_shape=(jax.ShapeDtypeStruct((width,...  10.4 us
    pallas_call x1, Pallas kernels, body(): pl.pallas_call(prep_kernel, out_shape=jax.ShapeDtypeStruct((2 * stations...  7.51 us
    all_to_all x1, starting transfers between devices, body(): got = lax.all_to_all(send, 'sta', split_axis=0, concat_axis=0, tiled=True)  7.33 us
    pallas_call x1, Pallas kernels, add_call(): pl.pallas_call(add_kernel, out_shape=(jax.ShapeDtypeStruct((tpl_dev, PHAS...  3.05 us
    pallas_call x1, Pallas kernels, body(): pl.pallas_call(pack_kernel, out_shape=(jax.ShapeDtypeStruct((width, ROWS,...  2.79 us
  transfers between devices with their start and end apart: 9, of which 9 were waited for; matrix products, arithmetic and copies ran while one was open for 2% of the time, Pallas kernels for 8%

profile of v4, /device:TPU:32, one launch (start us, length us, event | category | flops | bytes accessed | tf_op | source)
XLA Modules:
  0.0 92.2 jit_solution(13792143146973542121)
XLA Ops:
  0.6 2.8 %shard_map.77 = (bf16[32,8,896]{2,1,0:T(8,128)(2,1)}, s32[8,128]{1,0:T(8,128)S(1)}) custom-call(s32[8,20]{1,0:T(8,128)} %stations_hbm.1, s32[8,20]{1,0:T(8,128)} %moves_hbm.1, s32[8]{0:T(128)} %counts_hbm.1, s32[4,128]{1,0:T(4,128)} %bitcast.14, bf16[20,8,768]{2,1,0:T(8,128)(2,1)} %bitcast.11), custom_call_target="tpu_custom_call" | custom-call | tf_op jit(solution)/shard_map/pallas_call | solution.py:437
  3.4 7.3 %all-to-all-start.3 = ((bf16[32,8,896]{2,1,0:T(8,128)(2,1)}), bf16[32,8,896]{2,1,0:T(8,128)(2,1)S(1)}, u32[]{:S(2)}, u32[]{:S(2)}) async-start(bf16[32,8,896]{2,1,0:T(8,128)(2,1)} %get-tuple-element.30), calls=%async_computation.3 | async-start | bytes 917504 | tf_op jit(solution)/shard_map/all_to_all | solution.py:461
  10.8 0.0 copy-start
  10.8 1.0 %copy-done = bf16[16,3,5376]{2,0,1:T(8,128)(2,1)S(1)} copy-done((bf16[16,3,5376]{2,0,1:T(8,128)(2,1)S(1)}, bf16[16,3,5376]{2,0,1:T(8,128)(2,1)}, u32[]{:S(2)}) %copy-start) | copy-done | bytes 516120
  11.8 7.5 %shard_map.78.xs_hbm = bf16[36,896,384]{2,1,0:T(8,128)(2,1)} custom-call(bf16[3,16,5376]{2,1,0:T(8,128)(2,1)S(1)} %bitcast.9), custom_call_target="tpu_custom_call" | custom-call | flops 2000000000 | bytes 12582912 | tf_op jit(solution)/shard_map/pallas_call | solution.py:462
  19.3 0.0 copy-start.1
  19.3 2.0 %all-to-all-done.3.got_ref = bf16[32,8,896]{2,1,0:T(8,128)(2,1)S(1)} async-done(((bf16[32,8,896]{2,1,0:T(8,128)(2,1)}), bf16[32,8,896]{2,1,0:T(8,128)(2,1)S(1)}, u32[]{:S(2)}, u32[]{:S(2)}) %all-to-all-start.3) | async-done | bytes 458784 | tf_op jit(solution)/shard_map/all_to_all | solution.py:461
  21.3 10.4 %shard_map.79 = (s16[32,7,16,128]{3,2,1,0:T(8,128)(2,1)S(1)}, s16[32,7,16,128]{3,2,1,0:T(8,128)(2,1)S(1)}, s32[1,128]{1,0:T(1,128)S(1)}) custom-call(bf16[32,8,896]{2,1,0:T(8,128)(2,1)S(1)} %all-to-all-done.3.got_ref, bf16[36,896,384]{2,1,0:T(8,128)(2,1)} %shard_map.78.xs_hbm), custom_call_target="tpu_custom_call" | custom-call | tf_op jit(solution)/shard_map/pallas_call | solution.py:392
  31.7 0.0 copy-done.1
  31.7 25.3 %conditional.1 = ((f32[8,16,288]{2,1,0:T(8,128)S(1)}, f32[16,288]{1,0:T(8,128)S(1)})) conditional(s32[]{:T(128)} %bitcast.3, (s16[32,7,16,128]{3,2,1,0:T(8,128)(2,1)S(1)}, s32[8,128]{1,0:T(8,128)S(1)}, s32[8]{0:T(128)S(1)}) %tuple.21, (s16[32,7,16,128]{3,2,1,0:T(8,128)(2,1)S(1)}, s16[32,7,16,128]{3,2,1,0:T(8,128)(2,1)S(1)}, s32[8,128]{1,0:T(8,128)S(1)}, ...), branch_computations={%region_0.0_spmd, %region_1.0_spmd} | conditional | flops 917504 | bytes 7340040 | solution.py:486
  31.7 22.2 %all_to_all.17.back_ref = s16[32,7,16,128]{3,2,1,0:T(8,128)(2,1)S(1)} all-to-all(s16[32,7,16,128]{3,2,1,0:T(8,128)(2,1)S(1)} %get-tuple-element.16), channel_id=1, replica_groups=mesh['sta'=32,'tpl'=8] {'sta'}, dimensions={0} | all-to-all | bytes 1835008 | tf_op jit(solution)/shard_map/cond/branch_0_fun/all_to_all | solution.py:478
  54.0 3.0 %branch_0_fun.1 = (f32[8,16,288]{2,1,0:T(8,128)S(1)}, f32[16,288]{1,0:T(8,128)S(1)}) custom-call(s32[8,128]{1,0:T(8,128)S(1)} %get-tuple-element.14.list_ref, s32[8]{0:T(128)S(1)} %get-tuple-element.15.count_ref, s16[32,7,16,128]{3,2,1,0:T(8,128)(2,1)S(1)} %all_to_all.17.back_ref), custom_call_target="tpu_custom_call" | custom-call | tf_op jit(solution)/shard_map/cond/branch_0_fun/pallas_call | solution.py:416
  57.0 0.1 copy.10
  57.1 0.1 reshape_reshape.3
  57.3 0.1 collective-permute-start
  57.4 3.8 %collective-permute-done = f32[36,128]{1,0:T(8,128)S(1)} collective-permute-done((f32[36,128]{1,0:T(8,128)S(1)}, f32[36,128]{1,0:T(8,128)S(1)}, u32[]{:S(2)}, u32[]{:S(2)}) %collective-permute-start) | collective-permute-done | bytes 18464 | tf_op jit(solution)/shard_map/ppermute | solution.py:497
  61.1 2.3 %collective-permute-start.1 = (f32[36,128]{1,0:T(8,128)S(1)}, f32[36,128]{1,0:T(8,128)S(1)}, u32[]{:S(2)}, u32[]{:S(2)}) collective-permute-start(f32[36,128]{1,0:T(8,128)S(1)} %max.24), channel_id=1, source_target_pairs={{0,2},{1,3},{2,0},{3,1},{4,6},{5,7},{6,4},{7,5},{8,10},{9,11},{10,... | collective-permute-start | bytes 55304 | tf_op jit(solution)/shard_map/ppermute | solution.py:497
  63.5 2.3 %collective-permute-done.1 = f32[36,128]{1,0:T(8,128)S(1)} collective-permute-done((f32[36,128]{1,0:T(8,128)S(1)}, f32[36,128]{1,0:T(8,128)S(1)}, u32[]{:S(2)}, u32[]{:S(2)}) %collective-permute-start.1) | collective-permute-done | bytes 18464 | tf_op jit(solution)/shard_map/ppermute | solution.py:497
  65.8 5.2 %collective-permute-start.2 = (f32[36,128]{1,0:T(8,128)S(1)}, f32[36,128]{1,0:T(8,128)S(1)}, u32[]{:S(2)}, u32[]{:S(2)}) collective-permute-start(f32[36,128]{1,0:T(8,128)S(1)} %max.25), channel_id=1, source_target_pairs={{0,6},{1,7},{2,4},{3,5},{4,2},{5,3},{6,0},{7,1},{8,14},{9,15},{10,... | collective-permute-start | bytes 55304 | tf_op jit(solution)/shard_map/ppermute | solution.py:497
  71.0 1.8 %collective-permute-done.2 = f32[36,128]{1,0:T(8,128)S(1)} collective-permute-done((f32[36,128]{1,0:T(8,128)S(1)}, f32[36,128]{1,0:T(8,128)S(1)}, u32[]{:S(2)}, u32[]{:S(2)}) %collective-permute-start.2) | collective-permute-done | bytes 18464 | tf_op jit(solution)/shard_map/ppermute | solution.py:497
  72.8 0.0 collective-permute-start.3
  72.8 1.2 %collective-permute-done.3 = f32[36,128]{1,0:T(8,128)S(1)} collective-permute-done((f32[36,128]{1,0:T(8,128)S(1)}, f32[36,128]{1,0:T(8,128)S(1)}, u32[]{:S(2)}, u32[]{:S(2)}) %collective-permute-start.3) | collective-permute-done | bytes 18464 | tf_op jit(solution)/shard_map/ppermute | solution.py:497
  74.0 0.6 collective-permute-start.4
  74.6 3.2 %collective-permute-done.4 = f32[36,128]{1,0:T(8,128)S(1)} collective-permute-done((f32[36,128]{1,0:T(8,128)S(1)}, f32[36,128]{1,0:T(8,128)S(1)}, u32[]{:S(2)}, u32[]{:S(2)}) %collective-permute-start.4) | collective-permute-done | bytes 18464 | tf_op jit(solution)/shard_map/ppermute | solution.py:497
  77.8 1.5 %collective-permute-start.5 = (f32[36,128]{1,0:T(8,128)S(1)}, f32[36,128]{1,0:T(8,128)S(1)}, u32[]{:S(2)}, u32[]{:S(2)}) collective-permute-start(f32[36,128]{1,0:T(8,128)S(1)} %max.28), channel_id=1, source_target_pairs={{0,48},{8,56},{16,32},{24,40},{32,16},{40,24},{48,0},{56,8},{64,11... | collective-permute-start | bytes 55304 | tf_op jit(solution)/shard_map/ppermute | solution.py:497
  79.3 3.5 %collective-permute-done.5 = f32[36,128]{1,0:T(8,128)S(1)} collective-permute-done((f32[36,128]{1,0:T(8,128)S(1)}, f32[36,128]{1,0:T(8,128)S(1)}, u32[]{:S(2)}, u32[]{:S(2)}) %collective-permute-start.5) | collective-permute-done | bytes 18464 | tf_op jit(solution)/shard_map/ppermute | solution.py:497
  82.8 0.0 collective-permute-start.6
  82.8 3.8 %collective-permute-done.6 = f32[36,128]{1,0:T(8,128)S(1)} collective-permute-done((f32[36,128]{1,0:T(8,128)S(1)}, f32[36,128]{1,0:T(8,128)S(1)}, u32[]{:S(2)}, u32[]{:S(2)}) %collective-permute-start.6) | collective-permute-done | bytes 18464 | tf_op jit(solution)/shard_map/ppermute | solution.py:497
  86.6 1.6 %collective-permute-start.7 = (f32[36,128]{1,0:T(8,128)S(1)}, f32[36,128]{1,0:T(8,128)S(1)}, u32[]{:S(2)}, u32[]{:S(2)}) collective-permute-start(f32[36,128]{1,0:T(8,128)S(1)} %max.30), channel_id=1, source_target_pairs={{0,192},{8,200},{16,208},{24,216},{32,224},{40,232},{48,240},{56,2... | collective-permute-start | bytes 55304 | tf_op jit(solution)/shard_map/ppermute | solution.py:497
  88.2 0.4 copy.9
  88.6 1.4 %reshape.18 = f32[8,4608]{1,0:T(8,128)} reshape(f32[8,288,16]{2,1,0:T(8,128)S(1)} %copy.9) | data formatting | bytes 294912 | tf_op jit(solution)/shard_map/reshape | solution.py:487
  89.9 1.6 %collective-permute-done.7 = f32[36,128]{1,0:T(8,128)S(1)} collective-permute-done((f32[36,128]{1,0:T(8,128)S(1)}, f32[36,128]{1,0:T(8,128)S(1)}, u32[]{:S(2)}, u32[]{:S(2)}) %collective-permute-start.7) | collective-permute-done | bytes 18464 | tf_op jit(solution)/shard_map/ppermute | solution.py:497
  91.6 0.6 maximum_bitcast_fusion
  (7 shorter events, 0.0 us)
Async XLA Ops:
  3.4 17.9 %all-to-all-start.3 = ((bf16[32,8,896]{2,1,0:T(8,128)(2,1)}), bf16[32,8,896]{2,1,0:T(8,128)(2,1)S(1)}, u32[]{:S(2)}, u32[]{:S(2)}) async-start(bf16[32,8,896]{2,1,0:T(8,128)(2,1)} %get-tuple-element.30), calls=%async_computation.3 | async-start | bytes 917504 | tf_op jit(solution)/shard_map/all_to_all | solution.py:461
  10.8 1.0 %copy-start = (bf16[16,3,5376]{2,0,1:T(8,128)(2,1)S(1)}, bf16[16,3,5376]{2,0,1:T(8,128)(2,1)}, u32[]{:S(2)}) copy-start(bf16[16,3,5376]{2,0,1:T(8,128)(2,1)} %param.8) | copy-start | bytes 1548292
  19.3 12.4 %copy-start.1 = (s32[8]{0:T(128)S(1)}, s32[8]{0:T(128)}, u32[]{:S(2)}) copy-start(s32[8]{0:T(128)} %counts_hbm.1) | copy-start | bytes 100
  57.3 3.9 %collective-permute-start = (f32[36,128]{1,0:T(8,128)S(1)}, f32[36,128]{1,0:T(8,128)S(1)}, u32[]{:S(2)}, u32[]{:S(2)}) collective-permute-start(f32[36,128]{1,0:T(8,128)S(1)} %reshape_reshape.3), channel_id=1, source_target_pairs={{0,1},{1,0},{2,3},{3,2},{4,5},{5,4},{6,7},{7,6},{8,9},{9,8},{10,11... | collective-permute-start | bytes 55304 | tf_op jit(solution)/shard_map/ppermute | solution.py:497
  61.1 4.7 %collective-permute-start.1 = (f32[36,128]{1,0:T(8,128)S(1)}, f32[36,128]{1,0:T(8,128)S(1)}, u32[]{:S(2)}, u32[]{:S(2)}) collective-permute-start(f32[36,128]{1,0:T(8,128)S(1)} %max.24), channel_id=1, source_target_pairs={{0,2},{1,3},{2,0},{3,1},{4,6},{5,7},{6,4},{7,5},{8,10},{9,11},{10,... | collective-permute-start | bytes 55304 | tf_op jit(solution)/shard_map/ppermute | solution.py:497
  65.8 7.0 %collective-permute-start.2 = (f32[36,128]{1,0:T(8,128)S(1)}, f32[36,128]{1,0:T(8,128)S(1)}, u32[]{:S(2)}, u32[]{:S(2)}) collective-permute-start(f32[36,128]{1,0:T(8,128)S(1)} %max.25), channel_id=1, source_target_pairs={{0,6},{1,7},{2,4},{3,5},{4,2},{5,3},{6,0},{7,1},{8,14},{9,15},{10,... | collective-permute-start | bytes 55304 | tf_op jit(solution)/shard_map/ppermute | solution.py:497
  72.8 1.2 %collective-permute-start.3 = (f32[36,128]{1,0:T(8,128)S(1)}, f32[36,128]{1,0:T(8,128)S(1)}, u32[]{:S(2)}, u32[]{:S(2)}) collective-permute-start(f32[36,128]{1,0:T(8,128)S(1)} %max.26), channel_id=1, source_target_pairs={{0,8},{8,0},{16,24},{24,16},{32,40},{40,32},{48,56},{56,48},{64,72... | collective-permute-start | bytes 55304 | tf_op jit(solution)/shard_map/ppermute | solution.py:497
  74.0 3.8 %collective-permute-start.4 = (f32[36,128]{1,0:T(8,128)S(1)}, f32[36,128]{1,0:T(8,128)S(1)}, u32[]{:S(2)}, u32[]{:S(2)}) collective-permute-start(f32[36,128]{1,0:T(8,128)S(1)} %max.27), channel_id=1, source_target_pairs={{0,16},{8,24},{16,0},{24,8},{32,48},{40,56},{48,32},{56,40},{64,80... | collective-permute-start | bytes 55304 | tf_op jit(solution)/shard_map/ppermute | solution.py:497
  77.8 5.0 %collective-permute-start.5 = (f32[36,128]{1,0:T(8,128)S(1)}, f32[36,128]{1,0:T(8,128)S(1)}, u32[]{:S(2)}, u32[]{:S(2)}) collective-permute-start(f32[36,128]{1,0:T(8,128)S(1)} %max.28), channel_id=1, source_target_pairs={{0,48},{8,56},{16,32},{24,40},{32,16},{40,24},{48,0},{56,8},{64,11... | collective-permute-start | bytes 55304 | tf_op jit(solution)/shard_map/ppermute | solution.py:497
  82.8 3.8 %collective-permute-start.6 = (f32[36,128]{1,0:T(8,128)S(1)}, f32[36,128]{1,0:T(8,128)S(1)}, u32[]{:S(2)}, u32[]{:S(2)}) collective-permute-start(f32[36,128]{1,0:T(8,128)S(1)} %max.29), channel_id=1, source_target_pairs={{0,64},{8,72},{16,80},{24,88},{32,96},{40,104},{48,112},{56,120},{... | collective-permute-start | bytes 55304 | tf_op jit(solution)/shard_map/ppermute | solution.py:497
  86.6 5.0 %collective-permute-start.7 = (f32[36,128]{1,0:T(8,128)S(1)}, f32[36,128]{1,0:T(8,128)S(1)}, u32[]{:S(2)}, u32[]{:S(2)}) collective-permute-start(f32[36,128]{1,0:T(8,128)S(1)} %max.30), channel_id=1, source_target_pairs={{0,192},{8,200},{16,208},{24,216},{32,224},{40,232},{48,240},{56,2... | collective-permute-start | bytes 55304 | tf_op jit(solution)/shard_map/ppermute | solution.py:497

commit v5 on v4

--- a/solution.py
+++ b/solution.py
@@ -240,9 +240,9 @@
     sorted_ref[...] = dot(pick, pieces)
     blank = jnp.zeros((PHASES, WIDE), jnp.float32)
 
-    @pl.loop(0, held_ref.shape[0] // 8)
+    @pl.loop(0, jnp.where(over > 0.5, width, width // 2))
     def _(i):
-        for r in range(8):
+        for r in (0, 1, 2, 4, 5, 6):
             held_ref[8 * i + r] = blank
 
     copy.wait()
@@ -323,10 +323,10 @@
             last = jnp.where(lane == HALF * end + r, power, last)
         ref[o, 2 * HALF] = last.astype(jnp.int32).astype(jnp.int16)
 
-    @pl.loop(0, width // 2)
+    @pl.loop(0, width // 4)
     def _(i):
-        finish(out_ref, 2 * i, 2 * i)
-        finish(out_ref, 2 * i + 1, 2 * i + 1)
+        for r in range(4):
+            finish(out_ref, 4 * i + r, 4 * i + r)
 
     @pl.when(table_ref[5, 0] > 0)
     def _():
@@ -341,9 +341,10 @@
     def wide(x):
         return x.astype(jnp.int32).astype(jnp.float32)
 
-    @pl.loop(0, back_ref.shape[0] // 2)
+    @pl.loop(0, back_ref.shape[0] // 4)
     def _(i):
-        for o in (2 * i, 2 * i + 1):
+        for part in range(4):
+            o = 4 * i + part
             last = wide(back_ref[o, 2 * HALF])
             scales = jnp.exp2(last * (1.0 / FINE)) * (1.0 / FULL)
             for r in range(HALF):
@@ -491,10 +492,11 @@
 
 
 def best_of_all(best):
-    for axis, steps in (("tpl", (1, 2, 6)), ("sta", (1, 2, 6, 8, 24))):
+    rounds = (("tpl", (1, 2, 3)), ("tpl", (6,)), ("sta", (1,)), ("sta", (2, 6, 4)), ("sta", (8, 24, 16)))
+    for axis, steps in rounds:
         size = lax.axis_size(axis)
-        for step in steps:
-            other = lax.ppermute(best, axis, [(i, i ^ step) for i in range(size)])
+        others = [lax.ppermute(best, axis, [(i, i ^ step) for i in range(size)]) for step in steps]
+        for other in others:
             best = jnp.maximum(best, other)
     return best
 

time: 92.8 us -> 85.6 us (0.922)
  waiting for transfers between devices: 23.1 us -> 12.6 us
  starting transfers between devices: 18.7 us -> 23.8 us
  blocking collectives: 22.2 us -> 21.2 us
    ppermute x8 -> x11, waiting for transfers between devices: 21.1 us -> 10.6 us  [best_of_all(): lax.ppermute(best, axis, [(i, i ^ step) for i in range(size)])]
    ppermute x8 -> x11, starting transfers between devices: 11.4 us -> 16.5 us  [best_of_all(): lax.ppermute(best, axis, [(i, i ^ step) for i in range(size)])]
    all_to_all x1, blocking collectives: 22.2 us -> 21.2 us  [home(): return lax.all_to_all(x, 'sta', split_axis=0, concat_axis=0, tiled=True)]
  transfers between devices with their start and end apart: 9 -> 12, of which waited for: 9 -> 10; matrix products, arithmetic and copies ran while one was open for 2% -> 2% of each run, Pallas kernels for 8% -> 9%
where the time goes in v5:
time: 85.6 us; the launch traced here: 84.8 us
  starting transfers between devices  23.8 us (28%)
  Pallas kernels  22.8 us (27%)
  blocking collectives  21.2 us (25%)
  waiting for transfers between devices  12.6 us (15%)
  local copies, waits for them, and re-layouts  2.97 us (3%)
    all_to_all x1, blocking collectives, home(): return lax.all_to_all(x, 'sta', split_axis=0, concat_axis=0, tiled=True)  21.2 us
    ppermute x11, starting transfers between devices, best_of_all(): lax.ppermute(best, axis, [(i, i ^ step) for i in range(size)])  16.5 us
    ppermute x11, waiting for transfers between devices, best_of_all(): lax.ppermute(best, axis, [(i, i ^ step) for i in range(size)])  10.6 us
    pallas_call x1, Pallas kernels, correlate_call(): pl.pallas_call(correlate_kernel, out_shape=(jax.ShapeDtypeStruct((width,...  9.96 us
    pallas_call x1, Pallas kernels, body(): pl.pallas_call(prep_kernel, out_shape=jax.ShapeDtypeStruct((2 * stations...  7.51 us
    all_to_all x1, starting transfers between devices, body(): got = lax.all_to_all(send, 'sta', split_axis=0, concat_axis=0, tiled=True)  7.33 us
    pallas_call x1, Pallas kernels, body(): pl.pallas_call(pack_kernel, out_shape=(jax.ShapeDtypeStruct((width, ROWS,...  2.79 us
    pallas_call x1, Pallas kernels, add_call(): pl.pallas_call(add_kernel, out_shape=(jax.ShapeDtypeStruct((tpl_dev, PHAS...  2.58 us
  transfers between devices with their start and end apart: 12, of which 10 were waited for; matrix products, arithmetic and copies ran while one was open for 2% of the time, Pallas kernels for 9%

profile of v5, /device:TPU:32, one launch (start us, length us, event | category | flops | bytes accessed | tf_op | source)
XLA Modules:
  0.0 84.8 jit_solution(12628658734346056488)
XLA Ops:
  0.6 2.8 %shard_map.77 = (bf16[32,8,896]{2,1,0:T(8,128)(2,1)}, s32[8,128]{1,0:T(8,128)S(1)}) custom-call(s32[8,20]{1,0:T(8,128)} %stations_hbm.1, s32[8,20]{1,0:T(8,128)} %moves_hbm.1, s32[8]{0:T(128)} %counts_hbm.1, s32[4,128]{1,0:T(4,128)} %bitcast.14, bf16[20,8,768]{2,1,0:T(8,128)(2,1)} %bitcast.11), custom_call_target="tpu_custom_call" | custom-call | tf_op jit(solution)/shard_map/pallas_call | solution.py:438
  3.4 7.3 %all-to-all-start.3 = ((bf16[32,8,896]{2,1,0:T(8,128)(2,1)}), bf16[32,8,896]{2,1,0:T(8,128)(2,1)S(1)}, u32[]{:S(2)}, u32[]{:S(2)}) async-start(bf16[32,8,896]{2,1,0:T(8,128)(2,1)} %get-tuple-element.30), calls=%async_computation.3 | async-start | bytes 917504 | tf_op jit(solution)/shard_map/all_to_all | solution.py:462
  10.8 0.0 copy-start
  10.8 1.0 %copy-done = bf16[16,3,5376]{2,0,1:T(8,128)(2,1)S(1)} copy-done((bf16[16,3,5376]{2,0,1:T(8,128)(2,1)S(1)}, bf16[16,3,5376]{2,0,1:T(8,128)(2,1)}, u32[]{:S(2)}) %copy-start) | copy-done | bytes 516120
  11.8 7.5 %shard_map.78.xs_hbm = bf16[36,896,384]{2,1,0:T(8,128)(2,1)} custom-call(bf16[3,16,5376]{2,1,0:T(8,128)(2,1)S(1)} %bitcast.9), custom_call_target="tpu_custom_call" | custom-call | flops 2000000000 | bytes 12582912 | tf_op jit(solution)/shard_map/pallas_call | solution.py:463
  19.3 0.0 copy-start.1
  19.3 2.0 %all-to-all-done.3.got_ref = bf16[32,8,896]{2,1,0:T(8,128)(2,1)S(1)} async-done(((bf16[32,8,896]{2,1,0:T(8,128)(2,1)}), bf16[32,8,896]{2,1,0:T(8,128)(2,1)S(1)}, u32[]{:S(2)}, u32[]{:S(2)}) %all-to-all-start.3) | async-done | bytes 458784 | tf_op jit(solution)/shard_map/all_to_all | solution.py:462
  21.3 10.0 %shard_map.79 = (s16[32,7,16,128]{3,2,1,0:T(8,128)(2,1)S(1)}, s16[32,7,16,128]{3,2,1,0:T(8,128)(2,1)S(1)}, s32[1,128]{1,0:T(1,128)S(1)}) custom-call(bf16[32,8,896]{2,1,0:T(8,128)(2,1)S(1)} %all-to-all-done.3.got_ref, bf16[36,896,384]{2,1,0:T(8,128)(2,1)} %shard_map.78.xs_hbm), custom_call_target="tpu_custom_call" | custom-call | tf_op jit(solution)/shard_map/pallas_call | solution.py:393
  31.3 0.0 copy-done.1
  31.3 23.8 %conditional.1 = ((f32[8,16,288]{2,1,0:T(8,128)S(1)}, f32[16,288]{1,0:T(8,128)S(1)})) conditional(s32[]{:T(128)} %bitcast.3, (s16[32,7,16,128]{3,2,1,0:T(8,128)(2,1)S(1)}, s32[8,128]{1,0:T(8,128)S(1)}, s32[8]{0:T(128)S(1)}) %tuple.21, (s16[32,7,16,128]{3,2,1,0:T(8,128)(2,1)S(1)}, s16[32,7,16,128]{3,2,1,0:T(8,128)(2,1)S(1)}, s32[8,128]{1,0:T(8,128)S(1)}, ...), branch_computations={%region_0.0_spmd, %region_1.0_spmd} | conditional | flops 917504 | bytes 7340040 | solution.py:487
  31.3 21.2 %all_to_all.17.back_ref = s16[32,7,16,128]{3,2,1,0:T(8,128)(2,1)S(1)} all-to-all(s16[32,7,16,128]{3,2,1,0:T(8,128)(2,1)S(1)} %get-tuple-element.16), channel_id=1, replica_groups=mesh['sta'=32,'tpl'=8] {'sta'}, dimensions={0} | all-to-all | bytes 1835008 | tf_op jit(solution)/shard_map/cond/branch_0_fun/all_to_all | solution.py:479
  52.6 2.6 %branch_0_fun.1 = (f32[8,16,288]{2,1,0:T(8,128)S(1)}, f32[16,288]{1,0:T(8,128)S(1)}) custom-call(s32[8,128]{1,0:T(8,128)S(1)} %get-tuple-element.14.list_ref, s32[8]{0:T(128)S(1)} %get-tuple-element.15.count_ref, s16[32,7,16,128]{3,2,1,0:T(8,128)(2,1)S(1)} %all_to_all.17.back_ref), custom_call_target="tpu_custom_call" | custom-call | tf_op jit(solution)/shard_map/cond/branch_0_fun/pallas_call | solution.py:417
  55.2 0.1 copy.10
  55.3 0.1 reshape_reshape.3
  55.4 2.7 %collective-permute-start.2 = (f32[36,128]{1,0:T(8,128)S(1)}, f32[36,128]{1,0:T(8,128)S(1)}, u32[]{:S(2)}, u32[]{:S(2)}) collective-permute-start(f32[36,128]{1,0:T(8,128)S(1)} %reshape_reshape.3), channel_id=1, source_target_pairs={{0,3},{1,2},{2,1},{3,0},{4,7},{5,6},{6,5},{7,4},{8,11},{9,10},{10,... | collective-permute-start | bytes 55304 | tf_op jit(solution)/shard_map/ppermute | solution.py:498
  58.1 0.9 %collective-permute-start.1 = (f32[36,128]{1,0:T(8,128)S(1)}, f32[36,128]{1,0:T(8,128)S(1)}, u32[]{:S(2)}, u32[]{:S(2)}) collective-permute-start(f32[36,128]{1,0:T(8,128)S(1)} %reshape_reshape.3), channel_id=1, source_target_pairs={{0,2},{1,3},{2,0},{3,1},{4,6},{5,7},{6,4},{7,5},{8,10},{9,11},{10,... | collective-permute-start | bytes 55304 | tf_op jit(solution)/shard_map/ppermute | solution.py:498
  59.0 1.4 %collective-permute-start = (f32[36,128]{1,0:T(8,128)S(1)}, f32[36,128]{1,0:T(8,128)S(1)}, u32[]{:S(2)}, u32[]{:S(2)}) collective-permute-start(f32[36,128]{1,0:T(8,128)S(1)} %reshape_reshape.3), channel_id=1, source_target_pairs={{0,1},{1,0},{2,3},{3,2},{4,5},{5,4},{6,7},{7,6},{8,9},{9,8},{10,11... | collective-permute-start | bytes 55304 | tf_op jit(solution)/shard_map/ppermute | solution.py:498
  60.3 0.0 collective-permute-done.2
  60.3 2.4 %collective-permute-done.1 = f32[36,128]{1,0:T(8,128)S(1)} collective-permute-done((f32[36,128]{1,0:T(8,128)S(1)}, f32[36,128]{1,0:T(8,128)S(1)}, u32[]{:S(2)}, u32[]{:S(2)}) %collective-permute-start.1) | collective-permute-done | bytes 18464 | tf_op jit(solution)/shard_map/ppermute | solution.py:498
  62.8 0.0 collective-permute-done
  62.8 4.4 %collective-permute-start.3 = (f32[36,128]{1,0:T(8,128)S(1)}, f32[36,128]{1,0:T(8,128)S(1)}, u32[]{:S(2)}, u32[]{:S(2)}) collective-permute-start(f32[36,128]{1,0:T(8,128)S(1)} %maximum_maximum_fusion.1), channel_id=1, source_target_pairs={{0,6},{1,7},{2,4},{3,5},{4,2},{5,3},{6,0},{7,1},{8,14},{9,15},{10,... | collective-permute-start | bytes 55304 | tf_op jit(solution)/shard_map/ppermute | solution.py:498
  67.2 1.8 %collective-permute-done.3 = f32[36,128]{1,0:T(8,128)S(1)} collective-permute-done((f32[36,128]{1,0:T(8,128)S(1)}, f32[36,128]{1,0:T(8,128)S(1)}, u32[]{:S(2)}, u32[]{:S(2)}) %collective-permute-start.3) | collective-permute-done | bytes 18464 | tf_op jit(solution)/shard_map/ppermute | solution.py:498
  69.0 0.0 collective-permute-start.4
  69.0 1.2 %collective-permute-done.4 = f32[36,128]{1,0:T(8,128)S(1)} collective-permute-done((f32[36,128]{1,0:T(8,128)S(1)}, f32[36,128]{1,0:T(8,128)S(1)}, u32[]{:S(2)}, u32[]{:S(2)}) %collective-permute-start.4) | collective-permute-done | bytes 18464 | tf_op jit(solution)/shard_map/ppermute | solution.py:498
  70.2 1.9 %collective-permute-start.7 = (f32[36,128]{1,0:T(8,128)S(1)}, f32[36,128]{1,0:T(8,128)S(1)}, u32[]{:S(2)}, u32[]{:S(2)}) collective-permute-start(f32[36,128]{1,0:T(8,128)S(1)} %max.37), channel_id=1, source_target_pairs={{0,32},{8,40},{16,48},{24,56},{32,0},{40,8},{48,16},{56,24},{64,96... | collective-permute-start | bytes 55304 | tf_op jit(solution)/shard_map/ppermute | solution.py:498
  72.1 1.5 %collective-permute-start.6 = (f32[36,128]{1,0:T(8,128)S(1)}, f32[36,128]{1,0:T(8,128)S(1)}, u32[]{:S(2)}, u32[]{:S(2)}) collective-permute-start(f32[36,128]{1,0:T(8,128)S(1)} %max.37), channel_id=1, source_target_pairs={{0,48},{8,56},{16,32},{24,40},{32,16},{40,24},{48,0},{56,8},{64,11... | collective-permute-start | bytes 55304 | tf_op jit(solution)/shard_map/ppermute | solution.py:498
  73.6 0.1 collective-permute-start.5
  73.7 1.8 %collective-permute-done.7 = f32[36,128]{1,0:T(8,128)S(1)} collective-permute-done((f32[36,128]{1,0:T(8,128)S(1)}, f32[36,128]{1,0:T(8,128)S(1)}, u32[]{:S(2)}, u32[]{:S(2)}) %collective-permute-start.7) | collective-permute-done | bytes 18464 | tf_op jit(solution)/shard_map/ppermute | solution.py:498
  75.5 1.6 %collective-permute-done.6 = f32[36,128]{1,0:T(8,128)S(1)} collective-permute-done((f32[36,128]{1,0:T(8,128)S(1)}, f32[36,128]{1,0:T(8,128)S(1)}, u32[]{:S(2)}, u32[]{:S(2)}) %collective-permute-start.6) | collective-permute-done | bytes 18464 | tf_op jit(solution)/shard_map/ppermute | solution.py:498
  77.1 0.3 collective-permute-done.5
  77.4 1.4 %collective-permute-start.10 = (f32[36,128]{1,0:T(8,128)S(1)}, f32[36,128]{1,0:T(8,128)S(1)}, u32[]{:S(2)}, u32[]{:S(2)}) collective-permute-start(f32[36,128]{1,0:T(8,128)S(1)} %maximum_maximum_fusion), channel_id=1, source_target_pairs={{0,128},{8,136},{16,144},{24,152},{32,160},{40,168},{48,176},{56,1... | collective-permute-start | bytes 55304 | tf_op jit(solution)/shard_map/ppermute | solution.py:498
  78.7 1.7 %collective-permute-start.9 = (f32[36,128]{1,0:T(8,128)S(1)}, f32[36,128]{1,0:T(8,128)S(1)}, u32[]{:S(2)}, u32[]{:S(2)}) collective-permute-start(f32[36,128]{1,0:T(8,128)S(1)} %maximum_maximum_fusion), channel_id=1, source_target_pairs={{0,192},{8,200},{16,208},{24,216},{32,224},{40,232},{48,240},{56,2... | collective-permute-start | bytes 55304 | tf_op jit(solution)/shard_map/ppermute | solution.py:498
  80.4 0.5 collective-permute-start.8
  81.0 0.4 copy.9
  81.3 1.4 %reshape.18 = f32[8,4608]{1,0:T(8,128)} reshape(f32[8,288,16]{2,1,0:T(8,128)S(1)} %copy.9) | data formatting | bytes 294912 | tf_op jit(solution)/shard_map/reshape | solution.py:488
  82.7 0.1 collective-permute-done.10
  82.8 1.0 %collective-permute-done.9 = f32[36,128]{1,0:T(8,128)S(1)} collective-permute-done((f32[36,128]{1,0:T(8,128)S(1)}, f32[36,128]{1,0:T(8,128)S(1)}, u32[]{:S(2)}, u32[]{:S(2)}) %collective-permute-start.9) | collective-permute-done | bytes 18464 | tf_op jit(solution)/shard_map/ppermute | solution.py:498
  83.7 0.5 collective-permute-done.8
  84.2 0.6 maximum_bitcast_fusion
  (4 shorter events, 0.0 us)
Async XLA Ops:
  3.4 17.9 %all-to-all-start.3 = ((bf16[32,8,896]{2,1,0:T(8,128)(2,1)}), bf16[32,8,896]{2,1,0:T(8,128)(2,1)S(1)}, u32[]{:S(2)}, u32[]{:S(2)}) async-start(bf16[32,8,896]{2,1,0:T(8,128)(2,1)} %get-tuple-element.30), calls=%async_computation.3 | async-start | bytes 917504 | tf_op jit(solution)/shard_map/all_to_all | solution.py:462
  10.8 1.0 %copy-start = (bf16[16,3,5376]{2,0,1:T(8,128)(2,1)S(1)}, bf16[16,3,5376]{2,0,1:T(8,128)(2,1)}, u32[]{:S(2)}) copy-start(bf16[16,3,5376]{2,0,1:T(8,128)(2,1)} %param.8) | copy-start | bytes 1548292
  19.3 12.0 %copy-start.1 = (s32[8]{0:T(128)S(1)}, s32[8]{0:T(128)}, u32[]{:S(2)}) copy-start(s32[8]{0:T(128)} %counts_hbm.1) | copy-start | bytes 100
  55.4 5.0 %collective-permute-start.2 = (f32[36,128]{1,0:T(8,128)S(1)}, f32[36,128]{1,0:T(8,128)S(1)}, u32[]{:S(2)}, u32[]{:S(2)}) collective-permute-start(f32[36,128]{1,0:T(8,128)S(1)} %reshape_reshape.3), channel_id=1, source_target_pairs={{0,3},{1,2},{2,1},{3,0},{4,7},{5,6},{6,5},{7,4},{8,11},{9,10},{10,... | collective-permute-start | bytes 55304 | tf_op jit(solution)/shard_map/ppermute | solution.py:498
  58.1 4.7 %collective-permute-start.1 = (f32[36,128]{1,0:T(8,128)S(1)}, f32[36,128]{1,0:T(8,128)S(1)}, u32[]{:S(2)}, u32[]{:S(2)}) collective-permute-start(f32[36,128]{1,0:T(8,128)S(1)} %reshape_reshape.3), channel_id=1, source_target_pairs={{0,2},{1,3},{2,0},{3,1},{4,6},{5,7},{6,4},{7,5},{8,10},{9,11},{10,... | collective-permute-start | bytes 55304 | tf_op jit(solution)/shard_map/ppermute | solution.py:498
  59.0 3.8 %collective-permute-start = (f32[36,128]{1,0:T(8,128)S(1)}, f32[36,128]{1,0:T(8,128)S(1)}, u32[]{:S(2)}, u32[]{:S(2)}) collective-permute-start(f32[36,128]{1,0:T(8,128)S(1)} %reshape_reshape.3), channel_id=1, source_target_pairs={{0,1},{1,0},{2,3},{3,2},{4,5},{5,4},{6,7},{7,6},{8,9},{9,8},{10,11... | collective-permute-start | bytes 55304 | tf_op jit(solution)/shard_map/ppermute | solution.py:498
  62.8 6.2 %collective-permute-start.3 = (f32[36,128]{1,0:T(8,128)S(1)}, f32[36,128]{1,0:T(8,128)S(1)}, u32[]{:S(2)}, u32[]{:S(2)}) collective-permute-start(f32[36,128]{1,0:T(8,128)S(1)} %maximum_maximum_fusion.1), channel_id=1, source_target_pairs={{0,6},{1,7},{2,4},{3,5},{4,2},{5,3},{6,0},{7,1},{8,14},{9,15},{10,... | collective-permute-start | bytes 55304 | tf_op jit(solution)/shard_map/ppermute | solution.py:498
  69.0 1.2 %collective-permute-start.4 = (f32[36,128]{1,0:T(8,128)S(1)}, f32[36,128]{1,0:T(8,128)S(1)}, u32[]{:S(2)}, u32[]{:S(2)}) collective-permute-start(f32[36,128]{1,0:T(8,128)S(1)} %max.36), channel_id=1, source_target_pairs={{0,8},{8,0},{16,24},{24,16},{32,40},{40,32},{48,56},{56,48},{64,72... | collective-permute-start | bytes 55304 | tf_op jit(solution)/shard_map/ppermute | solution.py:498
  70.2 5.3 %collective-permute-start.7 = (f32[36,128]{1,0:T(8,128)S(1)}, f32[36,128]{1,0:T(8,128)S(1)}, u32[]{:S(2)}, u32[]{:S(2)}) collective-permute-start(f32[36,128]{1,0:T(8,128)S(1)} %max.37), channel_id=1, source_target_pairs={{0,32},{8,40},{16,48},{24,56},{32,0},{40,8},{48,16},{56,24},{64,96... | collective-permute-start | bytes 55304 | tf_op jit(solution)/shard_map/ppermute | solution.py:498
  72.1 5.0 %collective-permute-start.6 = (f32[36,128]{1,0:T(8,128)S(1)}, f32[36,128]{1,0:T(8,128)S(1)}, u32[]{:S(2)}, u32[]{:S(2)}) collective-permute-start(f32[36,128]{1,0:T(8,128)S(1)} %max.37), channel_id=1, source_target_pairs={{0,48},{8,56},{16,32},{24,40},{32,16},{40,24},{48,0},{56,8},{64,11... | collective-permute-start | bytes 55304 | tf_op jit(solution)/shard_map/ppermute | solution.py:498
  73.6 3.8 %collective-permute-start.5 = (f32[36,128]{1,0:T(8,128)S(1)}, f32[36,128]{1,0:T(8,128)S(1)}, u32[]{:S(2)}, u32[]{:S(2)}) collective-permute-start(f32[36,128]{1,0:T(8,128)S(1)} %max.37), channel_id=1, source_target_pairs={{0,16},{8,24},{16,0},{24,8},{32,48},{40,56},{48,32},{56,40},{64,80... | collective-permute-start | bytes 55304 | tf_op jit(solution)/shard_map/ppermute | solution.py:498
  77.4 5.4 %collective-permute-start.10 = (f32[36,128]{1,0:T(8,128)S(1)}, f32[36,128]{1,0:T(8,128)S(1)}, u32[]{:S(2)}, u32[]{:S(2)}) collective-permute-start(f32[36,128]{1,0:T(8,128)S(1)} %maximum_maximum_fusion), channel_id=1, source_target_pairs={{0,128},{8,136},{16,144},{24,152},{32,160},{40,168},{48,176},{56,1... | collective-permute-start | bytes 55304 | tf_op jit(solution)/shard_map/ppermute | solution.py:498
  78.7 5.0 %collective-permute-start.9 = (f32[36,128]{1,0:T(8,128)S(1)}, f32[36,128]{1,0:T(8,128)S(1)}, u32[]{:S(2)}, u32[]{:S(2)}) collective-permute-start(f32[36,128]{1,0:T(8,128)S(1)} %maximum_maximum_fusion), channel_id=1, source_target_pairs={{0,192},{8,200},{16,208},{24,216},{32,224},{40,232},{48,240},{56,2... | collective-permute-start | bytes 55304 | tf_op jit(solution)/shard_map/ppermute | solution.py:498
  80.4 3.8 %collective-permute-start.8 = (f32[36,128]{1,0:T(8,128)S(1)}, f32[36,128]{1,0:T(8,128)S(1)}, u32[]{:S(2)}, u32[]{:S(2)}) collective-permute-start(f32[36,128]{1,0:T(8,128)S(1)} %maximum_maximum_fusion), channel_id=1, source_target_pairs={{0,64},{8,72},{16,80},{24,88},{32,96},{40,104},{48,112},{56,120},{... | collective-permute-start | bytes 55304 | tf_op jit(solution)/shard_map/ppermute | solution.py:498

commit v6 on v5

--- a/solution.py
+++ b/solution.py
@@ -158,7 +158,7 @@
             squares = squares + x * x
             for r in range(REACH + 1):
                 moved = x if r == 0 else pltpu.roll(x, WIDE - r, 1)
-                at = c * L + r * PHASES if r < REACH else 3 * L + c * PHASES
+                at = (c * (REACH + 1) + r) * PHASES
                 xs_ref[s, at : at + PHASES, :] = moved.astype(jnp.bfloat16)
         up = squares
         down = jnp.where(sub >= 1, pltpu.roll(squares, 1, 0), 0.0)
@@ -253,24 +253,24 @@
 
     sub = iota((PHASES, BLOCK), 0)
     lane = iota((PHASES, BLOCK), 1)
-    late = lane >= sub
+    own = [lane >= PHASES * c + sub for c in range(3)]
 
     def toeplitz(slot):
         bands = []
         for k in range(CHUNK):
-            tail = jnp.zeros((PHASES, BLOCK), jnp.float32)
             band = []
+            before = None
             for c in range(3):
                 turned = []
                 for h in range(2):
                     at = c * L + h * BLOCK
                     row = jnp.broadcast_to(slot[k : k + 1, at : at + BLOCK], (PHASES, BLOCK))
-                    turned.append(pltpu.roll(row, 0, 1, stride=1, stride_axis=0))
-                band.append(jnp.where(late, turned[0], 0.0).astype(jnp.bfloat16))
-                band.append(jnp.where(late, turned[1], turned[0]).astype(jnp.bfloat16))
-                rest = jnp.where(late, 0.0, turned[1])
-                tail = tail + (rest if c == 0 else pltpu.roll(rest, c * PHASES, 1))
-            band.append(tail.astype(jnp.bfloat16))
+                    turned.append(pltpu.roll(row, c * PHASES, 1, stride=1, stride_axis=0))
+                rest = 0.0 if c == 0 else jnp.where(own[c - 1], 0.0, before)
+                band.append(jnp.where(own[c], turned[0], rest).astype(jnp.bfloat16))
+                band.append(jnp.where(own[c], turned[1], turned[0]).astype(jnp.bfloat16))
+                before = turned[1]
+            band.append(jnp.where(own[2], 0.0, before).astype(jnp.bfloat16))
             bands.append(jnp.concatenate(band, axis=1))
         return jnp.concatenate(bands, axis=0)
 
@@ -295,14 +295,16 @@
             held_ref[target, :, BLOCK : 2 * BLOCK] += jnp.where(stay, turned[1], turned[2])
             held_ref[target, :, 2 * BLOCK :] += turned[2]
 
-    def two_chunks(i, ready):
-        last = jnp.maximum(table_ref[0, 16 * i], table_ref[0, 16 * i + 8]) + 1
-        lax.fori_loop(ready, last, arrive, 0)
-        chunk(2 * i)
-        chunk(2 * i + 1)
-        return jnp.maximum(ready, last)
-
-    ready = lax.fori_loop(0, (table_ref[4, 0] + 1) // 2, two_chunks, 0)
+    def three_chunks(i, ready):
+        last = table_ref[0, 3 * CHUNK * i]
+        for k in range(1, 3):
+            last = jnp.maximum(last, table_ref[0, (3 * i + k) * CHUNK])
+        lax.fori_loop(ready, last + 1, arrive, 0)
+        for k in range(3):
+            chunk(3 * i + k)
+        return jnp.maximum(ready, last + 1)
+
+    ready = lax.fori_loop(0, (table_ref[4, 0] + 2) // 3, three_chunks, 0)
     lax.fori_loop(ready, stations, arrive, 0)
     end = KEPT - 2 * BLOCK
 
@@ -385,6 +387,23 @@
 
 def params(mib):
     return pltpu.CompilerParams(vmem_limit_bytes=mib * 2**20)
+
+
+def prep_call(waveforms):
+    stations, _, samples = waveforms.shape
+    return pl.pallas_call(
+        prep_kernel,
+        out_shape=jax.ShapeDtypeStruct((2 * stations + 4, DEPTH, WIDE), jnp.bfloat16),
+        in_specs=[VMEM],
+        out_specs=ANY,
+        scratch_shapes=[
+            pltpu.VMEM((stations, DEPTH, WIDE), jnp.bfloat16),
+            pltpu.VMEM((3, stations, samples), jnp.float32),
+            pltpu.SemaphoreType.DMA((stations // 2,)),
+        ],
+        compiler_params=params(40),
+        cost_estimate=pl.CostEstimate(flops=2 * 10**9, bytes_accessed=12 * 2**20, transcendentals=0),
+    )(waveforms.transpose(1, 0, 2))
 
 
 def correlate_call(got, xs, stations):
@@ -460,19 +479,7 @@
         templates.transpose(1, 0, 2),
     )
     got = lax.all_to_all(send, "sta", split_axis=0, concat_axis=0, tiled=True)
-    xs = pl.pallas_call(
-        prep_kernel,
-        out_shape=jax.ShapeDtypeStruct((2 * stations + 4, DEPTH, WIDE), jnp.bfloat16),
-        in_specs=[VMEM],
-        out_specs=ANY,
-        scratch_shapes=[
-            pltpu.VMEM((stations, DEPTH, WIDE), jnp.bfloat16),
-            pltpu.VMEM((3, stations, samples), jnp.float32),
-            pltpu.SemaphoreType.DMA((stations // 2,)),
-        ],
-        compiler_params=params(40),
-        cost_estimate=pl.CostEstimate(flops=2 * 10**9, bytes_accessed=12 * 2**20, transcendentals=0),
-    )(waveforms.transpose(1, 0, 2))
+    xs = prep_call(waveforms)
     traces, more, flag = correlate_call(got, xs, stations)
 
     def home(x):
@@ -485,20 +492,21 @@
         return add_call(listed, station_counts, jnp.concatenate([home(traces), home(more)]))
 
     stack, best = lax.cond(flag[0, 0] > 0, two_exchanges, one_exchange, traces, more)
-    stack = stack.transpose(0, 2, 1).reshape(tpl_dev, PHASES * KEPT)
-    best = best.T.reshape(PHASES * KEPT)
-    network = best_of_all(best.reshape(-1, BLOCK)).reshape(PHASES * KEPT)
-    return (stack, network)
-
-
-def best_of_all(best):
-    rounds = (("tpl", (1, 2, 3)), ("tpl", (6,)), ("sta", (1,)), ("sta", (2, 6, 4)), ("sta", (8, 24, 16)))
-    for axis, steps in rounds:
+    best = best.T.reshape(-1, BLOCK)
+    for n, (axis, steps) in enumerate(ROUNDS):
         size = lax.axis_size(axis)
         others = [lax.ppermute(best, axis, [(i, i ^ step) for i in range(size)]) for step in steps]
         for other in others:
             best = jnp.maximum(best, other)
-    return best
+        if n == 0:
+            best, stack = lax.optimization_barrier((best, stack))
+            stack = stack.transpose(0, 2, 1).reshape(tpl_dev, PHASES * KEPT)
+        if n == 1:
+            best, stack = lax.optimization_barrier((best, stack))
+    return (stack, best.reshape(PHASES * KEPT))
+
+
+ROUNDS = (("tpl", (1, 2, 3)), ("tpl", (6,)), ("sta", (1,)), ("sta", (2, 6, 4)), ("sta", (8, 24, 16)))
 
 
 def solution(mesh):

time: 85.6 us -> 84.7 us (0.989)
  Pallas kernels: 22.8 us -> 21.7 us
    pallas_call x1, Pallas kernels: 9.96 us -> 8.85 us  [correlate_call(): pl.pallas_call(correlate_kernel, out_shape=(jax.ShapeDtypeStruct((width,...]
where the time goes in v6:
time: 84.7 us; the launch traced here: 83.8 us
  starting transfers between devices  24.6 us (29%)
  Pallas kernels  21.7 us (26%)
  blocking collectives  20.4 us (24%)
  waiting for transfers between devices  12.6 us (15%)
  local copies, waits for them, and re-layouts  2.97 us (4%)
    all_to_all x1, blocking collectives, home(): return lax.all_to_all(x, 'sta', split_axis=0, concat_axis=0, tiled=True)  20.4 us
    ppermute x11, starting transfers between devices, body(): lax.ppermute(best, axis, [(i, i ^ step) for i in range(size)])  17.3 us
    ppermute x11, waiting for transfers between devices, body(): lax.ppermute(best, axis, [(i, i ^ step) for i in range(size)])  10.6 us
    pallas_call x1, Pallas kernels, correlate_call(): pl.pallas_call(correlate_kernel, out_shape=(jax.ShapeDtypeStruct((width,...  8.85 us
    pallas_call x1, Pallas kernels, prep_call(): pl.pallas_call(prep_kernel, out_shape=jax.ShapeDtypeStruct((2 * stations...  7.51 us
    all_to_all x1, starting transfers between devices, body(): got = lax.all_to_all(send, 'sta', split_axis=0, concat_axis=0, tiled=True)  7.33 us
    pallas_call x1, Pallas kernels, body(): pl.pallas_call(pack_kernel, out_shape=(jax.ShapeDtypeStruct((width, ROWS,...  2.79 us
    pallas_call x1, Pallas kernels, add_call(): pl.pallas_call(add_kernel, out_shape=(jax.ShapeDtypeStruct((tpl_dev, PHAS...  2.58 us
  transfers between devices with their start and end apart: 12, of which 10 were waited for; matrix products, arithmetic and copies ran while one was open for 2% of the time, Pallas kernels for 9%

profile of v6, /device:TPU:32, one launch (start us, length us, event | category | flops | bytes accessed | tf_op | source)
XLA Modules:
  0.0 83.8 jit_solution(8191866598311266315)
XLA Ops:
  0.6 2.8 %shard_map.77 = (bf16[32,8,896]{2,1,0:T(8,128)(2,1)}, s32[8,128]{1,0:T(8,128)S(1)}) custom-call(s32[8,20]{1,0:T(8,128)} %stations_hbm.1, s32[8,20]{1,0:T(8,128)} %moves_hbm.1, s32[8]{0:T(128)} %counts_hbm.1, s32[4,128]{1,0:T(4,128)} %bitcast.14, bf16[20,8,768]{2,1,0:T(8,128)(2,1)} %bitcast.11), custom_call_target="tpu_custom_call" | custom-call | tf_op jit(solution)/shard_map/pallas_call | solution.py:457
  3.4 7.3 %all-to-all-start.3 = ((bf16[32,8,896]{2,1,0:T(8,128)(2,1)}), bf16[32,8,896]{2,1,0:T(8,128)(2,1)S(1)}, u32[]{:S(2)}, u32[]{:S(2)}) async-start(bf16[32,8,896]{2,1,0:T(8,128)(2,1)} %get-tuple-element.34), calls=%async_computation.3 | async-start | bytes 917504 | tf_op jit(solution)/shard_map/all_to_all | solution.py:481
  10.8 0.0 copy-start
  10.8 1.0 %copy-done = bf16[16,3,5376]{2,0,1:T(8,128)(2,1)S(1)} copy-done((bf16[16,3,5376]{2,0,1:T(8,128)(2,1)S(1)}, bf16[16,3,5376]{2,0,1:T(8,128)(2,1)}, u32[]{:S(2)}) %copy-start) | copy-done | bytes 516120
  11.8 7.5 %shard_map.78.xs_hbm = bf16[36,896,384]{2,1,0:T(8,128)(2,1)} custom-call(bf16[3,16,5376]{2,1,0:T(8,128)(2,1)S(1)} %bitcast.9), custom_call_target="tpu_custom_call" | custom-call | flops 2000000000 | bytes 12582912 | tf_op jit(solution)/shard_map/pallas_call | solution.py:394
  19.3 0.0 copy-start.1
  19.3 2.0 %all-to-all-done.3.got_ref = bf16[32,8,896]{2,1,0:T(8,128)(2,1)S(1)} async-done(((bf16[32,8,896]{2,1,0:T(8,128)(2,1)}), bf16[32,8,896]{2,1,0:T(8,128)(2,1)S(1)}, u32[]{:S(2)}, u32[]{:S(2)}) %all-to-all-start.3) | async-done | bytes 458784 | tf_op jit(solution)/shard_map/all_to_all | solution.py:481
  21.3 8.8 %shard_map.79 = (s16[32,7,16,128]{3,2,1,0:T(8,128)(2,1)S(1)}, s16[32,7,16,128]{3,2,1,0:T(8,128)(2,1)S(1)}, s32[1,128]{1,0:T(1,128)S(1)}) custom-call(bf16[32,8,896]{2,1,0:T(8,128)(2,1)S(1)} %all-to-all-done.3.got_ref, bf16[36,896,384]{2,1,0:T(8,128)(2,1)} %shard_map.78.xs_hbm), custom_call_target="tpu_custom_call" | custom-call | tf_op jit(solution)/shard_map/pallas_call | solution.py:412
  30.2 0.0 copy-done.1
  30.2 23.0 %conditional.1 = ((f32[8,16,288]{2,1,0:T(8,128)S(1)}, f32[16,288]{1,0:T(8,128)S(1)})) conditional(s32[]{:T(128)} %bitcast.3, (s16[32,7,16,128]{3,2,1,0:T(8,128)(2,1)S(1)}, s32[8,128]{1,0:T(8,128)S(1)}, s32[8]{0:T(128)S(1)}) %tuple.25, (s16[32,7,16,128]{3,2,1,0:T(8,128)(2,1)S(1)}, s16[32,7,16,128]{3,2,1,0:T(8,128)(2,1)S(1)}, s32[8,128]{1,0:T(8,128)S(1)}, ...), branch_computations={%region_0.0_spmd, %region_1.0_spmd} | conditional | flops 917504 | bytes 7340040 | solution.py:494
  30.2 20.4 %all_to_all.17.back_ref = s16[32,7,16,128]{3,2,1,0:T(8,128)(2,1)S(1)} all-to-all(s16[32,7,16,128]{3,2,1,0:T(8,128)(2,1)S(1)} %get-tuple-element.16), channel_id=1, replica_groups=mesh['sta'=32,'tpl'=8] {'sta'}, dimensions={0} | all-to-all | bytes 1835008 | tf_op jit(solution)/shard_map/cond/branch_0_fun/all_to_all | solution.py:486
  50.7 2.6 %branch_0_fun.1 = (f32[8,16,288]{2,1,0:T(8,128)S(1)}, f32[16,288]{1,0:T(8,128)S(1)}) custom-call(s32[8,128]{1,0:T(8,128)S(1)} %get-tuple-element.14.list_ref, s32[8]{0:T(128)S(1)} %get-tuple-element.15.count_ref, s16[32,7,16,128]{3,2,1,0:T(8,128)(2,1)S(1)} %all_to_all.17.back_ref), custom_call_target="tpu_custom_call" | custom-call | tf_op jit(solution)/shard_map/cond/branch_0_fun/pallas_call | solution.py:436
  53.3 0.1 copy.9
  53.4 0.1 reshape.21
  53.5 1.9 %collective-permute-start.2 = (f32[36,128]{1,0:T(8,128)S(1)}, f32[36,128]{1,0:T(8,128)S(1)}, u32[]{:S(2)}, u32[]{:S(2)}) collective-permute-start(f32[36,128]{1,0:T(8,128)S(1)} %reshape.21), channel_id=1, source_target_pairs={{0,3},{1,2},{2,1},{3,0},{4,7},{5,6},{6,5},{7,4},{8,11},{9,10},{10,... | collective-permute-start | bytes 55304 | tf_op jit(solution)/shard_map/ppermute | solution.py:498
  55.4 1.6 %collective-permute-start.1 = (f32[36,128]{1,0:T(8,128)S(1)}, f32[36,128]{1,0:T(8,128)S(1)}, u32[]{:S(2)}, u32[]{:S(2)}) collective-permute-start(f32[36,128]{1,0:T(8,128)S(1)} %reshape.21), channel_id=1, source_target_pairs={{0,2},{1,3},{2,0},{3,1},{4,6},{5,7},{6,4},{7,5},{8,10},{9,11},{10,... | collective-permute-start | bytes 55304 | tf_op jit(solution)/shard_map/ppermute | solution.py:498
  57.0 1.4 %collective-permute-start = (f32[36,128]{1,0:T(8,128)S(1)}, f32[36,128]{1,0:T(8,128)S(1)}, u32[]{:S(2)}, u32[]{:S(2)}) collective-permute-start(f32[36,128]{1,0:T(8,128)S(1)} %reshape.21), channel_id=1, source_target_pairs={{0,1},{1,0},{2,3},{3,2},{4,5},{5,4},{6,7},{7,6},{8,9},{9,8},{10,11... | collective-permute-start | bytes 55304 | tf_op jit(solution)/shard_map/ppermute | solution.py:498
  58.4 0.0 collective-permute-done.2
  58.4 1.7 %collective-permute-done.1 = f32[36,128]{1,0:T(8,128)S(1)} collective-permute-done((f32[36,128]{1,0:T(8,128)S(1)}, f32[36,128]{1,0:T(8,128)S(1)}, u32[]{:S(2)}, u32[]{:S(2)}) %collective-permute-start.1) | collective-permute-done | bytes 18464 | tf_op jit(solution)/shard_map/ppermute | solution.py:498
  60.1 0.7 collective-permute-done
  60.8 5.3 %collective-permute-start.3 = (f32[36,128]{1,0:T(8,128)S(1)}, f32[36,128]{1,0:T(8,128)S(1)}, u32[]{:S(2)}, u32[]{:S(2)}) collective-permute-start(f32[36,128]{1,0:T(8,128)S(1)} %maximum_maximum_fusion.1), channel_id=1, source_target_pairs={{0,6},{1,7},{2,4},{3,5},{4,2},{5,3},{6,0},{7,1},{8,14},{9,15},{10,... | collective-permute-start | bytes 55304 | tf_op jit(solution)/shard_map/ppermute | solution.py:498
  66.1 0.4 copy.10
  66.4 1.4 %reshape.22 = f32[8,4608]{1,0:T(8,128)} reshape(f32[8,288,16]{2,1,0:T(8,128)S(1)} %copy.10) | data formatting | bytes 294912 | tf_op jit(solution)/shard_map/reshape | solution.py:503
  67.8 0.0 collective-permute-done.3
  67.8 0.1 collective-permute-start.4
  67.9 1.2 %collective-permute-done.4 = f32[36,128]{1,0:T(8,128)S(1)} collective-permute-done((f32[36,128]{1,0:T(8,128)S(1)}, f32[36,128]{1,0:T(8,128)S(1)}, u32[]{:S(2)}, u32[]{:S(2)}) %collective-permute-start.4) | collective-permute-done | bytes 18464 | tf_op jit(solution)/shard_map/ppermute | solution.py:498
  69.1 2.0 %collective-permute-start.7 = (f32[36,128]{1,0:T(8,128)S(1)}, f32[36,128]{1,0:T(8,128)S(1)}, u32[]{:S(2)}, u32[]{:S(2)}) collective-permute-start(f32[36,128]{1,0:T(8,128)S(1)} %max.37), channel_id=1, source_target_pairs={{0,32},{8,40},{16,48},{24,56},{32,0},{40,8},{48,16},{56,24},{64,96... | collective-permute-start | bytes 55304 | tf_op jit(solution)/shard_map/ppermute | solution.py:498
  71.1 1.6 %collective-permute-start.6 = (f32[36,128]{1,0:T(8,128)S(1)}, f32[36,128]{1,0:T(8,128)S(1)}, u32[]{:S(2)}, u32[]{:S(2)}) collective-permute-start(f32[36,128]{1,0:T(8,128)S(1)} %max.37), channel_id=1, source_target_pairs={{0,48},{8,56},{16,32},{24,40},{32,16},{40,24},{48,0},{56,8},{64,11... | collective-permute-start | bytes 55304 | tf_op jit(solution)/shard_map/ppermute | solution.py:498
  72.6 0.0 collective-permute-start.5
  72.6 1.8 %collective-permute-done.7 = f32[36,128]{1,0:T(8,128)S(1)} collective-permute-done((f32[36,128]{1,0:T(8,128)S(1)}, f32[36,128]{1,0:T(8,128)S(1)}, u32[]{:S(2)}, u32[]{:S(2)}) %collective-permute-start.7) | collective-permute-done | bytes 18464 | tf_op jit(solution)/shard_map/ppermute | solution.py:498
  74.4 1.7 %collective-permute-done.6 = f32[36,128]{1,0:T(8,128)S(1)} collective-permute-done((f32[36,128]{1,0:T(8,128)S(1)}, f32[36,128]{1,0:T(8,128)S(1)}, u32[]{:S(2)}, u32[]{:S(2)}) %collective-permute-start.6) | collective-permute-done | bytes 18464 | tf_op jit(solution)/shard_map/ppermute | solution.py:498
  76.0 0.3 collective-permute-done.5
  76.4 1.2 %collective-permute-start.10 = (f32[36,128]{1,0:T(8,128)S(1)}, f32[36,128]{1,0:T(8,128)S(1)}, u32[]{:S(2)}, u32[]{:S(2)}) collective-permute-start(f32[36,128]{1,0:T(8,128)S(1)} %maximum_maximum_fusion), channel_id=1, source_target_pairs={{0,128},{8,136},{16,144},{24,152},{32,160},{40,168},{48,176},{56,1... | collective-permute-start | bytes 55304 | tf_op jit(solution)/shard_map/ppermute | solution.py:498
  77.6 1.8 %collective-permute-start.9 = (f32[36,128]{1,0:T(8,128)S(1)}, f32[36,128]{1,0:T(8,128)S(1)}, u32[]{:S(2)}, u32[]{:S(2)}) collective-permute-start(f32[36,128]{1,0:T(8,128)S(1)} %maximum_maximum_fusion), channel_id=1, source_target_pairs={{0,192},{8,200},{16,208},{24,216},{32,224},{40,232},{48,240},{56,2... | collective-permute-start | bytes 55304 | tf_op jit(solution)/shard_map/ppermute | solution.py:498
  79.4 0.6 collective-permute-start.8
  80.0 1.8 %collective-permute-done.10 = f32[36,128]{1,0:T(8,128)S(1)} collective-permute-done((f32[36,128]{1,0:T(8,128)S(1)}, f32[36,128]{1,0:T(8,128)S(1)}, u32[]{:S(2)}, u32[]{:S(2)}) %collective-permute-start.10) | collective-permute-done | bytes 18464 | tf_op jit(solution)/shard_map/ppermute | solution.py:498
  81.8 0.8 collective-permute-done.9
  82.6 0.6 collective-permute-done.8
  83.2 0.6 maximum_bitcast_fusion
  (4 shorter events, 0.0 us)
Async XLA Ops:
  3.4 17.9 %all-to-all-start.3 = ((bf16[32,8,896]{2,1,0:T(8,128)(2,1)}), bf16[32,8,896]{2,1,0:T(8,128)(2,1)S(1)}, u32[]{:S(2)}, u32[]{:S(2)}) async-start(bf16[32,8,896]{2,1,0:T(8,128)(2,1)} %get-tuple-element.34), calls=%async_computation.3 | async-start | bytes 917504 | tf_op jit(solution)/shard_map/all_to_all | solution.py:481
  10.8 1.0 %copy-start = (bf16[16,3,5376]{2,0,1:T(8,128)(2,1)S(1)}, bf16[16,3,5376]{2,0,1:T(8,128)(2,1)}, u32[]{:S(2)}) copy-start(bf16[16,3,5376]{2,0,1:T(8,128)(2,1)} %param.8) | copy-start | bytes 1548292
  19.3 10.9 %copy-start.1 = (s32[8]{0:T(128)S(1)}, s32[8]{0:T(128)}, u32[]{:S(2)}) copy-start(s32[8]{0:T(128)} %counts_hbm.1) | copy-start | bytes 100
  53.5 4.9 %collective-permute-start.2 = (f32[36,128]{1,0:T(8,128)S(1)}, f32[36,128]{1,0:T(8,128)S(1)}, u32[]{:S(2)}, u32[]{:S(2)}) collective-permute-start(f32[36,128]{1,0:T(8,128)S(1)} %reshape.21), channel_id=1, source_target_pairs={{0,3},{1,2},{2,1},{3,0},{4,7},{5,6},{6,5},{7,4},{8,11},{9,10},{10,... | collective-permute-start | bytes 55304 | tf_op jit(solution)/shard_map/ppermute | solution.py:498
  55.4 4.7 %collective-permute-start.1 = (f32[36,128]{1,0:T(8,128)S(1)}, f32[36,128]{1,0:T(8,128)S(1)}, u32[]{:S(2)}, u32[]{:S(2)}) collective-permute-start(f32[36,128]{1,0:T(8,128)S(1)} %reshape.21), channel_id=1, source_target_pairs={{0,2},{1,3},{2,0},{3,1},{4,6},{5,7},{6,4},{7,5},{8,10},{9,11},{10,... | collective-permute-start | bytes 55304 | tf_op jit(solution)/shard_map/ppermute | solution.py:498
  57.0 3.8 %collective-permute-start = (f32[36,128]{1,0:T(8,128)S(1)}, f32[36,128]{1,0:T(8,128)S(1)}, u32[]{:S(2)}, u32[]{:S(2)}) collective-permute-start(f32[36,128]{1,0:T(8,128)S(1)} %reshape.21), channel_id=1, source_target_pairs={{0,1},{1,0},{2,3},{3,2},{4,5},{5,4},{6,7},{7,6},{8,9},{9,8},{10,11... | collective-permute-start | bytes 55304 | tf_op jit(solution)/shard_map/ppermute | solution.py:498
  60.8 7.0 %collective-permute-start.3 = (f32[36,128]{1,0:T(8,128)S(1)}, f32[36,128]{1,0:T(8,128)S(1)}, u32[]{:S(2)}, u32[]{:S(2)}) collective-permute-start(f32[36,128]{1,0:T(8,128)S(1)} %maximum_maximum_fusion.1), channel_id=1, source_target_pairs={{0,6},{1,7},{2,4},{3,5},{4,2},{5,3},{6,0},{7,1},{8,14},{9,15},{10,... | collective-permute-start | bytes 55304 | tf_op jit(solution)/shard_map/ppermute | solution.py:498
  67.8 1.2 %collective-permute-start.4 = (f32[36,128]{1,0:T(8,128)S(1)}, f32[36,128]{1,0:T(8,128)S(1)}, u32[]{:S(2)}, u32[]{:S(2)}) collective-permute-start(f32[36,128]{1,0:T(8,128)S(1)} %max.36), channel_id=1, source_target_pairs={{0,8},{8,0},{16,24},{24,16},{32,40},{40,32},{48,56},{56,48},{64,72... | collective-permute-start | bytes 55304 | tf_op jit(solution)/shard_map/ppermute | solution.py:498
  69.1 5.3 %collective-permute-start.7 = (f32[36,128]{1,0:T(8,128)S(1)}, f32[36,128]{1,0:T(8,128)S(1)}, u32[]{:S(2)}, u32[]{:S(2)}) collective-permute-start(f32[36,128]{1,0:T(8,128)S(1)} %max.37), channel_id=1, source_target_pairs={{0,32},{8,40},{16,48},{24,56},{32,0},{40,8},{48,16},{56,24},{64,96... | collective-permute-start | bytes 55304 | tf_op jit(solution)/shard_map/ppermute | solution.py:498
  71.1 5.0 %collective-permute-start.6 = (f32[36,128]{1,0:T(8,128)S(1)}, f32[36,128]{1,0:T(8,128)S(1)}, u32[]{:S(2)}, u32[]{:S(2)}) collective-permute-start(f32[36,128]{1,0:T(8,128)S(1)} %max.37), channel_id=1, source_target_pairs={{0,48},{8,56},{16,32},{24,40},{32,16},{40,24},{48,0},{56,8},{64,11... | collective-permute-start | bytes 55304 | tf_op jit(solution)/shard_map/ppermute | solution.py:498
  72.6 3.8 %collective-permute-start.5 = (f32[36,128]{1,0:T(8,128)S(1)}, f32[36,128]{1,0:T(8,128)S(1)}, u32[]{:S(2)}, u32[]{:S(2)}) collective-permute-start(f32[36,128]{1,0:T(8,128)S(1)} %max.37), channel_id=1, source_target_pairs={{0,16},{8,24},{16,0},{24,8},{32,48},{40,56},{48,32},{56,40},{64,80... | collective-permute-start | bytes 55304 | tf_op jit(solution)/shard_map/ppermute | solution.py:498
  76.4 5.4 %collective-permute-start.10 = (f32[36,128]{1,0:T(8,128)S(1)}, f32[36,128]{1,0:T(8,128)S(1)}, u32[]{:S(2)}, u32[]{:S(2)}) collective-permute-start(f32[36,128]{1,0:T(8,128)S(1)} %maximum_maximum_fusion), channel_id=1, source_target_pairs={{0,128},{8,136},{16,144},{24,152},{32,160},{40,168},{48,176},{56,1... | collective-permute-start | bytes 55304 | tf_op jit(solution)/shard_map/ppermute | solution.py:498
  77.6 5.0 %collective-permute-start.9 = (f32[36,128]{1,0:T(8,128)S(1)}, f32[36,128]{1,0:T(8,128)S(1)}, u32[]{:S(2)}, u32[]{:S(2)}) collective-permute-start(f32[36,128]{1,0:T(8,128)S(1)} %maximum_maximum_fusion), channel_id=1, source_target_pairs={{0,192},{8,200},{16,208},{24,216},{32,224},{40,232},{48,240},{56,2... | collective-permute-start | bytes 55304 | tf_op jit(solution)/shard_map/ppermute | solution.py:498
  79.4 3.8 %collective-permute-start.8 = (f32[36,128]{1,0:T(8,128)S(1)}, f32[36,128]{1,0:T(8,128)S(1)}, u32[]{:S(2)}, u32[]{:S(2)}) collective-permute-start(f32[36,128]{1,0:T(8,128)S(1)} %maximum_maximum_fusion), channel_id=1, source_target_pairs={{0,64},{8,72},{16,80},{24,88},{32,96},{40,104},{48,112},{56,120},{... | collective-permute-start | bytes 55304 | tf_op jit(solution)/shard_map/ppermute | solution.py:498

commit v7 on v6

--- a/solution.py
+++ b/solution.py
@@ -156,10 +156,10 @@
         for c in range(3):
             x = phases[c * PHASES : (c + 1) * PHASES]
             squares = squares + x * x
+            short = x.astype(jnp.bfloat16)
             for r in range(REACH + 1):
-                moved = x if r == 0 else pltpu.roll(x, WIDE - r, 1)
                 at = (c * (REACH + 1) + r) * PHASES
-                xs_ref[s, at : at + PHASES, :] = moved.astype(jnp.bfloat16)
+                xs_ref[s, at : at + PHASES, :] = short if r == 0 else pltpu.roll(short, WIDE - r, 1)
         up = squares
         down = jnp.where(sub >= 1, pltpu.roll(squares, 1, 0), 0.0)
         for step in (1, 2, 4, 8):
@@ -343,10 +343,10 @@
     def wide(x):
         return x.astype(jnp.int32).astype(jnp.float32)
 
-    @pl.loop(0, back_ref.shape[0] // 4)
+    @pl.loop(0, back_ref.shape[0] // 8)
     def _(i):
-        for part in range(4):
-            o = 4 * i + part
+        for part in range(8):
+            o = 8 * i + part
             last = wide(back_ref[o, 2 * HALF])
             scales = jnp.exp2(last * (1.0 / FINE)) * (1.0 / FULL)
             for r in range(HALF):

time: 84.7 us -> 84 us (level)
  Pallas kernels: 21.7 us -> 20 us
  blocking collectives: 20.4 us -> 21.7 us
    all_to_all x1, blocking collectives: 20.4 us -> 21.7 us  [home(): return lax.all_to_all(x, 'sta', split_axis=0, concat_axis=0, tiled=True)]
  transfers between devices with their start and end apart: 12 -> 12, of which waited for: 10 -> 9; matrix products, arithmetic and copies ran while one was open for 2% -> 2% of each run, Pallas kernels for 9% -> 8%
where the time goes in v7:
time: 84 us; the launch traced here: 83.1 us
  starting transfers between devices  23.8 us (28%)
  blocking collectives  21.7 us (26%)
  Pallas kernels  20 us (24%)
  waiting for transfers between devices  13.2 us (16%)
  local copies, waits for them, and re-layouts  2.97 us (4%)
    all_to_all x1, blocking collectives, home(): return lax.all_to_all(x, 'sta', split_axis=0, concat_axis=0, tiled=True)  21.7 us
    ppermute x11, starting transfers between devices, body(): lax.ppermute(best, axis, [(i, i ^ step) for i in range(size)])  16.5 us
    ppermute x11, waiting for transfers between devices, body(): lax.ppermute(best, axis, [(i, i ^ step) for i in range(size)])  10.7 us
    pallas_call x1, Pallas kernels, correlate_call(): pl.pallas_call(correlate_kernel, out_shape=(jax.ShapeDtypeStruct((width,...  8.09 us
    all_to_all x1, starting transfers between devices, body(): got = lax.all_to_all(send, 'sta', split_axis=0, concat_axis=0, tiled=True)  7.33 us
    pallas_call x1, Pallas kernels, prep_call(): pl.pallas_call(prep_kernel, out_shape=jax.ShapeDtypeStruct((2 * stations...  6.97 us
    pallas_call x1, Pallas kernels, body(): pl.pallas_call(pack_kernel, out_shape=(jax.ShapeDtypeStruct((width, ROWS,...  2.79 us
    all_to_all x1, waiting for transfers between devices, body(): got = lax.all_to_all(send, 'sta', split_axis=0, concat_axis=0, tiled=True)  2.52 us
  transfers between devices with their start and end apart: 12, of which 9 were waited for; matrix products, arithmetic and copies ran while one was open for 2% of the time, Pallas kernels for 8%

profile of v7, /device:TPU:32, one launch (start us, length us, event | category | flops | bytes accessed | tf_op | source)
XLA Modules:
  0.0 83.1 jit_solution(10977362343173084243)
XLA Ops:
  0.6 2.8 %shard_map.77 = (bf16[32,8,896]{2,1,0:T(8,128)(2,1)}, s32[8,128]{1,0:T(8,128)S(1)}) custom-call(s32[8,20]{1,0:T(8,128)} %stations_hbm.1, s32[8,20]{1,0:T(8,128)} %moves_hbm.1, s32[8]{0:T(128)} %counts_hbm.1, s32[4,128]{1,0:T(4,128)} %bitcast.14, bf16[20,8,768]{2,1,0:T(8,128)(2,1)} %bitcast.11), custom_call_target="tpu_custom_call" | custom-call | tf_op jit(solution)/shard_map/pallas_call | solution.py:457
  3.4 7.3 %all-to-all-start.3 = ((bf16[32,8,896]{2,1,0:T(8,128)(2,1)}), bf16[32,8,896]{2,1,0:T(8,128)(2,1)S(1)}, u32[]{:S(2)}, u32[]{:S(2)}) async-start(bf16[32,8,896]{2,1,0:T(8,128)(2,1)} %get-tuple-element.34), calls=%async_computation.3 | async-start | bytes 917504 | tf_op jit(solution)/shard_map/all_to_all | solution.py:481
  10.8 0.0 copy-start
  10.8 1.0 %copy-done = bf16[16,3,5376]{2,0,1:T(8,128)(2,1)S(1)} copy-done((bf16[16,3,5376]{2,0,1:T(8,128)(2,1)S(1)}, bf16[16,3,5376]{2,0,1:T(8,128)(2,1)}, u32[]{:S(2)}) %copy-start) | copy-done | bytes 516120
  11.8 7.0 %shard_map.78.xs_hbm = bf16[36,896,384]{2,1,0:T(8,128)(2,1)} custom-call(bf16[3,16,5376]{2,1,0:T(8,128)(2,1)S(1)} %bitcast.9), custom_call_target="tpu_custom_call" | custom-call | flops 2000000000 | bytes 12582912 | tf_op jit(solution)/shard_map/pallas_call | solution.py:394
  18.8 0.0 copy-start.1
  18.8 2.5 %all-to-all-done.3.got_ref = bf16[32,8,896]{2,1,0:T(8,128)(2,1)S(1)} async-done(((bf16[32,8,896]{2,1,0:T(8,128)(2,1)}), bf16[32,8,896]{2,1,0:T(8,128)(2,1)S(1)}, u32[]{:S(2)}, u32[]{:S(2)}) %all-to-all-start.3) | async-done | bytes 458784 | tf_op jit(solution)/shard_map/all_to_all | solution.py:481
  21.3 8.1 %shard_map.79 = (s16[32,7,16,128]{3,2,1,0:T(8,128)(2,1)S(1)}, s16[32,7,16,128]{3,2,1,0:T(8,128)(2,1)S(1)}, s32[1,128]{1,0:T(1,128)S(1)}) custom-call(bf16[32,8,896]{2,1,0:T(8,128)(2,1)S(1)} %all-to-all-done.3.got_ref, bf16[36,896,384]{2,1,0:T(8,128)(2,1)} %shard_map.78.xs_hbm), custom_call_target="tpu_custom_call" | custom-call | tf_op jit(solution)/shard_map/pallas_call | solution.py:412
  29.4 0.0 copy-done.1
  29.5 23.9 %conditional.1 = ((f32[8,16,288]{2,1,0:T(8,128)S(1)}, f32[16,288]{1,0:T(8,128)S(1)})) conditional(s32[]{:T(128)} %bitcast.3, (s16[32,7,16,128]{3,2,1,0:T(8,128)(2,1)S(1)}, s32[8,128]{1,0:T(8,128)S(1)}, s32[8]{0:T(128)S(1)}) %tuple.25, (s16[32,7,16,128]{3,2,1,0:T(8,128)(2,1)S(1)}, s16[32,7,16,128]{3,2,1,0:T(8,128)(2,1)S(1)}, s32[8,128]{1,0:T(8,128)S(1)}, ...), branch_computations={%region_0.0_spmd, %region_1.0_spmd} | conditional | flops 917504 | bytes 7340040 | solution.py:494
  29.5 21.7 %all_to_all.17.back_ref = s16[32,7,16,128]{3,2,1,0:T(8,128)(2,1)S(1)} all-to-all(s16[32,7,16,128]{3,2,1,0:T(8,128)(2,1)S(1)} %get-tuple-element.16), channel_id=1, replica_groups=mesh['sta'=32,'tpl'=8] {'sta'}, dimensions={0} | all-to-all | bytes 1835008 | tf_op jit(solution)/shard_map/cond/branch_0_fun/all_to_all | solution.py:486
  51.1 2.2 %branch_0_fun.1 = (f32[8,16,288]{2,1,0:T(8,128)S(1)}, f32[16,288]{1,0:T(8,128)S(1)}) custom-call(s32[8,128]{1,0:T(8,128)S(1)} %get-tuple-element.14.list_ref, s32[8]{0:T(128)S(1)} %get-tuple-element.15.count_ref, s16[32,7,16,128]{3,2,1,0:T(8,128)(2,1)S(1)} %all_to_all.17.back_ref), custom_call_target="tpu_custom_call" | custom-call | tf_op jit(solution)/shard_map/cond/branch_0_fun/pallas_call | solution.py:436
  53.4 0.1 copy.9
  53.5 0.1 reshape.21
  53.6 1.8 %collective-permute-start.2 = (f32[36,128]{1,0:T(8,128)S(1)}, f32[36,128]{1,0:T(8,128)S(1)}, u32[]{:S(2)}, u32[]{:S(2)}) collective-permute-start(f32[36,128]{1,0:T(8,128)S(1)} %reshape.21), channel_id=1, source_target_pairs={{0,3},{1,2},{2,1},{3,0},{4,7},{5,6},{6,5},{7,4},{8,11},{9,10},{10,... | collective-permute-start | bytes 55304 | tf_op jit(solution)/shard_map/ppermute | solution.py:498
  55.4 1.0 %collective-permute-start.1 = (f32[36,128]{1,0:T(8,128)S(1)}, f32[36,128]{1,0:T(8,128)S(1)}, u32[]{:S(2)}, u32[]{:S(2)}) collective-permute-start(f32[36,128]{1,0:T(8,128)S(1)} %reshape.21), channel_id=1, source_target_pairs={{0,2},{1,3},{2,0},{3,1},{4,6},{5,7},{6,4},{7,5},{8,10},{9,11},{10,... | collective-permute-start | bytes 55304 | tf_op jit(solution)/shard_map/ppermute | solution.py:498
  56.3 1.4 %collective-permute-start = (f32[36,128]{1,0:T(8,128)S(1)}, f32[36,128]{1,0:T(8,128)S(1)}, u32[]{:S(2)}, u32[]{:S(2)}) collective-permute-start(f32[36,128]{1,0:T(8,128)S(1)} %reshape.21), channel_id=1, source_target_pairs={{0,1},{1,0},{2,3},{3,2},{4,5},{5,4},{6,7},{7,6},{8,9},{9,8},{10,11... | collective-permute-start | bytes 55304 | tf_op jit(solution)/shard_map/ppermute | solution.py:498
  57.7 0.0 collective-permute-done.2
  57.7 2.5 %collective-permute-done.1 = f32[36,128]{1,0:T(8,128)S(1)} collective-permute-done((f32[36,128]{1,0:T(8,128)S(1)}, f32[36,128]{1,0:T(8,128)S(1)}, u32[]{:S(2)}, u32[]{:S(2)}) %collective-permute-start.1) | collective-permute-done | bytes 18464 | tf_op jit(solution)/shard_map/ppermute | solution.py:498
  60.2 0.0 collective-permute-done
  60.2 5.2 %collective-permute-start.3 = (f32[36,128]{1,0:T(8,128)S(1)}, f32[36,128]{1,0:T(8,128)S(1)}, u32[]{:S(2)}, u32[]{:S(2)}) collective-permute-start(f32[36,128]{1,0:T(8,128)S(1)} %maximum_maximum_fusion.1), channel_id=1, source_target_pairs={{0,6},{1,7},{2,4},{3,5},{4,2},{5,3},{6,0},{7,1},{8,14},{9,15},{10,... | collective-permute-start | bytes 55304 | tf_op jit(solution)/shard_map/ppermute | solution.py:498
  65.4 0.4 copy.10
  65.8 1.4 %reshape.22 = f32[8,4608]{1,0:T(8,128)} reshape(f32[8,288,16]{2,1,0:T(8,128)S(1)} %copy.10) | data formatting | bytes 294912 | tf_op jit(solution)/shard_map/reshape | solution.py:503
  67.1 0.0 collective-permute-done.3
  67.2 0.1 collective-permute-start.4
  67.2 1.2 %collective-permute-done.4 = f32[36,128]{1,0:T(8,128)S(1)} collective-permute-done((f32[36,128]{1,0:T(8,128)S(1)}, f32[36,128]{1,0:T(8,128)S(1)}, u32[]{:S(2)}, u32[]{:S(2)}) %collective-permute-start.4) | collective-permute-done | bytes 18464 | tf_op jit(solution)/shard_map/ppermute | solution.py:498
  68.4 1.9 %collective-permute-start.7 = (f32[36,128]{1,0:T(8,128)S(1)}, f32[36,128]{1,0:T(8,128)S(1)}, u32[]{:S(2)}, u32[]{:S(2)}) collective-permute-start(f32[36,128]{1,0:T(8,128)S(1)} %max.37), channel_id=1, source_target_pairs={{0,32},{8,40},{16,48},{24,56},{32,0},{40,8},{48,16},{56,24},{64,96... | collective-permute-start | bytes 55304 | tf_op jit(solution)/shard_map/ppermute | solution.py:498
  70.3 1.5 %collective-permute-start.6 = (f32[36,128]{1,0:T(8,128)S(1)}, f32[36,128]{1,0:T(8,128)S(1)}, u32[]{:S(2)}, u32[]{:S(2)}) collective-permute-start(f32[36,128]{1,0:T(8,128)S(1)} %max.37), channel_id=1, source_target_pairs={{0,48},{8,56},{16,32},{24,40},{32,16},{40,24},{48,0},{56,8},{64,11... | collective-permute-start | bytes 55304 | tf_op jit(solution)/shard_map/ppermute | solution.py:498
  71.9 0.0 collective-permute-start.5
  71.9 1.8 %collective-permute-done.7 = f32[36,128]{1,0:T(8,128)S(1)} collective-permute-done((f32[36,128]{1,0:T(8,128)S(1)}, f32[36,128]{1,0:T(8,128)S(1)}, u32[]{:S(2)}, u32[]{:S(2)}) %collective-permute-start.7) | collective-permute-done | bytes 18464 | tf_op jit(solution)/shard_map/ppermute | solution.py:498
  73.7 1.6 %collective-permute-done.6 = f32[36,128]{1,0:T(8,128)S(1)} collective-permute-done((f32[36,128]{1,0:T(8,128)S(1)}, f32[36,128]{1,0:T(8,128)S(1)}, u32[]{:S(2)}, u32[]{:S(2)}) %collective-permute-start.6) | collective-permute-done | bytes 18464 | tf_op jit(solution)/shard_map/ppermute | solution.py:498
  75.3 0.3 collective-permute-done.5
  75.7 1.2 %collective-permute-start.10 = (f32[36,128]{1,0:T(8,128)S(1)}, f32[36,128]{1,0:T(8,128)S(1)}, u32[]{:S(2)}, u32[]{:S(2)}) collective-permute-start(f32[36,128]{1,0:T(8,128)S(1)} %maximum_maximum_fusion), channel_id=1, source_target_pairs={{0,128},{8,136},{16,144},{24,152},{32,160},{40,168},{48,176},{56,1... | collective-permute-start | bytes 55304 | tf_op jit(solution)/shard_map/ppermute | solution.py:498
  76.8 1.9 %collective-permute-start.9 = (f32[36,128]{1,0:T(8,128)S(1)}, f32[36,128]{1,0:T(8,128)S(1)}, u32[]{:S(2)}, u32[]{:S(2)}) collective-permute-start(f32[36,128]{1,0:T(8,128)S(1)} %maximum_maximum_fusion), channel_id=1, source_target_pairs={{0,192},{8,200},{16,208},{24,216},{32,224},{40,232},{48,240},{56,2... | collective-permute-start | bytes 55304 | tf_op jit(solution)/shard_map/ppermute | solution.py:498
  78.7 0.5 collective-permute-start.8
  79.3 1.8 %collective-permute-done.10 = f32[36,128]{1,0:T(8,128)S(1)} collective-permute-done((f32[36,128]{1,0:T(8,128)S(1)}, f32[36,128]{1,0:T(8,128)S(1)}, u32[]{:S(2)}, u32[]{:S(2)}) %collective-permute-start.10) | collective-permute-done | bytes 18464 | tf_op jit(solution)/shard_map/ppermute | solution.py:498
  81.1 0.8 collective-permute-done.9
  81.8 0.7 collective-permute-done.8
  82.5 0.6 maximum_bitcast_fusion
  (4 shorter events, 0.0 us)
Async XLA Ops:
  3.4 17.9 %all-to-all-start.3 = ((bf16[32,8,896]{2,1,0:T(8,128)(2,1)}), bf16[32,8,896]{2,1,0:T(8,128)(2,1)S(1)}, u32[]{:S(2)}, u32[]{:S(2)}) async-start(bf16[32,8,896]{2,1,0:T(8,128)(2,1)} %get-tuple-element.34), calls=%async_computation.3 | async-start | bytes 917504 | tf_op jit(solution)/shard_map/all_to_all | solution.py:481
  10.8 1.0 %copy-start = (bf16[16,3,5376]{2,0,1:T(8,128)(2,1)S(1)}, bf16[16,3,5376]{2,0,1:T(8,128)(2,1)}, u32[]{:S(2)}) copy-start(bf16[16,3,5376]{2,0,1:T(8,128)(2,1)} %param.8) | copy-start | bytes 1548292
  18.8 10.7 %copy-start.1 = (s32[8]{0:T(128)S(1)}, s32[8]{0:T(128)}, u32[]{:S(2)}) copy-start(s32[8]{0:T(128)} %counts_hbm.1) | copy-start | bytes 100
  53.6 4.1 %collective-permute-start.2 = (f32[36,128]{1,0:T(8,128)S(1)}, f32[36,128]{1,0:T(8,128)S(1)}, u32[]{:S(2)}, u32[]{:S(2)}) collective-permute-start(f32[36,128]{1,0:T(8,128)S(1)} %reshape.21), channel_id=1, source_target_pairs={{0,3},{1,2},{2,1},{3,0},{4,7},{5,6},{6,5},{7,4},{8,11},{9,10},{10,... | collective-permute-start | bytes 55304 | tf_op jit(solution)/shard_map/ppermute | solution.py:498
  55.4 4.8 %collective-permute-start.1 = (f32[36,128]{1,0:T(8,128)S(1)}, f32[36,128]{1,0:T(8,128)S(1)}, u32[]{:S(2)}, u32[]{:S(2)}) collective-permute-start(f32[36,128]{1,0:T(8,128)S(1)} %reshape.21), channel_id=1, source_target_pairs={{0,2},{1,3},{2,0},{3,1},{4,6},{5,7},{6,4},{7,5},{8,10},{9,11},{10,... | collective-permute-start | bytes 55304 | tf_op jit(solution)/shard_map/ppermute | solution.py:498
  56.3 3.8 %collective-permute-start = (f32[36,128]{1,0:T(8,128)S(1)}, f32[36,128]{1,0:T(8,128)S(1)}, u32[]{:S(2)}, u32[]{:S(2)}) collective-permute-start(f32[36,128]{1,0:T(8,128)S(1)} %reshape.21), channel_id=1, source_target_pairs={{0,1},{1,0},{2,3},{3,2},{4,5},{5,4},{6,7},{7,6},{8,9},{9,8},{10,11... | collective-permute-start | bytes 55304 | tf_op jit(solution)/shard_map/ppermute | solution.py:498
  60.2 7.0 %collective-permute-start.3 = (f32[36,128]{1,0:T(8,128)S(1)}, f32[36,128]{1,0:T(8,128)S(1)}, u32[]{:S(2)}, u32[]{:S(2)}) collective-permute-start(f32[36,128]{1,0:T(8,128)S(1)} %maximum_maximum_fusion.1), channel_id=1, source_target_pairs={{0,6},{1,7},{2,4},{3,5},{4,2},{5,3},{6,0},{7,1},{8,14},{9,15},{10,... | collective-permute-start | bytes 55304 | tf_op jit(solution)/shard_map/ppermute | solution.py:498
  67.2 1.2 %collective-permute-start.4 = (f32[36,128]{1,0:T(8,128)S(1)}, f32[36,128]{1,0:T(8,128)S(1)}, u32[]{:S(2)}, u32[]{:S(2)}) collective-permute-start(f32[36,128]{1,0:T(8,128)S(1)} %max.36), channel_id=1, source_target_pairs={{0,8},{8,0},{16,24},{24,16},{32,40},{40,32},{48,56},{56,48},{64,72... | collective-permute-start | bytes 55304 | tf_op jit(solution)/shard_map/ppermute | solution.py:498
  68.4 5.3 %collective-permute-start.7 = (f32[36,128]{1,0:T(8,128)S(1)}, f32[36,128]{1,0:T(8,128)S(1)}, u32[]{:S(2)}, u32[]{:S(2)}) collective-permute-start(f32[36,128]{1,0:T(8,128)S(1)} %max.37), channel_id=1, source_target_pairs={{0,32},{8,40},{16,48},{24,56},{32,0},{40,8},{48,16},{56,24},{64,96... | collective-permute-start | bytes 55304 | tf_op jit(solution)/shard_map/ppermute | solution.py:498
  70.3 5.0 %collective-permute-start.6 = (f32[36,128]{1,0:T(8,128)S(1)}, f32[36,128]{1,0:T(8,128)S(1)}, u32[]{:S(2)}, u32[]{:S(2)}) collective-permute-start(f32[36,128]{1,0:T(8,128)S(1)} %max.37), channel_id=1, source_target_pairs={{0,48},{8,56},{16,32},{24,40},{32,16},{40,24},{48,0},{56,8},{64,11... | collective-permute-start | bytes 55304 | tf_op jit(solution)/shard_map/ppermute | solution.py:498
  71.9 3.8 %collective-permute-start.5 = (f32[36,128]{1,0:T(8,128)S(1)}, f32[36,128]{1,0:T(8,128)S(1)}, u32[]{:S(2)}, u32[]{:S(2)}) collective-permute-start(f32[36,128]{1,0:T(8,128)S(1)} %max.37), channel_id=1, source_target_pairs={{0,16},{8,24},{16,0},{24,8},{32,48},{40,56},{48,32},{56,40},{64,80... | collective-permute-start | bytes 55304 | tf_op jit(solution)/shard_map/ppermute | solution.py:498
  75.7 5.4 %collective-permute-start.10 = (f32[36,128]{1,0:T(8,128)S(1)}, f32[36,128]{1,0:T(8,128)S(1)}, u32[]{:S(2)}, u32[]{:S(2)}) collective-permute-start(f32[36,128]{1,0:T(8,128)S(1)} %maximum_maximum_fusion), channel_id=1, source_target_pairs={{0,128},{8,136},{16,144},{24,152},{32,160},{40,168},{48,176},{56,1... | collective-permute-start | bytes 55304 | tf_op jit(solution)/shard_map/ppermute | solution.py:498
  76.8 5.0 %collective-permute-start.9 = (f32[36,128]{1,0:T(8,128)S(1)}, f32[36,128]{1,0:T(8,128)S(1)}, u32[]{:S(2)}, u32[]{:S(2)}) collective-permute-start(f32[36,128]{1,0:T(8,128)S(1)} %maximum_maximum_fusion), channel_id=1, source_target_pairs={{0,192},{8,200},{16,208},{24,216},{32,224},{40,232},{48,240},{56,2... | collective-permute-start | bytes 55304 | tf_op jit(solution)/shard_map/ppermute | solution.py:498
  78.7 3.8 %collective-permute-start.8 = (f32[36,128]{1,0:T(8,128)S(1)}, f32[36,128]{1,0:T(8,128)S(1)}, u32[]{:S(2)}, u32[]{:S(2)}) collective-permute-start(f32[36,128]{1,0:T(8,128)S(1)} %maximum_maximum_fusion), channel_id=1, source_target_pairs={{0,64},{8,72},{16,80},{24,88},{32,96},{40,104},{48,112},{56,120},{... | collective-permute-start | bytes 55304 | tf_op jit(solution)/shard_map/ppermute | solution.py:498

commit v8 on v7

--- a/solution.py
+++ b/solution.py
@@ -123,7 +123,7 @@
     tail = dot(pick, fields, NT)
     tail = jnp.where(iota(tail.shape, 1) == 4, over, tail).astype(jnp.bfloat16)
     copies[4].wait()
-    send = dot(pick, templates_ref[...].reshape(total, 3 * L)).astype(jnp.bfloat16)
+    send = dot(pick, templates_ref[...]).astype(jnp.bfloat16)
     send_ref[:, :, : 3 * L] = send.reshape(width, ROWS, 3 * L)
     send_ref[:, :, 3 * L :] = tail.reshape(width, ROWS, BLOCK)
 
@@ -467,7 +467,7 @@
             pltpu.VMEM((tpl_dev, SLOTS), jnp.int32),
             pltpu.SMEM((tpl_dev,), jnp.int32),
             pltpu.VMEM((parts, BLOCK), jnp.int32),
-            pltpu.VMEM((SLOTS, tpl_dev, 3 * L), jnp.bfloat16),
+            pltpu.VMEM((tpl_dev * SLOTS, 3 * L), jnp.bfloat16),
             pltpu.SemaphoreType.DMA((5,)),
         ],
         compiler_params=params(60),
@@ -476,7 +476,7 @@
         moveouts,
         station_counts,
         station_home.reshape(parts, BLOCK),
-        templates.transpose(1, 0, 2),
+        templates.transpose(1, 0, 2).reshape(tpl_dev * SLOTS, 3 * L),
     )
     got = lax.all_to_all(send, "sta", split_axis=0, concat_axis=0, tiled=True)
     xs = prep_call(waveforms)
@@ -506,7 +506,7 @@
     return (stack, best.reshape(PHASES * KEPT))
 
 
-ROUNDS = (("tpl", (1, 2, 3)), ("tpl", (6,)), ("sta", (1,)), ("sta", (2, 6, 4)), ("sta", (8, 24, 16)))
+ROUNDS = (("sta", (1,)), ("tpl", (6,)), ("tpl", (1, 2, 3)), ("sta", (2, 6, 4)), ("sta", (8, 24, 16)))
 
 
 def solution(mesh):

time: 84 us -> 83.8 us (level)
  blocking collectives: 21.7 us -> 19.9 us
  Pallas kernels: 20 us -> 21.2 us
  waiting for transfers between devices: 13.2 us -> 14.2 us
    all_to_all x1, blocking collectives: 21.7 us -> 19.9 us  [home(): return lax.all_to_all(x, 'sta', split_axis=0, concat_axis=0, tiled=True)]
    ppermute x11, waiting for transfers between devices: 10.7 us -> 11.6 us  [body(): lax.ppermute(best, axis, [(i, i ^ step) for i in range(size)])]
    pallas_call x1, Pallas kernels: 8.09 us -> 8.99 us  [correlate_call(): pl.pallas_call(correlate_kernel, out_shape=(jax.ShapeDtypeStruct((width,...]
  transfers between devices with their start and end apart: 12 -> 12, of which waited for: 9 -> 11; matrix products, arithmetic and copies ran while one was open for 2% -> 2% of each run, Pallas kernels for 8% -> 8%
where the time goes in v8:
time: 83.8 us; the launch traced here: 83.4 us
  starting transfers between devices  23.8 us (28%)
  Pallas kernels  21.2 us (25%)
  blocking collectives  19.9 us (24%)
  waiting for transfers between devices  14.2 us (17%)
  local copies, waits for them, and re-layouts  2.97 us (4%)
    all_to_all x1, blocking collectives, home(): return lax.all_to_all(x, 'sta', split_axis=0, concat_axis=0, tiled=True)  19.9 us
    ppermute x11, starting transfers between devices, body(): lax.ppermute(best, axis, [(i, i ^ step) for i in range(size)])  16.5 us
    ppermute x11, waiting for transfers between devices, body(): lax.ppermute(best, axis, [(i, i ^ step) for i in range(size)])  11.6 us
    pallas_call x1, Pallas kernels, correlate_call(): pl.pallas_call(correlate_kernel, out_shape=(jax.ShapeDtypeStruct((width,...  8.99 us
    all_to_all x1, starting transfers between devices, body(): got = lax.all_to_all(send, 'sta', split_axis=0, concat_axis=0, tiled=True)  7.33 us
    pallas_call x1, Pallas kernels, prep_call(): pl.pallas_call(prep_kernel, out_shape=jax.ShapeDtypeStruct((2 * stations...  6.97 us
    pallas_call x1, Pallas kernels, body(): pl.pallas_call(pack_kernel, out_shape=(jax.ShapeDtypeStruct((width, ROWS,...  2.79 us
    all_to_all x1, waiting for transfers between devices, body(): got = lax.all_to_all(send, 'sta', split_axis=0, concat_axis=0, tiled=True)  2.52 us
  transfers between devices with their start and end apart: 12, of which 11 were waited for; matrix products, arithmetic and copies ran while one was open for 2% of the time, Pallas kernels for 8%

profile of v8, /device:TPU:32, one launch (start us, length us, event | category | flops | bytes accessed | tf_op | source)
XLA Modules:
  0.0 83.4 jit_solution(6149588194059787278)
XLA Ops:
  0.6 2.8 %shard_map.77 = (bf16[32,8,896]{2,1,0:T(8,128)(2,1)}, s32[8,128]{1,0:T(8,128)S(1)}) custom-call(s32[8,20]{1,0:T(8,128)} %stations_hbm.1, s32[8,20]{1,0:T(8,128)} %moves_hbm.1, s32[8]{0:T(128)} %counts_hbm.1, s32[4,128]{1,0:T(4,128)} %bitcast.16, bf16[160,768]{1,0:T(8,128)(2,1)} %bitcast.13), custom_call_target="tpu_custom_call" | custom-call | tf_op jit(solution)/shard_map/pallas_call | solution.py:457
  3.4 7.3 %all-to-all-start.3 = ((bf16[32,8,896]{2,1,0:T(8,128)(2,1)}), bf16[32,8,896]{2,1,0:T(8,128)(2,1)S(1)}, u32[]{:S(2)}, u32[]{:S(2)}) async-start(bf16[32,8,896]{2,1,0:T(8,128)(2,1)} %get-tuple-element.34), calls=%async_computation.3 | async-start | bytes 917504 | tf_op jit(solution)/shard_map/all_to_all | solution.py:481
  10.8 0.0 copy-start
  10.8 1.0 %copy-done = bf16[16,3,5376]{2,0,1:T(8,128)(2,1)S(1)} copy-done((bf16[16,3,5376]{2,0,1:T(8,128)(2,1)S(1)}, bf16[16,3,5376]{2,0,1:T(8,128)(2,1)}, u32[]{:S(2)}) %copy-start) | copy-done | bytes 516120
  11.8 7.0 %shard_map.78.xs_hbm = bf16[36,896,384]{2,1,0:T(8,128)(2,1)} custom-call(bf16[3,16,5376]{2,1,0:T(8,128)(2,1)S(1)} %bitcast.11), custom_call_target="tpu_custom_call" | custom-call | flops 2000000000 | bytes 12582912 | tf_op jit(solution)/shard_map/pallas_call | solution.py:394
  18.8 0.0 copy-start.1
  18.8 2.5 %all-to-all-done.3.got_ref = bf16[32,8,896]{2,1,0:T(8,128)(2,1)S(1)} async-done(((bf16[32,8,896]{2,1,0:T(8,128)(2,1)}), bf16[32,8,896]{2,1,0:T(8,128)(2,1)S(1)}, u32[]{:S(2)}, u32[]{:S(2)}) %all-to-all-start.3) | async-done | bytes 458784 | tf_op jit(solution)/shard_map/all_to_all | solution.py:481
  21.3 9.0 %shard_map.79 = (s16[32,7,16,128]{3,2,1,0:T(8,128)(2,1)S(1)}, s16[32,7,16,128]{3,2,1,0:T(8,128)(2,1)S(1)}, s32[1,128]{1,0:T(1,128)S(1)}) custom-call(bf16[32,8,896]{2,1,0:T(8,128)(2,1)S(1)} %all-to-all-done.3.got_ref, bf16[36,896,384]{2,1,0:T(8,128)(2,1)} %shard_map.78.xs_hbm), custom_call_target="tpu_custom_call" | custom-call | tf_op jit(solution)/shard_map/pallas_call | solution.py:412
  30.3 0.0 copy-done.1
  30.4 22.3 %conditional.1 = ((f32[8,16,288]{2,1,0:T(8,128)S(1)}, f32[16,288]{1,0:T(8,128)S(1)})) conditional(s32[]{:T(128)} %bitcast.4, (s16[32,7,16,128]{3,2,1,0:T(8,128)(2,1)S(1)}, s32[8,128]{1,0:T(8,128)S(1)}, s32[8]{0:T(128)S(1)}) %tuple.25, (s16[32,7,16,128]{3,2,1,0:T(8,128)(2,1)S(1)}, s16[32,7,16,128]{3,2,1,0:T(8,128)(2,1)S(1)}, s32[8,128]{1,0:T(8,128)S(1)}, ...), branch_computations={%region_0.0_spmd, %region_1.0_spmd} | conditional | flops 917504 | bytes 7340040 | solution.py:494
  30.4 19.9 %all_to_all.17.back_ref = s16[32,7,16,128]{3,2,1,0:T(8,128)(2,1)S(1)} all-to-all(s16[32,7,16,128]{3,2,1,0:T(8,128)(2,1)S(1)} %get-tuple-element.16), channel_id=1, replica_groups=mesh['sta'=32,'tpl'=8] {'sta'}, dimensions={0} | all-to-all | bytes 1835008 | tf_op jit(solution)/shard_map/cond/branch_0_fun/all_to_all | solution.py:486
  50.2 2.4 %branch_0_fun.1 = (f32[8,16,288]{2,1,0:T(8,128)S(1)}, f32[16,288]{1,0:T(8,128)S(1)}) custom-call(s32[8,128]{1,0:T(8,128)S(1)} %get-tuple-element.14.list_ref, s32[8]{0:T(128)S(1)} %get-tuple-element.15.count_ref, s16[32,7,16,128]{3,2,1,0:T(8,128)(2,1)S(1)} %all_to_all.17.back_ref), custom_call_target="tpu_custom_call" | custom-call | tf_op jit(solution)/shard_map/cond/branch_0_fun/pallas_call | solution.py:436
  52.7 0.1 copy.9
  52.8 0.1 reshape.25
  52.9 0.4 collective-permute-start
  53.3 0.9 %collective-permute-done = f32[36,128]{1,0:T(8,128)S(1)} collective-permute-done((f32[36,128]{1,0:T(8,128)S(1)}, f32[36,128]{1,0:T(8,128)S(1)}, u32[]{:S(2)}, u32[]{:S(2)}) %collective-permute-start) | collective-permute-done | bytes 18464 | tf_op jit(solution)/shard_map/ppermute | solution.py:498
  54.2 5.3 %collective-permute-start.1 = (f32[36,128]{1,0:T(8,128)S(1)}, f32[36,128]{1,0:T(8,128)S(1)}, u32[]{:S(2)}, u32[]{:S(2)}) collective-permute-start(f32[36,128]{1,0:T(8,128)S(1)} %max.33), channel_id=1, source_target_pairs={{0,6},{1,7},{2,4},{3,5},{4,2},{5,3},{6,0},{7,1},{8,14},{9,15},{10,... | collective-permute-start | bytes 55304 | tf_op jit(solution)/shard_map/ppermute | solution.py:498
  59.4 0.4 copy.10
  59.8 1.4 %reshape.26 = f32[8,4608]{1,0:T(8,128)} reshape(f32[8,288,16]{2,1,0:T(8,128)S(1)} %copy.10) | data formatting | bytes 294912 | tf_op jit(solution)/shard_map/reshape | solution.py:503
  61.2 0.0 collective-permute-done.1
  61.2 1.2 %collective-permute-start.4 = (f32[36,128]{1,0:T(8,128)S(1)}, f32[36,128]{1,0:T(8,128)S(1)}, u32[]{:S(2)}, u32[]{:S(2)}) collective-permute-start(f32[36,128]{1,0:T(8,128)S(1)} %max.34), channel_id=1, source_target_pairs={{0,3},{1,2},{2,1},{3,0},{4,7},{5,6},{6,5},{7,4},{8,11},{9,10},{10,... | collective-permute-start | bytes 55304 | tf_op jit(solution)/shard_map/ppermute | solution.py:498
  62.4 2.4 %collective-permute-start.3 = (f32[36,128]{1,0:T(8,128)S(1)}, f32[36,128]{1,0:T(8,128)S(1)}, u32[]{:S(2)}, u32[]{:S(2)}) collective-permute-start(f32[36,128]{1,0:T(8,128)S(1)} %max.34), channel_id=1, source_target_pairs={{0,2},{1,3},{2,0},{3,1},{4,6},{5,7},{6,4},{7,5},{8,10},{9,11},{10,... | collective-permute-start | bytes 55304 | tf_op jit(solution)/shard_map/ppermute | solution.py:498
  64.8 0.1 collective-permute-start.2
  64.9 0.1 collective-permute-done.4
  65.1 2.1 %collective-permute-done.3 = f32[36,128]{1,0:T(8,128)S(1)} collective-permute-done((f32[36,128]{1,0:T(8,128)S(1)}, f32[36,128]{1,0:T(8,128)S(1)}, u32[]{:S(2)}, u32[]{:S(2)}) %collective-permute-start.3) | collective-permute-done | bytes 18464 | tf_op jit(solution)/shard_map/ppermute | solution.py:498
  67.2 1.4 %collective-permute-done.2 = f32[36,128]{1,0:T(8,128)S(1)} collective-permute-done((f32[36,128]{1,0:T(8,128)S(1)}, f32[36,128]{1,0:T(8,128)S(1)}, u32[]{:S(2)}, u32[]{:S(2)}) %collective-permute-start.2) | collective-permute-done | bytes 18464 | tf_op jit(solution)/shard_map/ppermute | solution.py:498
  68.6 1.8 %collective-permute-start.7 = (f32[36,128]{1,0:T(8,128)S(1)}, f32[36,128]{1,0:T(8,128)S(1)}, u32[]{:S(2)}, u32[]{:S(2)}) collective-permute-start(f32[36,128]{1,0:T(8,128)S(1)} %maximum_maximum_fusion.1), channel_id=1, source_target_pairs={{0,32},{8,40},{16,48},{24,56},{32,0},{40,8},{48,16},{56,24},{64,96... | collective-permute-start | bytes 55304 | tf_op jit(solution)/shard_map/ppermute | solution.py:498
  70.5 1.4 %collective-permute-start.6 = (f32[36,128]{1,0:T(8,128)S(1)}, f32[36,128]{1,0:T(8,128)S(1)}, u32[]{:S(2)}, u32[]{:S(2)}) collective-permute-start(f32[36,128]{1,0:T(8,128)S(1)} %maximum_maximum_fusion.1), channel_id=1, source_target_pairs={{0,48},{8,56},{16,32},{24,40},{32,16},{40,24},{48,0},{56,8},{64,11... | collective-permute-start | bytes 55304 | tf_op jit(solution)/shard_map/ppermute | solution.py:498
  71.9 0.3 collective-permute-start.5
  72.2 2.0 %collective-permute-done.7 = f32[36,128]{1,0:T(8,128)S(1)} collective-permute-done((f32[36,128]{1,0:T(8,128)S(1)}, f32[36,128]{1,0:T(8,128)S(1)}, u32[]{:S(2)}, u32[]{:S(2)}) %collective-permute-start.7) | collective-permute-done | bytes 18464 | tf_op jit(solution)/shard_map/ppermute | solution.py:498
  74.2 1.3 %collective-permute-done.6 = f32[36,128]{1,0:T(8,128)S(1)} collective-permute-done((f32[36,128]{1,0:T(8,128)S(1)}, f32[36,128]{1,0:T(8,128)S(1)}, u32[]{:S(2)}, u32[]{:S(2)}) %collective-permute-start.6) | collective-permute-done | bytes 18464 | tf_op jit(solution)/shard_map/ppermute | solution.py:498
  75.5 0.2 collective-permute-done.5
  75.7 1.6 %collective-permute-start.10 = (f32[36,128]{1,0:T(8,128)S(1)}, f32[36,128]{1,0:T(8,128)S(1)}, u32[]{:S(2)}, u32[]{:S(2)}) collective-permute-start(f32[36,128]{1,0:T(8,128)S(1)} %maximum_maximum_fusion), channel_id=1, source_target_pairs={{0,128},{8,136},{16,144},{24,152},{32,160},{40,168},{48,176},{56,1... | collective-permute-start | bytes 55304 | tf_op jit(solution)/shard_map/ppermute | solution.py:498
  77.3 1.8 %collective-permute-start.9 = (f32[36,128]{1,0:T(8,128)S(1)}, f32[36,128]{1,0:T(8,128)S(1)}, u32[]{:S(2)}, u32[]{:S(2)}) collective-permute-start(f32[36,128]{1,0:T(8,128)S(1)} %maximum_maximum_fusion), channel_id=1, source_target_pairs={{0,192},{8,200},{16,208},{24,216},{32,224},{40,232},{48,240},{56,2... | collective-permute-start | bytes 55304 | tf_op jit(solution)/shard_map/ppermute | solution.py:498
  79.0 0.2 collective-permute-start.8
  79.2 1.8 %collective-permute-done.10 = f32[36,128]{1,0:T(8,128)S(1)} collective-permute-done((f32[36,128]{1,0:T(8,128)S(1)}, f32[36,128]{1,0:T(8,128)S(1)}, u32[]{:S(2)}, u32[]{:S(2)}) %collective-permute-start.10) | collective-permute-done | bytes 18464 | tf_op jit(solution)/shard_map/ppermute | solution.py:498
  81.0 1.2 %collective-permute-done.9 = f32[36,128]{1,0:T(8,128)S(1)} collective-permute-done((f32[36,128]{1,0:T(8,128)S(1)}, f32[36,128]{1,0:T(8,128)S(1)}, u32[]{:S(2)}, u32[]{:S(2)}) %collective-permute-start.9) | collective-permute-done | bytes 18464 | tf_op jit(solution)/shard_map/ppermute | solution.py:498
  82.3 0.5 collective-permute-done.8
  82.8 0.6 maximum_bitcast_fusion
  (4 shorter events, 0.0 us)
Async XLA Ops:
  3.4 17.9 %all-to-all-start.3 = ((bf16[32,8,896]{2,1,0:T(8,128)(2,1)}), bf16[32,8,896]{2,1,0:T(8,128)(2,1)S(1)}, u32[]{:S(2)}, u32[]{:S(2)}) async-start(bf16[32,8,896]{2,1,0:T(8,128)(2,1)} %get-tuple-element.34), calls=%async_computation.3 | async-start | bytes 917504 | tf_op jit(solution)/shard_map/all_to_all | solution.py:481
  10.8 1.0 %copy-start = (bf16[16,3,5376]{2,0,1:T(8,128)(2,1)S(1)}, bf16[16,3,5376]{2,0,1:T(8,128)(2,1)}, u32[]{:S(2)}) copy-start(bf16[16,3,5376]{2,0,1:T(8,128)(2,1)} %param.8) | copy-start | bytes 1548292
  18.8 11.6 %copy-start.1 = (s32[8]{0:T(128)S(1)}, s32[8]{0:T(128)}, u32[]{:S(2)}) copy-start(s32[8]{0:T(128)} %counts_hbm.1) | copy-start | bytes 100
  52.9 1.3 %collective-permute-start = (f32[36,128]{1,0:T(8,128)S(1)}, f32[36,128]{1,0:T(8,128)S(1)}, u32[]{:S(2)}, u32[]{:S(2)}) collective-permute-start(f32[36,128]{1,0:T(8,128)S(1)} %reshape.25), channel_id=1, source_target_pairs={{0,8},{8,0},{16,24},{24,16},{32,40},{40,32},{48,56},{56,48},{64,72... | collective-permute-start | bytes 55304 | tf_op jit(solution)/shard_map/ppermute | solution.py:498
  54.2 7.0 %collective-permute-start.1 = (f32[36,128]{1,0:T(8,128)S(1)}, f32[36,128]{1,0:T(8,128)S(1)}, u32[]{:S(2)}, u32[]{:S(2)}) collective-permute-start(f32[36,128]{1,0:T(8,128)S(1)} %max.33), channel_id=1, source_target_pairs={{0,6},{1,7},{2,4},{3,5},{4,2},{5,3},{6,0},{7,1},{8,14},{9,15},{10,... | collective-permute-start | bytes 55304 | tf_op jit(solution)/shard_map/ppermute | solution.py:498
  61.2 3.8 %collective-permute-start.4 = (f32[36,128]{1,0:T(8,128)S(1)}, f32[36,128]{1,0:T(8,128)S(1)}, u32[]{:S(2)}, u32[]{:S(2)}) collective-permute-start(f32[36,128]{1,0:T(8,128)S(1)} %max.34), channel_id=1, source_target_pairs={{0,3},{1,2},{2,1},{3,0},{4,7},{5,6},{6,5},{7,4},{8,11},{9,10},{10,... | collective-permute-start | bytes 55304 | tf_op jit(solution)/shard_map/ppermute | solution.py:498
  62.4 4.8 %collective-permute-start.3 = (f32[36,128]{1,0:T(8,128)S(1)}, f32[36,128]{1,0:T(8,128)S(1)}, u32[]{:S(2)}, u32[]{:S(2)}) collective-permute-start(f32[36,128]{1,0:T(8,128)S(1)} %max.34), channel_id=1, source_target_pairs={{0,2},{1,3},{2,0},{3,1},{4,6},{5,7},{6,4},{7,5},{8,10},{9,11},{10,... | collective-permute-start | bytes 55304 | tf_op jit(solution)/shard_map/ppermute | solution.py:498
  64.8 3.8 %collective-permute-start.2 = (f32[36,128]{1,0:T(8,128)S(1)}, f32[36,128]{1,0:T(8,128)S(1)}, u32[]{:S(2)}, u32[]{:S(2)}) collective-permute-start(f32[36,128]{1,0:T(8,128)S(1)} %max.34), channel_id=1, source_target_pairs={{0,1},{1,0},{2,3},{3,2},{4,5},{5,4},{6,7},{7,6},{8,9},{9,8},{10,11... | collective-permute-start | bytes 55304 | tf_op jit(solution)/shard_map/ppermute | solution.py:498
  68.6 5.5 %collective-permute-start.7 = (f32[36,128]{1,0:T(8,128)S(1)}, f32[36,128]{1,0:T(8,128)S(1)}, u32[]{:S(2)}, u32[]{:S(2)}) collective-permute-start(f32[36,128]{1,0:T(8,128)S(1)} %maximum_maximum_fusion.1), channel_id=1, source_target_pairs={{0,32},{8,40},{16,48},{24,56},{32,0},{40,8},{48,16},{56,24},{64,96... | collective-permute-start | bytes 55304 | tf_op jit(solution)/shard_map/ppermute | solution.py:498
  70.5 5.0 %collective-permute-start.6 = (f32[36,128]{1,0:T(8,128)S(1)}, f32[36,128]{1,0:T(8,128)S(1)}, u32[]{:S(2)}, u32[]{:S(2)}) collective-permute-start(f32[36,128]{1,0:T(8,128)S(1)} %maximum_maximum_fusion.1), channel_id=1, source_target_pairs={{0,48},{8,56},{16,32},{24,40},{32,16},{40,24},{48,0},{56,8},{64,11... | collective-permute-start | bytes 55304 | tf_op jit(solution)/shard_map/ppermute | solution.py:498
  71.9 3.8 %collective-permute-start.5 = (f32[36,128]{1,0:T(8,128)S(1)}, f32[36,128]{1,0:T(8,128)S(1)}, u32[]{:S(2)}, u32[]{:S(2)}) collective-permute-start(f32[36,128]{1,0:T(8,128)S(1)} %maximum_maximum_fusion.1), channel_id=1, source_target_pairs={{0,16},{8,24},{16,0},{24,8},{32,48},{40,56},{48,32},{56,40},{64,80... | collective-permute-start | bytes 55304 | tf_op jit(solution)/shard_map/ppermute | solution.py:498
  75.7 5.4 %collective-permute-start.10 = (f32[36,128]{1,0:T(8,128)S(1)}, f32[36,128]{1,0:T(8,128)S(1)}, u32[]{:S(2)}, u32[]{:S(2)}) collective-permute-start(f32[36,128]{1,0:T(8,128)S(1)} %maximum_maximum_fusion), channel_id=1, source_target_pairs={{0,128},{8,136},{16,144},{24,152},{32,160},{40,168},{48,176},{56,1... | collective-permute-start | bytes 55304 | tf_op jit(solution)/shard_map/ppermute | solution.py:498
  77.3 5.0 %collective-permute-start.9 = (f32[36,128]{1,0:T(8,128)S(1)}, f32[36,128]{1,0:T(8,128)S(1)}, u32[]{:S(2)}, u32[]{:S(2)}) collective-permute-start(f32[36,128]{1,0:T(8,128)S(1)} %maximum_maximum_fusion), channel_id=1, source_target_pairs={{0,192},{8,200},{16,208},{24,216},{32,224},{40,232},{48,240},{56,2... | collective-permute-start | bytes 55304 | tf_op jit(solution)/shard_map/ppermute | solution.py:498
  79.0 3.8 %collective-permute-start.8 = (f32[36,128]{1,0:T(8,128)S(1)}, f32[36,128]{1,0:T(8,128)S(1)}, u32[]{:S(2)}, u32[]{:S(2)}) collective-permute-start(f32[36,128]{1,0:T(8,128)S(1)} %maximum_maximum_fusion), channel_id=1, source_target_pairs={{0,64},{8,72},{16,80},{24,88},{32,96},{40,104},{48,112},{56,120},{... | collective-permute-start | bytes 55304 | tf_op jit(solution)/shard_map/ppermute | solution.py:498

commit v9 on v8

--- a/solution.py
+++ b/solution.py
@@ -21,6 +21,7 @@
 REACH = L // PHASES
 DEPTH = 3 * L + BLOCK
 INV = 3 * L + 3 * PHASES
+USED = INV + 3 * PHASES
 CHUNK = 8
 CAP = 6
 ROWS = 8
@@ -181,19 +182,18 @@
             term = inv.astype(jnp.bfloat16)
             xs_ref[s, INV + i * PHASES : INV + (i + 1) * PHASES, :] = term
             inv = inv - term.astype(jnp.float32)
-        xs_ref[s, INV + 3 * PHASES :, :] = jnp.zeros((DEPTH - INV - 3 * PHASES, WIDE), jnp.bfloat16)
 
     @pl.loop(0, wave_ref.shape[1] // 2)
     def _(i):
         one_station(2 * i)
         one_station(2 * i + 1)
         pair = pl.ds(2 * i, 2)
-        pltpu.make_async_copy(xs_ref.at[pair], xs_hbm.at[pair], sems.at[i]).start()
+        pltpu.make_async_copy(xs_ref.at[pair, pl.ds(0, USED)], xs_hbm.at[pair, pl.ds(0, USED)], sems.at[i]).start()
 
     @pl.loop(0, wave_ref.shape[1] // 2)
     def _(i):
         pair = pl.ds(2 * i, 2)
-        pltpu.make_async_copy(xs_ref.at[pair], xs_hbm.at[pair], sems.at[i]).wait()
+        pltpu.make_async_copy(xs_ref.at[pair, pl.ds(0, USED)], xs_hbm.at[pair, pl.ds(0, USED)], sems.at[i]).wait()
 
 
 def correlate_kernel(
@@ -203,9 +203,11 @@
     stations = xs_ref.shape[0]
     total = width * ROWS
     room = sorted_ref.shape[0]
-    loads = [pltpu.make_async_copy(xs_hbm.at[s], xs_ref.at[s], xs_sems.at[s]) for s in range(stations)]
+    loads = [pltpu.make_async_copy(xs_hbm.at[s, pl.ds(0, USED)], xs_ref.at[s, pl.ds(0, USED)], xs_sems.at[s]) for s in range(stations)]
     for load in loads:
         load.start()
+    for s in range(stations):
+        xs_ref[s, USED:, :] = jnp.zeros((DEPTH - USED, WIDE), jnp.bfloat16)
     got = got_ref[...].reshape(total, DEPTH)
     pieces = got[:, : 3 * L]
     eye = (iota((8, BLOCK), 0) == iota((8, BLOCK), 1)).astype(jnp.bfloat16)
@@ -248,7 +250,7 @@
     copy.wait()
 
     def arrive(s, carry):
-        pltpu.make_async_copy(xs_hbm.at[s], xs_ref.at[s], xs_sems.at[s]).wait()
+        pltpu.make_async_copy(xs_hbm.at[s, pl.ds(0, USED)], xs_ref.at[s, pl.ds(0, USED)], xs_sems.at[s]).wait()
         return carry
 
     sub = iota((PHASES, BLOCK), 0)

time: 83.8 us -> 83.7 us (level)
  waiting for transfers between devices: 14.2 us -> 13.2 us
    ppermute x11, waiting for transfers between devices: 11.6 us -> 10.7 us  [body(): lax.ppermute(best, axis, [(i, i ^ step) for i in range(size)])]
where the time goes in v9:
time: 83.7 us; the launch traced here: 83.4 us
  starting transfers between devices  24.4 us (29%)
  Pallas kernels  20.9 us (25%)
  blocking collectives  20.6 us (25%)
  waiting for transfers between devices  13.2 us (16%)
  local copies, waits for them, and re-layouts  2.97 us (4%)
    all_to_all x1, blocking collectives, home(): return lax.all_to_all(x, 'sta', split_axis=0, concat_axis=0, tiled=True)  20.6 us
    ppermute x11, starting transfers between devices, body(): lax.ppermute(best, axis, [(i, i ^ step) for i in range(size)])  17 us
    ppermute x11, waiting for transfers between devices, body(): lax.ppermute(best, axis, [(i, i ^ step) for i in range(size)])  10.7 us
    pallas_call x1, Pallas kernels, correlate_call(): pl.pallas_call(correlate_kernel, out_shape=(jax.ShapeDtypeStruct((width,...  8.96 us
    all_to_all x1, starting transfers between devices, body(): got = lax.all_to_all(send, 'sta', split_axis=0, concat_axis=0, tiled=True)  7.33 us
    pallas_call x1, Pallas kernels, prep_call(): pl.pallas_call(prep_kernel, out_shape=jax.ShapeDtypeStruct((2 * stations...  6.97 us
    pallas_call x1, Pallas kernels, body(): pl.pallas_call(pack_kernel, out_shape=(jax.ShapeDtypeStruct((width, ROWS,...  2.79 us
    all_to_all x1, waiting for transfers between devices, body(): got = lax.all_to_all(send, 'sta', split_axis=0, concat_axis=0, tiled=True)  2.52 us
  transfers between devices with their start and end apart: 12, of which 11 were waited for; matrix products, arithmetic and copies ran while one was open for 2% of the time, Pallas kernels for 8%

profile of v9, /device:TPU:32, one launch (start us, length us, event | category | flops | bytes accessed | tf_op | source)
XLA Modules:
  0.0 83.4 jit_solution(1588888039942300263)
XLA Ops:
  0.6 2.8 %shard_map.77 = (bf16[32,8,896]{2,1,0:T(8,128)(2,1)}, s32[8,128]{1,0:T(8,128)S(1)}) custom-call(s32[8,20]{1,0:T(8,128)} %stations_hbm.1, s32[8,20]{1,0:T(8,128)} %moves_hbm.1, s32[8]{0:T(128)} %counts_hbm.1, s32[4,128]{1,0:T(4,128)} %bitcast.16, bf16[160,768]{1,0:T(8,128)(2,1)} %bitcast.13), custom_call_target="tpu_custom_call" | custom-call | tf_op jit(solution)/shard_map/pallas_call | solution.py:459
  3.4 7.3 %all-to-all-start.3 = ((bf16[32,8,896]{2,1,0:T(8,128)(2,1)}), bf16[32,8,896]{2,1,0:T(8,128)(2,1)S(1)}, u32[]{:S(2)}, u32[]{:S(2)}) async-start(bf16[32,8,896]{2,1,0:T(8,128)(2,1)} %get-tuple-element.34), calls=%async_computation.3 | async-start | bytes 917504 | tf_op jit(solution)/shard_map/all_to_all | solution.py:483
  10.8 0.0 copy-start
  10.8 1.0 %copy-done = bf16[16,3,5376]{2,0,1:T(8,128)(2,1)S(1)} copy-done((bf16[16,3,5376]{2,0,1:T(8,128)(2,1)S(1)}, bf16[16,3,5376]{2,0,1:T(8,128)(2,1)}, u32[]{:S(2)}) %copy-start) | copy-done | bytes 516120
  11.8 7.0 %shard_map.78.xs_hbm = bf16[36,896,384]{2,1,0:T(8,128)(2,1)} custom-call(bf16[3,16,5376]{2,1,0:T(8,128)(2,1)S(1)} %bitcast.11), custom_call_target="tpu_custom_call" | custom-call | flops 2000000000 | bytes 12582912 | tf_op jit(solution)/shard_map/pallas_call | solution.py:396
  18.8 0.0 copy-start.1
  18.8 2.5 %all-to-all-done.3.got_ref = bf16[32,8,896]{2,1,0:T(8,128)(2,1)S(1)} async-done(((bf16[32,8,896]{2,1,0:T(8,128)(2,1)}), bf16[32,8,896]{2,1,0:T(8,128)(2,1)S(1)}, u32[]{:S(2)}, u32[]{:S(2)}) %all-to-all-start.3) | async-done | bytes 458784 | tf_op jit(solution)/shard_map/all_to_all | solution.py:483
  21.3 9.0 %shard_map.79 = (s16[32,7,16,128]{3,2,1,0:T(8,128)(2,1)S(1)}, s16[32,7,16,128]{3,2,1,0:T(8,128)(2,1)S(1)}, s32[1,128]{1,0:T(1,128)S(1)}) custom-call(bf16[32,8,896]{2,1,0:T(8,128)(2,1)S(1)} %all-to-all-done.3.got_ref, bf16[36,896,384]{2,1,0:T(8,128)(2,1)} %shard_map.78.xs_hbm), custom_call_target="tpu_custom_call" | custom-call | tf_op jit(solution)/shard_map/pallas_call | solution.py:414
  30.3 0.0 copy-done.1
  30.3 22.8 %conditional.1 = ((f32[8,16,288]{2,1,0:T(8,128)S(1)}, f32[16,288]{1,0:T(8,128)S(1)})) conditional(s32[]{:T(128)} %bitcast.4, (s16[32,7,16,128]{3,2,1,0:T(8,128)(2,1)S(1)}, s32[8,128]{1,0:T(8,128)S(1)}, s32[8]{0:T(128)S(1)}) %tuple.25, (s16[32,7,16,128]{3,2,1,0:T(8,128)(2,1)S(1)}, s16[32,7,16,128]{3,2,1,0:T(8,128)(2,1)S(1)}, s32[8,128]{1,0:T(8,128)S(1)}, ...), branch_computations={%region_0.0_spmd, %region_1.0_spmd} | conditional | flops 917504 | bytes 7340040 | solution.py:496
  30.3 20.6 %all_to_all.17.back_ref = s16[32,7,16,128]{3,2,1,0:T(8,128)(2,1)S(1)} all-to-all(s16[32,7,16,128]{3,2,1,0:T(8,128)(2,1)S(1)} %get-tuple-element.16), channel_id=1, replica_groups=mesh['sta'=32,'tpl'=8] {'sta'}, dimensions={0} | all-to-all | bytes 1835008 | tf_op jit(solution)/shard_map/cond/branch_0_fun/all_to_all | solution.py:488
  50.9 2.2 %branch_0_fun.1 = (f32[8,16,288]{2,1,0:T(8,128)S(1)}, f32[16,288]{1,0:T(8,128)S(1)}) custom-call(s32[8,128]{1,0:T(8,128)S(1)} %get-tuple-element.14.list_ref, s32[8]{0:T(128)S(1)} %get-tuple-element.15.count_ref, s16[32,7,16,128]{3,2,1,0:T(8,128)(2,1)S(1)} %all_to_all.17.back_ref), custom_call_target="tpu_custom_call" | custom-call | tf_op jit(solution)/shard_map/cond/branch_0_fun/pallas_call | solution.py:438
  53.1 0.1 copy.9
  53.2 0.1 reshape.25
  53.3 0.7 collective-permute-start
  54.1 0.8 %collective-permute-done = f32[36,128]{1,0:T(8,128)S(1)} collective-permute-done((f32[36,128]{1,0:T(8,128)S(1)}, f32[36,128]{1,0:T(8,128)S(1)}, u32[]{:S(2)}, u32[]{:S(2)}) %collective-permute-start) | collective-permute-done | bytes 18464 | tf_op jit(solution)/shard_map/ppermute | solution.py:500
  54.9 5.6 %collective-permute-start.1 = (f32[36,128]{1,0:T(8,128)S(1)}, f32[36,128]{1,0:T(8,128)S(1)}, u32[]{:S(2)}, u32[]{:S(2)}) collective-permute-start(f32[36,128]{1,0:T(8,128)S(1)} %max.33), channel_id=1, source_target_pairs={{0,6},{1,7},{2,4},{3,5},{4,2},{5,3},{6,0},{7,1},{8,14},{9,15},{10,... | collective-permute-start | bytes 55304 | tf_op jit(solution)/shard_map/ppermute | solution.py:500
  60.5 0.4 copy.10
  60.9 1.4 %reshape.26 = f32[8,4608]{1,0:T(8,128)} reshape(f32[8,288,16]{2,1,0:T(8,128)S(1)} %copy.10) | data formatting | bytes 294912 | tf_op jit(solution)/shard_map/reshape | solution.py:505
  62.2 0.0 collective-permute-done.1
  62.3 0.1 collective-permute-start.4
  62.3 2.3 %collective-permute-start.3 = (f32[36,128]{1,0:T(8,128)S(1)}, f32[36,128]{1,0:T(8,128)S(1)}, u32[]{:S(2)}, u32[]{:S(2)}) collective-permute-start(f32[36,128]{1,0:T(8,128)S(1)} %max.34), channel_id=1, source_target_pairs={{0,2},{1,3},{2,0},{3,1},{4,6},{5,7},{6,4},{7,5},{8,10},{9,11},{10,... | collective-permute-start | bytes 55304 | tf_op jit(solution)/shard_map/ppermute | solution.py:500
  64.6 1.2 %collective-permute-start.2 = (f32[36,128]{1,0:T(8,128)S(1)}, f32[36,128]{1,0:T(8,128)S(1)}, u32[]{:S(2)}, u32[]{:S(2)}) collective-permute-start(f32[36,128]{1,0:T(8,128)S(1)} %max.34), channel_id=1, source_target_pairs={{0,1},{1,0},{2,3},{3,2},{4,5},{5,4},{6,7},{7,6},{8,9},{9,8},{10,11... | collective-permute-start | bytes 55304 | tf_op jit(solution)/shard_map/ppermute | solution.py:500
  65.8 0.9 %collective-permute-done.4 = f32[36,128]{1,0:T(8,128)S(1)} collective-permute-done((f32[36,128]{1,0:T(8,128)S(1)}, f32[36,128]{1,0:T(8,128)S(1)}, u32[]{:S(2)}, u32[]{:S(2)}) %collective-permute-start.4) | collective-permute-done | bytes 18464 | tf_op jit(solution)/shard_map/ppermute | solution.py:500
  66.7 0.5 collective-permute-done.3
  67.2 1.2 %collective-permute-done.2 = f32[36,128]{1,0:T(8,128)S(1)} collective-permute-done((f32[36,128]{1,0:T(8,128)S(1)}, f32[36,128]{1,0:T(8,128)S(1)}, u32[]{:S(2)}, u32[]{:S(2)}) %collective-permute-start.2) | collective-permute-done | bytes 18464 | tf_op jit(solution)/shard_map/ppermute | solution.py:500
  68.4 2.1 %collective-permute-start.7 = (f32[36,128]{1,0:T(8,128)S(1)}, f32[36,128]{1,0:T(8,128)S(1)}, u32[]{:S(2)}, u32[]{:S(2)}) collective-permute-start(f32[36,128]{1,0:T(8,128)S(1)} %maximum_maximum_fusion.1), channel_id=1, source_target_pairs={{0,32},{8,40},{16,48},{24,56},{32,0},{40,8},{48,16},{56,24},{64,96... | collective-permute-start | bytes 55304 | tf_op jit(solution)/shard_map/ppermute | solution.py:500
  70.5 1.5 %collective-permute-start.6 = (f32[36,128]{1,0:T(8,128)S(1)}, f32[36,128]{1,0:T(8,128)S(1)}, u32[]{:S(2)}, u32[]{:S(2)}) collective-permute-start(f32[36,128]{1,0:T(8,128)S(1)} %maximum_maximum_fusion.1), channel_id=1, source_target_pairs={{0,48},{8,56},{16,32},{24,40},{32,16},{40,24},{48,0},{56,8},{64,11... | collective-permute-start | bytes 55304 | tf_op jit(solution)/shard_map/ppermute | solution.py:500
  72.0 0.0 collective-permute-start.5
  72.0 1.9 %collective-permute-done.7 = f32[36,128]{1,0:T(8,128)S(1)} collective-permute-done((f32[36,128]{1,0:T(8,128)S(1)}, f32[36,128]{1,0:T(8,128)S(1)}, u32[]{:S(2)}, u32[]{:S(2)}) %collective-permute-start.7) | collective-permute-done | bytes 18464 | tf_op jit(solution)/shard_map/ppermute | solution.py:500
  74.0 1.6 %collective-permute-done.6 = f32[36,128]{1,0:T(8,128)S(1)} collective-permute-done((f32[36,128]{1,0:T(8,128)S(1)}, f32[36,128]{1,0:T(8,128)S(1)}, u32[]{:S(2)}, u32[]{:S(2)}) %collective-permute-start.6) | collective-permute-done | bytes 18464 | tf_op jit(solution)/shard_map/ppermute | solution.py:500
  75.5 0.3 collective-permute-done.5
  75.8 1.5 %collective-permute-start.10 = (f32[36,128]{1,0:T(8,128)S(1)}, f32[36,128]{1,0:T(8,128)S(1)}, u32[]{:S(2)}, u32[]{:S(2)}) collective-permute-start(f32[36,128]{1,0:T(8,128)S(1)} %maximum_maximum_fusion), channel_id=1, source_target_pairs={{0,128},{8,136},{16,144},{24,152},{32,160},{40,168},{48,176},{56,1... | collective-permute-start | bytes 55304 | tf_op jit(solution)/shard_map/ppermute | solution.py:500
  77.4 1.7 %collective-permute-start.9 = (f32[36,128]{1,0:T(8,128)S(1)}, f32[36,128]{1,0:T(8,128)S(1)}, u32[]{:S(2)}, u32[]{:S(2)}) collective-permute-start(f32[36,128]{1,0:T(8,128)S(1)} %maximum_maximum_fusion), channel_id=1, source_target_pairs={{0,192},{8,200},{16,208},{24,216},{32,224},{40,232},{48,240},{56,2... | collective-permute-start | bytes 55304 | tf_op jit(solution)/shard_map/ppermute | solution.py:500
  79.0 0.4 collective-permute-start.8
  79.4 1.8 %collective-permute-done.10 = f32[36,128]{1,0:T(8,128)S(1)} collective-permute-done((f32[36,128]{1,0:T(8,128)S(1)}, f32[36,128]{1,0:T(8,128)S(1)}, u32[]{:S(2)}, u32[]{:S(2)}) %collective-permute-start.10) | collective-permute-done | bytes 18464 | tf_op jit(solution)/shard_map/ppermute | solution.py:500
  81.2 1.2 %collective-permute-done.9 = f32[36,128]{1,0:T(8,128)S(1)} collective-permute-done((f32[36,128]{1,0:T(8,128)S(1)}, f32[36,128]{1,0:T(8,128)S(1)}, u32[]{:S(2)}, u32[]{:S(2)}) %collective-permute-start.9) | collective-permute-done | bytes 18464 | tf_op jit(solution)/shard_map/ppermute | solution.py:500
  82.3 0.5 collective-permute-done.8
  82.8 0.6 maximum_bitcast_fusion
  (4 shorter events, 0.0 us)
Async XLA Ops:
  3.4 17.9 %all-to-all-start.3 = ((bf16[32,8,896]{2,1,0:T(8,128)(2,1)}), bf16[32,8,896]{2,1,0:T(8,128)(2,1)S(1)}, u32[]{:S(2)}, u32[]{:S(2)}) async-start(bf16[32,8,896]{2,1,0:T(8,128)(2,1)} %get-tuple-element.34), calls=%async_computation.3 | async-start | bytes 917504 | tf_op jit(solution)/shard_map/all_to_all | solution.py:483
  10.8 1.0 %copy-start = (bf16[16,3,5376]{2,0,1:T(8,128)(2,1)S(1)}, bf16[16,3,5376]{2,0,1:T(8,128)(2,1)}, u32[]{:S(2)}) copy-start(bf16[16,3,5376]{2,0,1:T(8,128)(2,1)} %param.8) | copy-start | bytes 1548292
  18.8 11.5 %copy-start.1 = (s32[8]{0:T(128)S(1)}, s32[8]{0:T(128)}, u32[]{:S(2)}) copy-start(s32[8]{0:T(128)} %counts_hbm.1) | copy-start | bytes 100
  53.3 1.6 %collective-permute-start = (f32[36,128]{1,0:T(8,128)S(1)}, f32[36,128]{1,0:T(8,128)S(1)}, u32[]{:S(2)}, u32[]{:S(2)}) collective-permute-start(f32[36,128]{1,0:T(8,128)S(1)} %reshape.25), channel_id=1, source_target_pairs={{0,8},{8,0},{16,24},{24,16},{32,40},{40,32},{48,56},{56,48},{64,72... | collective-permute-start | bytes 55304 | tf_op jit(solution)/shard_map/ppermute | solution.py:500
  54.9 7.3 %collective-permute-start.1 = (f32[36,128]{1,0:T(8,128)S(1)}, f32[36,128]{1,0:T(8,128)S(1)}, u32[]{:S(2)}, u32[]{:S(2)}) collective-permute-start(f32[36,128]{1,0:T(8,128)S(1)} %max.33), channel_id=1, source_target_pairs={{0,6},{1,7},{2,4},{3,5},{4,2},{5,3},{6,0},{7,1},{8,14},{9,15},{10,... | collective-permute-start | bytes 55304 | tf_op jit(solution)/shard_map/ppermute | solution.py:500
  62.3 4.4 %collective-permute-start.4 = (f32[36,128]{1,0:T(8,128)S(1)}, f32[36,128]{1,0:T(8,128)S(1)}, u32[]{:S(2)}, u32[]{:S(2)}) collective-permute-start(f32[36,128]{1,0:T(8,128)S(1)} %max.34), channel_id=1, source_target_pairs={{0,3},{1,2},{2,1},{3,0},{4,7},{5,6},{6,5},{7,4},{8,11},{9,10},{10,... | collective-permute-start | bytes 55304 | tf_op jit(solution)/shard_map/ppermute | solution.py:500
  62.3 4.9 %collective-permute-start.3 = (f32[36,128]{1,0:T(8,128)S(1)}, f32[36,128]{1,0:T(8,128)S(1)}, u32[]{:S(2)}, u32[]{:S(2)}) collective-permute-start(f32[36,128]{1,0:T(8,128)S(1)} %max.34), channel_id=1, source_target_pairs={{0,2},{1,3},{2,0},{3,1},{4,6},{5,7},{6,4},{7,5},{8,10},{9,11},{10,... | collective-permute-start | bytes 55304 | tf_op jit(solution)/shard_map/ppermute | solution.py:500
  64.6 3.8 %collective-permute-start.2 = (f32[36,128]{1,0:T(8,128)S(1)}, f32[36,128]{1,0:T(8,128)S(1)}, u32[]{:S(2)}, u32[]{:S(2)}) collective-permute-start(f32[36,128]{1,0:T(8,128)S(1)} %max.34), channel_id=1, source_target_pairs={{0,1},{1,0},{2,3},{3,2},{4,5},{5,4},{6,7},{7,6},{8,9},{9,8},{10,11... | collective-permute-start | bytes 55304 | tf_op jit(solution)/shard_map/ppermute | solution.py:500
  68.4 5.5 %collective-permute-start.7 = (f32[36,128]{1,0:T(8,128)S(1)}, f32[36,128]{1,0:T(8,128)S(1)}, u32[]{:S(2)}, u32[]{:S(2)}) collective-permute-start(f32[36,128]{1,0:T(8,128)S(1)} %maximum_maximum_fusion.1), channel_id=1, source_target_pairs={{0,32},{8,40},{16,48},{24,56},{32,0},{40,8},{48,16},{56,24},{64,96... | collective-permute-start | bytes 55304 | tf_op jit(solution)/shard_map/ppermute | solution.py:500
  70.5 5.0 %collective-permute-start.6 = (f32[36,128]{1,0:T(8,128)S(1)}, f32[36,128]{1,0:T(8,128)S(1)}, u32[]{:S(2)}, u32[]{:S(2)}) collective-permute-start(f32[36,128]{1,0:T(8,128)S(1)} %maximum_maximum_fusion.1), channel_id=1, source_target_pairs={{0,48},{8,56},{16,32},{24,40},{32,16},{40,24},{48,0},{56,8},{64,11... | collective-permute-start | bytes 55304 | tf_op jit(solution)/shard_map/ppermute | solution.py:500
  72.0 3.8 %collective-permute-start.5 = (f32[36,128]{1,0:T(8,128)S(1)}, f32[36,128]{1,0:T(8,128)S(1)}, u32[]{:S(2)}, u32[]{:S(2)}) collective-permute-start(f32[36,128]{1,0:T(8,128)S(1)} %maximum_maximum_fusion.1), channel_id=1, source_target_pairs={{0,16},{8,24},{16,0},{24,8},{32,48},{40,56},{48,32},{56,40},{64,80... | collective-permute-start | bytes 55304 | tf_op jit(solution)/shard_map/ppermute | solution.py:500
  75.8 5.4 %collective-permute-start.10 = (f32[36,128]{1,0:T(8,128)S(1)}, f32[36,128]{1,0:T(8,128)S(1)}, u32[]{:S(2)}, u32[]{:S(2)}) collective-permute-start(f32[36,128]{1,0:T(8,128)S(1)} %maximum_maximum_fusion), channel_id=1, source_target_pairs={{0,128},{8,136},{16,144},{24,152},{32,160},{40,168},{48,176},{56,1... | collective-permute-start | bytes 55304 | tf_op jit(solution)/shard_map/ppermute | solution.py:500
  77.4 5.0 %collective-permute-start.9 = (f32[36,128]{1,0:T(8,128)S(1)}, f32[36,128]{1,0:T(8,128)S(1)}, u32[]{:S(2)}, u32[]{:S(2)}) collective-permute-start(f32[36,128]{1,0:T(8,128)S(1)} %maximum_maximum_fusion), channel_id=1, source_target_pairs={{0,192},{8,200},{16,208},{24,216},{32,224},{40,232},{48,240},{56,2... | collective-permute-start | bytes 55304 | tf_op jit(solution)/shard_map/ppermute | solution.py:500
  79.0 3.8 %collective-permute-start.8 = (f32[36,128]{1,0:T(8,128)S(1)}, f32[36,128]{1,0:T(8,128)S(1)}, u32[]{:S(2)}, u32[]{:S(2)}) collective-permute-start(f32[36,128]{1,0:T(8,128)S(1)} %maximum_maximum_fusion), channel_id=1, source_target_pairs={{0,64},{8,72},{16,80},{24,88},{32,96},{40,104},{48,112},{56,120},{... | collective-permute-start | bytes 55304 | tf_op jit(solution)/shard_map/ppermute | solution.py:500
